TPU v7x, 32 devices: a whole 2x2x4 slice. The times are simulated.
32 devices in a mesh: group: 2 (over x), tm: 8 (over z, y), space: 2 (over core).
Axes of the slice: x: 2, y: 2, z: 4, core: 2. Of those that a mesh axis runs over, the one named last changes fastest.
Arguments:
- right_side: float32 [16, 2, 32, 64, 128], P(('group', 'tm'), None, 'space'), parts along dimension 0, may hold values from -6 to 6
- diffusivity: float32 [32, 64, 128], P('space'), may hold values from 0.05 to 0.5
- velocity: float32 [3, 32, 64, 128], P(None, 'space'), may hold values from -0.5 to 0.5
Outputs:
- solution: float32 [16, 2, 32, 64, 128], P(('group', 'tm'), None, 'space'), parts along dimension 0
There are 2 independent parts, one for each index of `group`. A program takes and returns all parts, laid end to end along the dimension named above; an argument that names none is the same for every part. Nothing has to cross between parts.
All inputs are finite; a program needn't handle non-finite values.
Results may differ from a plain program's by a relative error of at most 0.0003.
Values sent between devices are 32-bit elements; how exact they have to be, the bound alone decides.
No kernel may reach another device: no remote copies, remote signals or barrier semaphores. Data moves between devices by JAX's collectives and lax.ppermute only.
A program may use at most 64 MiB of HBM per device.

v0:
```python
import jax
import jax.numpy as jnp
from jax import lax
from jax.sharding import PartitionSpec as P

SWEEPS = 4


alpha_circ = 0.1
inv_step = 2.0


def swapped(x, axis, distance):
    return lax.ppermute(x, axis, [(i, i ^ 1 << distance) for i in range(lax.axis_size(axis))])


def padded_2(block, sides, width):
    for axis, dim in sides:
        count = lax.axis_size(axis)
        forward = [(i, i + 1) for i in range(count - 1)]
        backward = [(target, source) for source, target in forward]
        low = lax.ppermute(
            lax.slice_in_dim(block, block.shape[dim] - width, None, axis=dim), axis, forward
        )
        high = lax.ppermute(lax.slice_in_dim(block, 0, width, axis=dim), axis, backward)
        block = jnp.concatenate([low, block, high], axis=dim)
    return block


def couple(padded, diffusivity, forward_flow, backward_flow):
    below_z = padded[..., :-2, 1:-1, 1:-1]
    above_z = padded[..., 2:, 1:-1, 1:-1]
    below_x = padded[..., 1:-1, :-2, 1:-1]
    above_x = padded[..., 1:-1, 2:, 1:-1]
    below_y = padded[..., 1:-1, 1:-1, :-2]
    above_y = padded[..., 1:-1, 1:-1, 2:]
    combined = diffusivity * (below_z + above_z + below_x + above_x + below_y + above_y)
    combined = combined + forward_flow[0] * below_z + backward_flow[0] * above_z
    combined = combined + forward_flow[1] * below_x + backward_flow[1] * above_x
    combined = combined + forward_flow[2] * below_y + backward_flow[2] * above_y
    return combined


def inverse_diagonal(diffusivity, velocity, lam_re, lam_im):
    real_part = lam_re + 6.0 * diffusivity + jnp.sum(jnp.abs(velocity), axis=0)
    magnitude = real_part * real_part + lam_im * lam_im
    return (real_part / magnitude, -lam_im / magnitude)


def rotate(real_part, imag_part, cos_part, sin_part):
    return (
        real_part * cos_part - imag_part * sin_part,
        real_part * sin_part + imag_part * cos_part,
    )


def jacobi_step(source, nearby, inv_real, inv_imag):
    combined = source + nearby
    new_real, new_imag = rotate(combined[:, 0], combined[:, 1], inv_real, inv_imag)
    return jnp.stack([new_real, new_imag], axis=1)


def turn_field(grid_field, cos_part, sin_part):
    new_real, new_imag = rotate(grid_field[:, 0], grid_field[:, 1], cos_part, sin_part)
    return jnp.stack([new_real, new_imag], axis=1)


def partner(grid_field, bit_level):
    return swapped(grid_field, "tm", bit_level)


def butterfly_forward(grid_field, position, levels):
    for bit_level in reversed(range(levels)):
        half_span = 1 << bit_level
        partner_field = partner(grid_field, bit_level)
        is_upper = position >> bit_level & 1 == 1
        offset = position % (2 * half_span) - half_span
        phase_angle = -jnp.pi / half_span * offset.astype(jnp.float32)
        rotated = turn_field(partner_field - grid_field, jnp.cos(phase_angle), jnp.sin(phase_angle))
        grid_field = jnp.where(is_upper, rotated, grid_field + partner_field)
    return grid_field


def butterfly_inverse(grid_field, position, levels):
    for bit_level in range(levels):
        half_span = 1 << bit_level
        partner_field = partner(grid_field, bit_level)
        is_upper = position >> bit_level & 1 == 1
        phase_angle = jnp.pi / half_span * (position % half_span).astype(jnp.float32)
        moving = jnp.where(is_upper, grid_field, partner_field)
        kept_part = jnp.where(is_upper, partner_field, grid_field)
        turned = turn_field(moving, jnp.cos(phase_angle), jnp.sin(phase_angle))
        grid_field = jnp.where(is_upper, kept_part - turned, kept_part + turned)
    return grid_field


def local(right_side, diffusivity, velocity):
    time_count = lax.axis_size("tm")
    levels = time_count.bit_length() - 1
    position = lax.axis_index("tm")
    step_float = position.astype(jnp.float32)
    log_alpha = jnp.log(jnp.float32(alpha_circ))
    weight = jnp.exp(step_float / time_count * log_alpha)
    grid_field = right_side * weight
    spectrum = butterfly_forward(grid_field, position, levels)
    frequency = jnp.zeros((), jnp.int32)
    for bit_level in range(levels):
        frequency = frequency + ((position >> bit_level & 1) << levels - 1 - bit_level)
    phase_angle = 2.0 * jnp.pi / time_count * frequency.astype(jnp.float32)
    radius = jnp.exp(log_alpha / time_count)
    lam_re = inv_step * (1.0 - radius * jnp.cos(phase_angle))
    lam_im = inv_step * radius * jnp.sin(phase_angle)
    inv_real, inv_imag = inverse_diagonal(diffusivity, velocity, lam_re, lam_im)
    forward_flow = jnp.maximum(velocity, 0.0)
    backward_flow = jnp.maximum(-velocity, 0.0)
    iterate = jacobi_step(spectrum, 0.0, inv_real, inv_imag)
    for sweep_number in range(SWEEPS - 1):
        padded = padded_2(iterate, (("space", 2),), 1)
        padded = jnp.pad(padded, ((0, 0), (0, 0), (0, 0), (1, 1), (1, 1)))
        iterate = jacobi_step(
            spectrum, couple(padded, diffusivity, forward_flow, backward_flow), inv_real, inv_imag
        )
    solved = butterfly_inverse(iterate, position, levels)
    return solved / time_count / weight


def solution(mesh):
    placed = (
        P(("group", "tm"), None, "space", None, None),
        P("space", None, None),
        P(None, "space", None, None),
    )
    return jax.shard_map(
        local,
        mesh=mesh,
        in_specs=placed,
        out_specs=P(("group", "tm"), None, "space", None, None),
        check_vma=False,
    )
```

profile of v0, /device:TPU:8, one launch (start us, length us, event | category | flops | bytes accessed | tf_op | source)
XLA Modules:
  0.0 225.9 jit_solution(12807071442739480317)
XLA Ops:
  0.1 1.4 broadcast_multiply_fusion
  1.4 2.7 %collective-permute-start = (f32[1,2,16,64,128]{4,3,2,1,0:T(8,128)S(1)}, f32[1,2,16,64,128]{4,3,2,1,0:T(8,128)S(1)}, u32[]{:S(2)}, u32[]{:S(2)}) collective-permute-start(f32[1,2,16,64,128]{4,3,2,1,0:T(8,128)S(1)} %broadcast_multiply_fusion), channel_id=1, source_target_pairs={{0,8},{2,10},{4,12},{6,14},{8,0},{10,2},{12,4},{14,6},{1,9},{3,11}... | collective-permute-start | bytes 3145736 | tf_op jit(solution)/shard_map/ppermute | solution.py:14
  4.2 44.6 %collective-permute-done = f32[1,2,16,64,128]{4,3,2,1,0:T(8,128)S(1)} collective-permute-done((f32[1,2,16,64,128]{4,3,2,1,0:T(8,128)S(1)}, f32[1,2,16,64,128]{4,3,2,1,0:T(8,128)S(1)}, u32[]{:S(2)}, u32[]{:S(2)}) %collective-permute-start) | collective-permute-done | bytes 1048608 | tf_op jit(solution)/shard_map/ppermute | solution.py:14
  49.6 1.4 collective-permute-start.1
  51.1 23.6 %collective-permute-done.1 = f32[1,2,16,64,128]{4,3,2,1,0:T(8,128)S(1)} collective-permute-done((f32[1,2,16,64,128]{4,3,2,1,0:T(8,128)S(1)}, f32[1,2,16,64,128]{4,3,2,1,0:T(8,128)S(1)}, u32[]{:S(2)}, u32[]{:S(2)}) %collective-permute-start.1) | collective-permute-done | bytes 1048608 | tf_op jit(solution)/shard_map/ppermute | solution.py:14
  75.3 1.6 collective-permute-start.2
  77.3 1.9 broadcast_maximum_fusion
  79.2 20.4 %collective-permute-done.2 = f32[1,2,16,64,128]{4,3,2,1,0:T(8,128)S(1)} collective-permute-done((f32[1,2,16,64,128]{4,3,2,1,0:T(8,128)S(1)}, f32[1,2,16,64,128]{4,3,2,1,0:T(8,128)S(1)}, u32[]{:S(2)}, u32[]{:S(2)}) %collective-permute-start.2) | collective-permute-done | bytes 1048608 | tf_op jit(solution)/shard_map/ppermute | solution.py:14
  101.4 1.3 collective-permute-start.3
  102.7 1.3 collective-permute-start.4
  104.4 1.4 collective-permute-done.4
  108.0 2.1 collective-permute-start.5
  111.4 1.8 collective-permute-done.6
  115.5 2.1 collective-permute-start.7
  117.6 1.5 collective-permute-start.8
  119.1 1.7 collective-permute-done.8
  123.0 1.6 collective-permute-start.9
  124.5 23.7 %collective-permute-done.9 = f32[1,2,16,64,128]{4,3,2,1,0:T(8,128)S(1)} collective-permute-done((f32[1,2,16,64,128]{4,3,2,1,0:T(8,128)S(1)}, f32[1,2,16,64,128]{4,3,2,1,0:T(8,128)S(1)}, u32[]{:S(2)}, u32[]{:S(2)}) %collective-permute-start.9) | collective-permute-done | bytes 1048608 | tf_op jit(solution)/shard_map/ppermute | solution.py:14
  148.6 1.3 add_select_fusion.1
  150.0 24.5 %collective-permute-done.10 = f32[1,2,16,64,128]{4,3,2,1,0:T(8,128)} collective-permute-done((f32[1,2,16,64,128]{4,3,2,1,0:T(8,128)}, f32[1,2,16,64,128]{4,3,2,1,0:T(8,128)}, u32[]{:S(2)}, u32[]{:S(2)}) %collective-permute-start.10) | collective-permute-done | bytes 1048608 | tf_op jit(solution)/shard_map/ppermute | solution.py:14
  175.2 2.1 add_select_fusion
  177.3 3.4 %collective-permute-start.11 = (f32[1,2,16,64,128]{4,3,2,1,0:T(8,128)S(1)}, f32[1,2,16,64,128]{4,3,2,1,0:T(8,128)S(1)}, u32[]{:S(2)}, u32[]{:S(2)}) collective-permute-start(f32[1,2,16,64,128]{4,3,2,1,0:T(8,128)S(1)} %add_select_fusion), channel_id=1, source_target_pairs={{0,8},{2,10},{4,12},{6,14},{8,0},{10,2},{12,4},{14,6},{1,9},{3,11}... | collective-permute-start | bytes 3145736 | tf_op jit(solution)/shard_map/ppermute | solution.py:14
  180.9 43.3 %collective-permute-done.11 = f32[1,2,16,64,128]{4,3,2,1,0:T(8,128)S(1)} collective-permute-done((f32[1,2,16,64,128]{4,3,2,1,0:T(8,128)S(1)}, f32[1,2,16,64,128]{4,3,2,1,0:T(8,128)S(1)}, u32[]{:S(2)}, u32[]{:S(2)}) %collective-permute-start.11) | collective-permute-done | bytes 1048608 | tf_op jit(solution)/shard_map/ppermute | solution.py:14
  224.6 1.3 multiply_divide_fusion
  (44 shorter events, 12.5 us)
Async XLA Ops:
  0.0 48.9 %copy-start = (f32[1,2,16,64,128]{4,3,2,1,0:T(8,128)S(1)}, f32[1,2,16,64,128]{4,3,2,1,0:T(8,128)}, u32[]{:S(2)}) copy-start(f32[1,2,16,64,128]{4,3,2,1,0:T(8,128)} %param.3) | copy-start | bytes 3145732
  1.4 47.4 %collective-permute-start = (f32[1,2,16,64,128]{4,3,2,1,0:T(8,128)S(1)}, f32[1,2,16,64,128]{4,3,2,1,0:T(8,128)S(1)}, u32[]{:S(2)}, u32[]{:S(2)}) collective-permute-start(f32[1,2,16,64,128]{4,3,2,1,0:T(8,128)S(1)} %broadcast_multiply_fusion), channel_id=1, source_target_pairs={{0,8},{2,10},{4,12},{6,14},{8,0},{10,2},{12,4},{14,6},{1,9},{3,11}... | collective-permute-start | bytes 3145736 | tf_op jit(solution)/shard_map/ppermute | solution.py:14
  49.6 25.1 %collective-permute-start.1 = (f32[1,2,16,64,128]{4,3,2,1,0:T(8,128)S(1)}, f32[1,2,16,64,128]{4,3,2,1,0:T(8,128)S(1)}, u32[]{:S(2)}, u32[]{:S(2)}) collective-permute-start(f32[1,2,16,64,128]{4,3,2,1,0:T(8,128)S(1)} %maximum_select_fusion), channel_id=1, source_target_pairs={{0,4},{2,6},{4,0},{6,2},{8,12},{10,14},{12,8},{14,10},{1,5},{3,7},... | collective-permute-start | bytes 3145736 | tf_op jit(solution)/shard_map/ppermute | solution.py:14
  75.3 24.3 %collective-permute-start.2 = (f32[1,2,16,64,128]{4,3,2,1,0:T(8,128)S(1)}, f32[1,2,16,64,128]{4,3,2,1,0:T(8,128)S(1)}, u32[]{:S(2)}, u32[]{:S(2)}) collective-permute-start(f32[1,2,16,64,128]{4,3,2,1,0:T(8,128)S(1)} %maximum_select_fusion.1), channel_id=1, source_target_pairs={{0,2},{2,0},{4,6},{6,4},{8,10},{10,8},{12,14},{14,12},{1,3},{3,1},... | collective-permute-start | bytes 3145736 | tf_op jit(solution)/shard_map/ppermute | solution.py:14
  99.8 1.0 copy-start.1
  101.4 3.0 %collective-permute-start.3 = (f32[1,2,1,64,128]{4,3,2,1,0:T(8,128)S(1)}, f32[1,2,1,64,128]{4,3,2,1,0:T(8,128)S(1)}, u32[]{:S(2)}, u32[]{:S(2)}) collective-permute-start(f32[1,2,1,64,128]{4,3,2,1,0:T(8,128)S(1)} %get-tuple-element.33), channel_id=1, source_target_pairs={{0,1},{2,3},{4,5},{6,7},{8,9},{10,11},{12,13},{14,15},{16,17},{18,... | collective-permute-start | bytes 196616 | tf_op jit(solution)/shard_map/ppermute | solution.py:22
  102.7 3.1 %collective-permute-start.4 = (f32[1,2,1,64,128]{4,3,2,1,0:T(8,128)S(1)}, f32[1,2,1,64,128]{4,3,2,1,0:T(8,128)S(1)}, u32[]{:S(2)}, u32[]{:S(2)}) collective-permute-start(f32[1,2,1,64,128]{4,3,2,1,0:T(8,128)S(1)} %get-tuple-element.34), channel_id=1, source_target_pairs={{1,0},{3,2},{5,4},{7,6},{9,8},{11,10},{13,12},{15,14},{17,16},{19,... | collective-permute-start | bytes 196616 | tf_op jit(solution)/shard_map/ppermute | solution.py:25
  108.0 3.4 %collective-permute-start.5 = (f32[1,2,1,64,128]{4,3,2,1,0:T(8,128)S(1)}, f32[1,2,1,64,128]{4,3,2,1,0:T(8,128)S(1)}, u32[]{:S(2)}, u32[]{:S(2)}) collective-permute-start(f32[1,2,1,64,128]{4,3,2,1,0:T(8,128)S(1)} %get-tuple-element.31), channel_id=1, source_target_pairs={{0,1},{2,3},{4,5},{6,7},{8,9},{10,11},{12,13},{14,15},{16,17},{18,... | collective-permute-start | bytes 196616 | tf_op jit(solution)/shard_map/ppermute | solution.py:22
  110.1 3.1 %collective-permute-start.6 = (f32[1,2,1,64,128]{4,3,2,1,0:T(8,128)S(1)}, f32[1,2,1,64,128]{4,3,2,1,0:T(8,128)S(1)}, u32[]{:S(2)}, u32[]{:S(2)}) collective-permute-start(f32[1,2,1,64,128]{4,3,2,1,0:T(8,128)S(1)} %get-tuple-element.32), channel_id=1, source_target_pairs={{1,0},{3,2},{5,4},{7,6},{9,8},{11,10},{13,12},{15,14},{17,16},{19,... | collective-permute-start | bytes 196616 | tf_op jit(solution)/shard_map/ppermute | solution.py:25
  115.5 3.6 %collective-permute-start.7 = (f32[1,2,1,64,128]{4,3,2,1,0:T(8,128)S(1)}, f32[1,2,1,64,128]{4,3,2,1,0:T(8,128)S(1)}, u32[]{:S(2)}, u32[]{:S(2)}) collective-permute-start(f32[1,2,1,64,128]{4,3,2,1,0:T(8,128)S(1)} %get-tuple-element.29), channel_id=1, source_target_pairs={{0,1},{2,3},{4,5},{6,7},{8,9},{10,11},{12,13},{14,15},{16,17},{18,... | collective-permute-start | bytes 196616 | tf_op jit(solution)/shard_map/ppermute | solution.py:22
  117.6 3.1 %collective-permute-start.8 = (f32[1,2,1,64,128]{4,3,2,1,0:T(8,128)S(1)}, f32[1,2,1,64,128]{4,3,2,1,0:T(8,128)S(1)}, u32[]{:S(2)}, u32[]{:S(2)}) collective-permute-start(f32[1,2,1,64,128]{4,3,2,1,0:T(8,128)S(1)} %get-tuple-element.30), channel_id=1, source_target_pairs={{1,0},{3,2},{5,4},{7,6},{9,8},{11,10},{13,12},{15,14},{17,16},{19,... | collective-permute-start | bytes 196616 | tf_op jit(solution)/shard_map/ppermute | solution.py:25
  123.0 25.3 %collective-permute-start.9 = (f32[1,2,16,64,128]{4,3,2,1,0:T(8,128)S(1)}, f32[1,2,16,64,128]{4,3,2,1,0:T(8,128)S(1)}, u32[]{:S(2)}, u32[]{:S(2)}) collective-permute-start(f32[1,2,16,64,128]{4,3,2,1,0:T(8,128)S(1)} %pad_maximum_fusion.12), channel_id=1, source_target_pairs={{0,2},{2,0},{4,6},{6,4},{8,10},{10,8},{12,14},{14,12},{1,3},{3,1},... | collective-permute-start | bytes 3145736 | tf_op jit(solution)/shard_map/ppermute | solution.py:14
  148.6 26.5 %copy-start.2 = (f32[1,1,16,64,128]{4,3,2,1,0:T(8,128)}, f32[1,1,16,64,128]{4,3,2,1,0:T(8,128)S(1)}, u32[]{:S(2)}) copy-start(f32[1,1,16,64,128]{4,3,2,1,0:T(8,128)S(1)} %get-tuple-element.27) | copy-start | bytes 1572868
  148.6 26.5 %copy-start.3 = (f32[1,1,16,64,128]{4,3,2,1,0:T(8,128)}, f32[1,1,16,64,128]{4,3,2,1,0:T(8,128)S(1)}, u32[]{:S(2)}) copy-start(f32[1,1,16,64,128]{4,3,2,1,0:T(8,128)S(1)} %get-tuple-element.28) | copy-start | bytes 1572868
  149.9 24.7 %collective-permute-start.10 = (f32[1,2,16,64,128]{4,3,2,1,0:T(8,128)}, f32[1,2,16,64,128]{4,3,2,1,0:T(8,128)}, u32[]{:S(2)}, u32[]{:S(2)}) collective-permute-start(f32[1,2,16,64,128]{4,3,2,1,0:T(8,128)} %add_select_fusion.1), channel_id=1, source_target_pairs={{0,4},{2,6},{4,0},{6,2},{8,12},{10,14},{12,8},{14,10},{1,5},{3,7},... | collective-permute-start | bytes 3145736 | tf_op jit(solution)/shard_map/ppermute | solution.py:14
  177.3 46.9 %collective-permute-start.11 = (f32[1,2,16,64,128]{4,3,2,1,0:T(8,128)S(1)}, f32[1,2,16,64,128]{4,3,2,1,0:T(8,128)S(1)}, u32[]{:S(2)}, u32[]{:S(2)}) collective-permute-start(f32[1,2,16,64,128]{4,3,2,1,0:T(8,128)S(1)} %add_select_fusion), channel_id=1, source_target_pairs={{0,8},{2,10},{4,12},{6,14},{8,0},{10,2},{12,4},{14,6},{1,9},{3,11}... | collective-permute-start | bytes 3145736 | tf_op jit(solution)/shard_map/ppermute | solution.py:14
where the time goes:
time: 229 us; the launch traced here: 226 us
  waiting for transfers between devices  185 us (81%)
  starting transfers between devices  20.1 us (9%)
  other arithmetic  18.3 us (8%)
    ppermute x6, waiting for transfers between devices, swapped(): lax.ppermute(x, axis, [(i, i ^ 1 << distance) for i in range(lax.axis_siz...  180 us
    ppermute x6, starting transfers between devices, swapped(): lax.ppermute(x, axis, [(i, i ^ 1 << distance) for i in range(lax.axis_siz...  10.6 us
    ppermute x3, starting transfers between devices, padded_2(): lax.ppermute(lax.slice_in_dim(block, block.shape[dim] - width, None, axis...  5.42 us
    ppermute x3, waiting for transfers between devices, padded_2(): lax.ppermute(lax.slice_in_dim(block, 0, width, axis=dim), axis, backward)  4.92 us
  transfers between devices with their start and end apart: 12, of which 9 were waited for; matrix products, arithmetic and copies ran while one was open for 1% of the time, Pallas kernels for 0%

commit v1 on v0

v1 whole, which is shorter than its diff:
```python
import functools

import jax
import jax.numpy as jnp
from jax import lax
from jax.experimental import pallas as pl
from jax.experimental.pallas import tpu as pltpu
from jax.sharding import PartitionSpec as P

SWEEPS = 4
GHOST = SWEEPS - 1
QUARTERS = 4
TILE = 8
COEFS = 9

alpha_circ = 0.1
inv_step = 2.0

FLAT = ("tm", "space")


class Plan:
    def __init__(self, steps, cores, half_z, nx, ny):
        self.steps, self.cores, self.half_z, self.nx, self.ny = steps, cores, half_z, nx, ny
        self.z_parts = steps // QUARTERS
        self.in_half = self.z_parts // cores
        self.nz = half_z // self.in_half
        self.rows = nx // QUARTERS
        self.main = self.rows // TILE
        self.tiles = self.main + 1
        self.ext = self.nz + 2 * GHOST
        order = [2, 3, 1, 0]
        self.rounds = [(a, m, c) for a in order for m in range(self.in_half) for c in range(2)]

    def flat(self, hi, zb, s):
        return (hi * self.z_parts + zb) * self.cores + s

    def pairs(self, a, m, c):
        result = []
        for hi in range(QUARTERS):
            for jm in range(self.in_half):
                for jb in range(2):
                    for h in range(self.cores):
                        source = self.flat(hi, jm * 2 + jb, h)
                        target = self.flat(hi ^ a, h * self.in_half + (jm ^ m), jb ^ c)
                        result.append((source, target))
        return result

    def x_pairs(self, first):
        result = []
        for hi in range(first, QUARTERS - 1, 2):
            for zb in range(self.z_parts):
                for s in range(self.cores):
                    one, two = self.flat(hi, zb, s), self.flat(hi + 1, zb, s)
                    result += [(one, two), (two, one)]
        return result

    def z_pairs(self, first):
        result = []
        for zb in range(first, self.z_parts - 1, 2):
            for hi in range(QUARTERS):
                for s in range(self.cores):
                    one, two = self.flat(hi, zb, s), self.flat(hi, zb + 1, s)
                    result += [(one, two), (two, one)]
        return result

    def time_of(self, hi, zb, s, a, m, c):
        return ((hi ^ a) * self.in_half + ((zb % self.in_half) ^ m)) * 2 + (s ^ c)


def kernel_call(body, outs, args, scalars=True, scratch=(), cost=None):
    in_specs = [pl.BlockSpec(memory_space=pltpu.VMEM)] * len(args)
    if scalars:
        in_specs[0] = pl.BlockSpec(memory_space=pltpu.SMEM)
    single = isinstance(outs, tuple)
    shapes = [outs] if single else list(outs)
    result = pl.pallas_call(
        body,
        out_shape=[jax.ShapeDtypeStruct(s, jnp.float32) for s in shapes],
        in_specs=in_specs,
        out_specs=[pl.BlockSpec(memory_space=pltpu.VMEM)] * len(shapes),
        scratch_shapes=list(scratch),
        compiler_params=pltpu.CompilerParams(vmem_limit_bytes=40 << 20),
    )(*args)
    return result[0] if single else result


def rows_at(index, count=1):
    return pl.ds(pl.multiple_of(index * TILE, TILE), count * TILE)


def sublane(plan):
    return lax.broadcasted_iota(jnp.int32, (TILE, plan.ny), 0)


def lane(plan):
    return lax.broadcasted_iota(jnp.int32, (TILE, plan.ny), 1)


def pack_coefs(plan, place, d_ref, v_ref, out_ref):
    hi = place[0]
    per = plan.nx // TILE
    below = jnp.maximum(hi * plan.main - 1, 0)
    above = jnp.minimum(hi * plan.main + plan.main, per - 1)
    row = sublane(plan)

    def layer(z, _):
        for n in range(4):
            ref, base = (d_ref, z * per) if n == 0 else (v_ref, ((n - 1) * plan.half_z + z) * per)
            at = (n * plan.half_z + z) * plan.tiles
            for k in range(plan.main):
                out_ref[rows_at(at + k), :] = ref[rows_at(base + hi * plan.main + k), :]
            over, under = ref[rows_at(base + above), :], ref[rows_at(base + below), :]
            edge = jnp.where(row < TILE // 2, over, under)
            out_ref[rows_at(at + plan.main), :] = edge
        return 0

    lax.fori_loop(0, plan.half_z, layer, 0)


def make_coefs(plan, place, own_ref, other_ref, out_ref):
    hi, zb, s = place[0], place[1], place[2]
    row, col = sublane(plan), lane(plan)

    def layer(e, _):
        depth = zb * plan.nz + e - GHOST
        inside = (depth >= 0) & (depth < plan.half_z * plan.cores)
        depth = jnp.clip(depth, 0, plan.half_z * plan.cores - 1)
        mine = depth // plan.half_z == s
        z = depth % plan.half_z
        for k in range(plan.tiles):
            values = []
            for n in range(4):
                at = rows_at((n * plan.half_z + z) * plan.tiles + k)
                values.append(jnp.where(mine, own_ref[at, :], other_ref[at, :]))
            d, vz, vx, vy = values
            if k < plan.main:
                x = row + k * TILE
            else:
                x = jnp.where(row < GHOST, row + plan.rows, row - TILE)
            x = x + hi * plan.rows
            keep = (x >= 0) & (x < plan.nx) & inside
            if k == plan.main:
                keep = keep & ((row < GHOST) | (row >= TILE - GHOST))
            total = inv_step + 6.0 * d + (jnp.abs(vz) + jnp.abs(vx) + jnp.abs(vy))
            w = jnp.where(keep, 1.0 / total, 0.0)
            c = inv_step * w
            power = c
            for _ in range(plan.steps.bit_length() - 1):
                power = power * power
            wrap = alpha_circ / (1.0 - alpha_circ * power)
            low = [w * (d + jnp.maximum(v, 0.0)) for v in (vz, vx, vy)]
            high = [w * (d + jnp.maximum(-v, 0.0)) for v in (vz, vx, vy)]
            low[2] = jnp.where(col == 0, 0.0, low[2])
            high[2] = jnp.where(col == plan.ny - 1, 0.0, high[2])
            made = [w, c, wrap] + low + high
            for n, value in enumerate(made):
                out_ref[rows_at((e * plan.tiles + k) * COEFS + n), :] = value
        return 0

    lax.fori_loop(0, plan.ext, layer, 0)


def gather_steps(plan, place, *refs):
    hi, zb, s = place[0], place[1], place[2]
    blocks, (field, x_even, x_odd, *z_sends) = refs[: plan.steps], refs[plan.steps :]
    size = plan.nz * plan.rows
    hi_odd = hi % 2 == 1
    zb_odd = zb % 2 == 1
    for block, (a, m, c) in zip(blocks, plan.rounds):
        step = plan.time_of(hi, zb, s, a, m, c)
        field[pl.ds(pl.multiple_of(step * size, TILE), size), :] = block[...]
        for r in range(GHOST):
            low = block[pl.ds(r, plan.nz, stride=plan.rows), :]
            high = block[pl.ds(plan.rows - GHOST + r, plan.nz, stride=plan.rows), :]
            at = pl.ds(r * plan.steps * plan.nz + step * plan.nz, plan.nz)
            x_even[at, :] = jnp.where(hi_odd, low, high)
            x_odd[at, :] = jnp.where(hi_odd, high, low)
        edge = GHOST * plan.rows
        at = pl.ds(pl.multiple_of(step * edge, TILE), edge)
        low, high = block[:edge, :], block[size - edge :, :]
        for first, z_send in enumerate(z_sends):
            z_send[at, :] = jnp.where(zb_odd ^ (first == 1), low, high)


def gather_ghosts(plan, place, even_ref, odd_ref, planes, *corners):
    hi, zb = place[0], place[1]
    hi_odd = hi % 2 == 1
    zb_odd = zb % 2 == 1
    count = plan.steps * plan.nz
    for r in range(GHOST):
        even, odd = even_ref[pl.ds(r * count, count), :], odd_ref[pl.ds(r * count, count), :]
        planes[pl.ds(r * count, count), :] = jnp.where(hi_odd, odd, even)
        planes[pl.ds((TILE - GHOST + r) * count, count), :] = jnp.where(hi_odd, even, odd)
    for r in range(GHOST, TILE - GHOST):
        planes[pl.ds(r * count, count), :] = jnp.zeros((count, plan.ny), jnp.float32)
    deep = GHOST - 1
    for step in range(plan.steps):
        for n in range(deep):
            low = planes[pl.ds(step * plan.nz + n, TILE, stride=count), :]
            high = planes[pl.ds(step * plan.nz + plan.nz - deep + n, TILE, stride=count), :]
            for first, corner in enumerate(corners):
                corner[rows_at(step * deep + n), :] = jnp.where(zb_odd ^ (first == 1), low, high)


def sweep_kernel(plan, place, coefs, field, planes, *refs):
    hi, zb, s = place[0], place[1], place[2]
    sides = 1 if plan.z_parts == 2 else 2
    z_in, refs = refs[:sides], refs[sides:]
    c_in, refs = refs[:sides], refs[sides:]
    outs, (source, ping, pong, last) = refs[: plan.steps], refs[plan.steps :]
    steps, tiles, main, ny = plan.steps, plan.tiles, plan.main, plan.ny
    count = steps * plan.nz
    deep = GHOST - 1
    zb_odd = zb % 2 == 1
    row = sublane(plan)
    has_low, has_high = zb > 0, zb < plan.z_parts - 1

    def spot(e, k, t):
        return rows_at((e * tiles + k) * steps + t)

    def coef(e, k, n):
        return coefs[rows_at((e * tiles + k) * COEFS + n), :]

    def solve(c, wrap, scaled):
        partial = [scaled[0]]
        for value in scaled[1:]:
            partial.append(value + c * partial[-1])
        carry = c * (wrap * partial[-1])
        result = []
        for value in partial:
            result.append(value + carry)
            carry = c * carry
        return result

    def first(e, k, values):
        w, c, wrap = (coef(e, k, n) for n in range(3))
        scaled = [w * value for value in values]
        for t, (value, solved) in enumerate(zip(scaled, solve(c, wrap, scaled))):
            source[spot(e, k, t), :] = value
            ping[spot(e, k, t), :] = solved

    def own_layer(z, _):
        e = z + GHOST
        for k in range(main):
            first(e, k, [field[rows_at((t * plan.nz + z) * main + k), :] for t in range(steps)])
        first(e, main, [planes[pl.ds(t * plan.nz + z, TILE, stride=count), :] for t in range(steps)])
        return 0

    lax.fori_loop(0, plan.nz, own_layer, 0)

    empty = jnp.zeros((TILE, ny), jnp.float32)

    def ghost_layers(at, upper, main_ref, corner_ref):
        for n in range(GHOST):
            e = at + n
            for k in range(main):
                first(e, k, [main_ref[rows_at((t * GHOST + n) * main + k), :] for t in range(steps)])
            c_at = n if upper else n - (GHOST - deep)
            if 0 <= c_at < deep:
                first(e, main, [corner_ref[rows_at(t * deep + c_at), :] for t in range(steps)])
            else:
                for t in range(steps):
                    ping[spot(e, main, t), :] = empty
                    source[spot(e, main, t), :] = empty

    def no_layer(e):
        for k in range(tiles):
            for t in range(steps):
                ping[spot(e, k, t), :] = empty
                pong[spot(e, k, t), :] = empty

    high_at = GHOST + plan.nz
    for odd in (False, True):

        @pl.when(has_low & (zb_odd == odd))
        def _():
            pick = 0 if odd else sides - 1
            ghost_layers(0, False, z_in[pick], c_in[pick])

        @pl.when(has_high & (zb_odd == odd))
        def _():
            pick = sides - 1 if odd else 0
            ghost_layers(high_at, True, z_in[pick], c_in[pick])

    @pl.when(jnp.logical_not(has_low))
    def _():
        no_layer(GHOST - 1)

    @pl.when(jnp.logical_not(has_high))
    def _():
        no_layer(high_at)

    buffers = (ping, pong)
    for sweep in range(1, SWEEPS):
        old, new = buffers[(sweep - 1) % 2], buffers[sweep % 2]
        final = sweep == SWEEPS - 1
        reach = SWEEPS - 1 - sweep
        wide = main if final else tiles

        def layer(e, _, old=old, new=new, final=final, wide=wide):
            c = [coef(e, k, 1) for k in range(wide)]
            near = [[coef(e, k, n) for n in range(3, COEFS)] for k in range(wide)]
            partial = [[] for _ in range(wide)]
            for t in range(steps):
                here = [old[spot(e, k, t), :] for k in range(tiles)]
                down = [pltpu.roll(value, 1, 0) for value in here]
                up = [pltpu.roll(value, TILE - 1, 0) for value in here]
                for k in range(wide):
                    z_low, x_low, y_low, z_high, x_high, y_high = near[k]
                    below = jnp.where(row == 0, down[k - 1], down[k])
                    above = jnp.where(row == TILE - 1, up[(k + 1) % tiles], up[k])
                    total = source[spot(e, k, t), :] + z_low * old[spot(e - 1, k, t), :]
                    total = total + z_high * old[spot(e + 1, k, t), :]
                    total = total + (x_low * below + x_high * above)
                    total = total + (
                        y_low * pltpu.roll(here[k], 1, 1) + y_high * pltpu.roll(here[k], ny - 1, 1)
                    )
                    if t:
                        total = total + c[k] * partial[k][-1]
                    partial[k].append(total)
            for k in range(wide):
                carry = c[k] * (coef(e, k, 2) * partial[k][-1])
                for t in range(steps):
                    value = partial[k][t] + carry
                    carry = c[k] * carry
                    if final:
                        last[rows_at((t * plan.nz + e - GHOST) * main + k), :] = value
                    else:
                        new[spot(e, k, t), :] = value
            return 0

        start = jnp.where(has_low, GHOST - reach, GHOST)
        stop = jnp.where(has_high, high_at + reach, high_at)
        lax.fori_loop(start, stop, layer, 0)

    size = plan.nz * plan.rows
    for out, (a, m, c) in zip(outs, plan.rounds):
        step = plan.time_of(hi, zb, s, a, m, c)
        out[...] = last[pl.ds(pl.multiple_of(step * size, TILE), size), :]


def place_blocks(plan, place, *refs):
    blocks, out, sems = refs[: plan.steps], refs[plan.steps], refs[plan.steps + 1]
    hi, lo = place[0], place[1]
    copies = []
    for n, (block, (a, m, c)) in enumerate(zip(blocks, plan.rounds)):
        part = (lo % 2) ^ c
        z = pl.multiple_of(((lo // 2) ^ m) * plan.nz, plan.nz)
        x = pl.multiple_of((hi ^ a) * plan.rows, plan.rows)
        target = out.at[part, pl.ds(z, plan.nz), pl.ds(x, plan.rows), :]
        copies.append(pltpu.make_async_copy(block, target, sems.at[n]))
    for copy in copies:
        copy.start()
    for copy in copies:
        copy.wait()


def local(right_side, diffusivity, velocity):
    steps, cores = lax.axis_size("tm"), lax.axis_size("space")
    _, parts, half_z, nx, ny = right_side.shape
    plan = Plan(steps, cores, half_z, nx, ny)
    t, s = lax.axis_index("tm"), lax.axis_index("space")
    hi, lo = t // plan.z_parts, t % plan.z_parts
    place = jnp.stack([hi, lo, s]).astype(jnp.int32)
    size = plan.nz * plan.rows

    blocks = []
    for a, m, c in plan.rounds:
        at = ((lo % 2) ^ c, ((lo // 2) ^ m) * plan.nz, (hi ^ a) * plan.rows, 0)
        block = lax.dynamic_slice(right_side[0], at, (1, plan.nz, plan.rows, ny))
        blocks.append(lax.ppermute(block.reshape(size, ny), FLAT, plan.pairs(a, m, c)))

    packed = kernel_call(
        functools.partial(pack_coefs, plan),
        (4 * half_z * plan.tiles * TILE, ny),
        (place, diffusivity.reshape(half_z * nx, ny), velocity.reshape(3 * half_z * nx, ny)),
    )
    other = lax.ppermute(packed, "space", [(i, cores - 1 - i) for i in range(cores)])
    coefs = kernel_call(
        functools.partial(make_coefs, plan),
        (plan.ext * plan.tiles * COEFS * TILE, ny),
        (place, packed, other),
    )

    sides = 1 if plan.z_parts == 2 else 2
    edge_x = (GHOST * steps * plan.nz, ny)
    edge_z = (GHOST * steps * plan.rows, ny)
    field, x_even, x_odd, *z_sends = kernel_call(
        functools.partial(gather_steps, plan),
        [(steps * size, ny), edge_x, edge_x] + [edge_z] * sides,
        (place, *blocks),
    )
    even = lax.ppermute(x_even, FLAT, plan.x_pairs(0))
    odd = lax.ppermute(x_odd, FLAT, plan.x_pairs(1))
    z_in = [lax.ppermute(send, FLAT, plan.z_pairs(first)) for first, send in enumerate(z_sends)]
    corner = ((GHOST - 1) * steps * TILE, ny)
    planes, *corners = kernel_call(
        functools.partial(gather_ghosts, plan),
        [(TILE * steps * plan.nz, ny)] + [corner] * sides,
        (place, even, odd),
    )
    c_in = [lax.ppermute(send, FLAT, plan.z_pairs(first)) for first, send in enumerate(corners)]

    grid = (plan.ext * plan.tiles * steps * TILE, ny)
    solved = kernel_call(
        functools.partial(sweep_kernel, plan),
        [(size, ny)] * steps,
        (place, coefs, field, planes, *z_in, *c_in),
        scratch=[pltpu.VMEM(grid, jnp.float32)] * 3 + [pltpu.VMEM((steps * size, ny), jnp.float32)],
    )
    back = []
    for block, (a, m, c) in zip(solved, plan.rounds):
        pairs = [(target, source) for source, target in plan.pairs(a, m, c)]
        back.append(lax.ppermute(block, FLAT, pairs).reshape(plan.nz, plan.rows, ny))

    out = pl.pallas_call(
        functools.partial(place_blocks, plan),
        out_shape=jax.ShapeDtypeStruct((parts, half_z, nx, ny), jnp.float32),
        in_specs=[pl.BlockSpec(memory_space=pltpu.SMEM)] + [pl.BlockSpec(memory_space=pl.ANY)] * steps,
        out_specs=pl.BlockSpec(memory_space=pl.ANY),
        scratch_shapes=[pltpu.SemaphoreType.DMA((steps,))],
    )(place, *back)
    return out[None]


def solution(mesh):
    placed = (
        P(("group", "tm"), None, "space", None, None),
        P("space", None, None),
        P(None, "space", None, None),
    )
    return jax.shard_map(
        local,
        mesh=mesh,
        in_specs=placed,
        out_specs=P(("group", "tm"), None, "space", None, None),
        check_vma=False,
    )
```

time: 229 us -> 120 us (0.52)
  the two profiles are of different devices: /device:TPU:8 before, /device:TPU:1 now
where the time goes in v1:
time: 120 us
  Pallas kernels  45.2 us (38%)
  starting transfers between devices  35.5 us (30%)
  waiting for transfers between devices  35 us (29%)
  local copies, waits for them, and re-layouts  3.57 us (3%)
    pallas_call x1, Pallas kernels, local(): pl.pallas_call(functools.partial(place_blocks, plan), out_shape=jax.Shape...  33.6 us
    ppermute x8, starting transfers between devices, local(): lax.ppermute(block.reshape(size, ny), FLAT, plan.pairs(a, m, c))  17.7 us
    ppermute x8, starting transfers between devices, local(): lax.ppermute(block, FLAT, pairs).reshape(plan.nz, plan.rows, ny)  16.4 us
    ppermute x8, waiting for transfers between devices, local(): lax.ppermute(block, FLAT, pairs).reshape(plan.nz, plan.rows, ny)  14.3 us
    ppermute x8, waiting for transfers between devices, local(): lax.ppermute(block.reshape(size, ny), FLAT, plan.pairs(a, m, c))  13.8 us
    pallas_call x5, Pallas kernels, kernel_call(): pl.pallas_call(body, out_shape=[jax.ShapeDtypeStruct(s, jnp.float32) for...  11.6 us
    ppermute x1, waiting for transfers between devices, local(): even = lax.ppermute(x_even, FLAT, plan.x_pairs(0))  5.42 us
    unnamed x24, local copies, waits for them, and re-layouts  3.46 us
  transfers between devices with their start and end apart: 21, of which 9 were waited for; matrix products, arithmetic and copies ran while one was open for 0% of the time, Pallas kernels for 2%

profile of v1, /device:TPU:1, one launch (start us, length us, event | category | flops | bytes accessed | tf_op | source)
XLA Modules:
  0.0 119.5 jit_solution(9842575308261394685)
XLA Ops:
  0.1 1.4 %copy-done = f32[3,16,64,128]{3,2,1,0:T(8,128)S(1)} copy-done((f32[3,16,64,128]{3,2,1,0:T(8,128)S(1)}, f32[3,16,64,128]{3,2,1,0:T(8,128)}, u32[]{:S(2)}) %copy-start) | copy-done | bytes 1572888
  1.5 1.0 copy-done.1
  2.5 0.7 shard_map.37.own_ref
  3.9 3.4 %collective-permute-start.6 = (f32[256,128]{1,0:T(8,128)S(1)}, f32[256,128]{1,0:T(8,128)S(1)}, u32[]{:S(2)}, u32[]{:S(2)}) collective-permute-start(f32[256,128]{1,0:T(8,128)S(1)} %bitcast.38), channel_id=1, source_target_pairs={{0,5},{1,7},{2,4},{3,6},{4,1},{5,3},{6,0},{7,2},{8,13},{9,15},{10,... | collective-permute-start | bytes 393224 | tf_op jit(solution)/shard_map/ppermute | solution.py:372
  8.1 3.3 %collective-permute-start.4 = (f32[256,128]{1,0:T(8,128)S(1)}, f32[256,128]{1,0:T(8,128)S(1)}, u32[]{:S(2)}, u32[]{:S(2)}) collective-permute-start(f32[256,128]{1,0:T(8,128)S(1)} %bitcast.32), channel_id=1, source_target_pairs={{0,13},{1,15},{2,12},{3,14},{4,9},{5,11},{6,8},{7,10},{8,5},{9,7},... | collective-permute-start | bytes 393224 | tf_op jit(solution)/shard_map/ppermute | solution.py:372
  11.4 3.5 %collective-permute-start.3 = (f32[256,128]{1,0:T(8,128)S(1)}, f32[256,128]{1,0:T(8,128)S(1)}, u32[]{:S(2)}, u32[]{:S(2)}) collective-permute-start(f32[256,128]{1,0:T(8,128)S(1)} %bitcast.29), channel_id=1, source_target_pairs={{0,12},{1,14},{2,13},{3,15},{4,8},{5,10},{6,9},{7,11},{8,4},{9,6},... | collective-permute-start | bytes 393224 | tf_op jit(solution)/shard_map/ppermute | solution.py:372
  14.9 2.9 %collective-permute-start.2 = (f32[256,128]{1,0:T(8,128)S(1)}, f32[256,128]{1,0:T(8,128)S(1)}, u32[]{:S(2)}, u32[]{:S(2)}) collective-permute-start(f32[256,128]{1,0:T(8,128)S(1)} %bitcast.27), channel_id=1, source_target_pairs={{0,9},{1,11},{2,8},{3,10},{4,13},{5,15},{6,12},{7,14},{8,1},{9,3},... | collective-permute-start | bytes 393224 | tf_op jit(solution)/shard_map/ppermute | solution.py:372
  17.8 1.8 %collective-permute-start.1 = (f32[256,128]{1,0:T(8,128)S(1)}, f32[256,128]{1,0:T(8,128)S(1)}, u32[]{:S(2)}, u32[]{:S(2)}) collective-permute-start(f32[256,128]{1,0:T(8,128)S(1)} %bitcast.25), channel_id=1, source_target_pairs={{0,8},{1,10},{2,9},{3,11},{4,12},{5,14},{6,13},{7,15},{8,0},{9,2},... | collective-permute-start | bytes 393224 | tf_op jit(solution)/shard_map/ppermute | solution.py:372
  19.7 1.9 %collective-permute-start.7 = (f32[256,128]{1,0:T(8,128)S(1)}, f32[256,128]{1,0:T(8,128)S(1)}, u32[]{:S(2)}, u32[]{:S(2)}) collective-permute-start(f32[256,128]{1,0:T(8,128)S(1)} %bitcast.24), channel_id=1, source_target_pairs={{0,0},{1,2},{2,1},{3,3},{4,4},{5,6},{6,5},{7,7},{8,8},{9,10},{10,9... | collective-permute-start | bytes 393224 | tf_op jit(solution)/shard_map/ppermute | solution.py:372
  21.6 0.9 collective-permute-done.3.refs_2_
  22.5 10.3 %collective-permute-done.2.refs_1_ = f32[256,128]{1,0:T(8,128)S(1)} collective-permute-done((f32[256,128]{1,0:T(8,128)S(1)}, f32[256,128]{1,0:T(8,128)S(1)}, u32[]{:S(2)}, u32[]{:S(2)}) %collective-permute-start.2) | collective-permute-done | bytes 131104 | tf_op jit(solution)/shard_map/ppermute | solution.py:372
  32.8 2.5 %collective-permute-done.1.refs_0_ = f32[256,128]{1,0:T(8,128)S(1)} collective-permute-done((f32[256,128]{1,0:T(8,128)S(1)}, f32[256,128]{1,0:T(8,128)S(1)}, u32[]{:S(2)}, u32[]{:S(2)}) %collective-permute-start.1) | collective-permute-done | bytes 131104 | tf_op jit(solution)/shard_map/ppermute | solution.py:372
  35.3 0.7 shard_map.39
  37.2 5.4 %collective-permute-done.9.even_ref = f32[384,128]{1,0:T(8,128)S(1)} collective-permute-done((f32[384,128]{1,0:T(8,128)S(1)}, f32[384,128]{1,0:T(8,128)S(1)}, u32[]{:S(2)}, u32[]{:S(2)}) %collective-permute-start.9) | collective-permute-done | bytes 196640 | tf_op jit(solution)/shard_map/ppermute | solution.py:394
  43.4 1.5 %shard_map.38.coefs = f32[4752,128]{1,0:T(8,128)S(1)} custom-call(s32[3]{0:T(128)S(1)} %pad_add_fusion.place, f32[1536,128]{1,0:T(8,128)S(1)} %shard_map.37.own_ref, f32[1536,128]{1,0:T(8,128)S(1)} %collective-permute-done.other_ref), custom_call_target="tpu_custom_call" | custom-call | tf_op jit(solution)/shard_map/pallas_call | solution.py:77
  44.9 1.5 %collective-permute-done.12.refs_1_ = f32[128,128]{1,0:T(8,128)S(1)} collective-permute-done((f32[128,128]{1,0:T(8,128)S(1)}, f32[128,128]{1,0:T(8,128)S(1)}, u32[]{:S(2)}, u32[]{:S(2)}) %collective-permute-start.12) | collective-permute-done | bytes 65568 | tf_op jit(solution)/shard_map/ppermute | solution.py:403
  46.4 8.0 %shard_map.41 = (f32[256,128]{1,0:T(8,128)S(1)}, f32[256,128]{1,0:T(8,128)S(1)}, f32[256,128]{1,0:T(8,128)S(1)}, f32[256,128]{1,0:T(8,128)S(1)}, f32[256,128]{1,...) custom-call(s32[3]{0:T(128)S(1)} %pad_add_fusion.place, ...), custom_call_target="tpu_custom_call" | custom-call | tf_op jit(solution)/shard_map/pallas_call | solution.py:77
  54.5 6.1 %collective-permute-start.13 = (f32[256,128]{1,0:T(8,128)S(1)}, f32[256,128]{1,0:T(8,128)S(1)}, u32[]{:S(2)}, u32[]{:S(2)}) collective-permute-start(f32[256,128]{1,0:T(8,128)S(1)} %get-tuple-element.25), channel_id=1, source_target_pairs={{8,0},{10,1},{9,2},{11,3},{12,4},{14,5},{13,6},{15,7},{0,8},{2,9},... | collective-permute-start | bytes 393224 | tf_op jit(solution)/shard_map/ppermute | solution.py:415
  60.9 3.7 %collective-permute-start.16 = (f32[256,128]{1,0:T(8,128)S(1)}, f32[256,128]{1,0:T(8,128)S(1)}, u32[]{:S(2)}, u32[]{:S(2)}) collective-permute-start(f32[256,128]{1,0:T(8,128)S(1)} %get-tuple-element.28), channel_id=1, source_target_pairs={{13,0},{15,1},{12,2},{14,3},{9,4},{11,5},{8,6},{10,7},{5,8},{7,9},... | collective-permute-start | bytes 393224 | tf_op jit(solution)/shard_map/ppermute | solution.py:415
  64.8 9.9 %collective-permute-done.13 = f32[256,128]{1,0:T(8,128)S(1)} collective-permute-done((f32[256,128]{1,0:T(8,128)S(1)}, f32[256,128]{1,0:T(8,128)S(1)}, u32[]{:S(2)}, u32[]{:S(2)}) %collective-permute-start.13) | collective-permute-done | bytes 131104 | tf_op jit(solution)/shard_map/ppermute | solution.py:415
  75.2 6.0 %collective-permute-start.19 = (f32[256,128]{1,0:T(8,128)S(1)}, f32[256,128]{1,0:T(8,128)S(1)}, u32[]{:S(2)}, u32[]{:S(2)}) collective-permute-start(f32[256,128]{1,0:T(8,128)S(1)} %get-tuple-element.31), channel_id=1, source_target_pairs={{0,0},{2,1},{1,2},{3,3},{4,4},{6,5},{5,6},{7,7},{8,8},{10,9},{9,10... | collective-permute-start | bytes 393224 | tf_op jit(solution)/shard_map/ppermute | solution.py:415
  81.3 2.7 %collective-permute-done.19 = f32[256,128]{1,0:T(8,128)S(1)} collective-permute-done((f32[256,128]{1,0:T(8,128)S(1)}, f32[256,128]{1,0:T(8,128)S(1)}, u32[]{:S(2)}, u32[]{:S(2)}) %collective-permute-start.19) | collective-permute-done | bytes 131104 | tf_op jit(solution)/shard_map/ppermute | solution.py:415
  84.0 1.2 %collective-permute-done.20 = f32[256,128]{1,0:T(8,128)S(1)} collective-permute-done((f32[256,128]{1,0:T(8,128)S(1)}, f32[256,128]{1,0:T(8,128)S(1)}, u32[]{:S(2)}, u32[]{:S(2)}) %collective-permute-start.20) | collective-permute-done | bytes 131104 | tf_op jit(solution)/shard_map/ppermute | solution.py:415
  85.9 33.6 %shard_map.42 = f32[2,16,64,128]{3,2,1,0:T(8,128)} custom-call(s32[3]{0:T(128)} %copy-done.2, f32[16,16,128]{2,1,0:T(8,128)} %bitcast.26, f32[16,16,128]{2,1,0:T(8,128)} %bitcast.28, f32[16,16,128]{2,1,0:T(8,128)} %bitcast.30, f32[16,16,128]{2,1,0:T(8,128)} %bitcast.31, f32[16,16,128]{2,1,0:T(8,128)} %bitcast.33, f32[16,16,128]{2,1,0:T(8,128)} %bitcast.35, ...), custom_call_target="tpu_custom_call" | custom-call | tf_op jit(solution)/shard_map/pallas_call | solution.py:417
  (50 shorter events, 5.1 us)
Async XLA Ops:
  0.1 46.4 %copy-start.2 = (s32[3]{0:T(128)}, s32[3]{0:T(128)S(1)}, u32[]{:S(2)}) copy-start(s32[3]{0:T(128)S(1)} %pad_add_fusion.place) | copy-start | bytes 40
  3.2 40.2 %collective-permute-start = (f32[1536,128]{1,0:T(8,128)S(1)}, f32[1536,128]{1,0:T(8,128)S(1)}, u32[]{:S(2)}, u32[]{:S(2)}) collective-permute-start(f32[1536,128]{1,0:T(8,128)S(1)} %shard_map.37.own_ref), channel_id=1, source_target_pairs={{0,1},{1,0},{2,3},{3,2},{4,5},{5,4},{6,7},{7,6},{8,9},{9,8},{10,11... | collective-permute-start | bytes 2359304 | tf_op jit(solution)/shard_map/ppermute | solution.py:379
  3.9 7.5 %collective-permute-start.6 = (f32[256,128]{1,0:T(8,128)S(1)}, f32[256,128]{1,0:T(8,128)S(1)}, u32[]{:S(2)}, u32[]{:S(2)}) collective-permute-start(f32[256,128]{1,0:T(8,128)S(1)} %bitcast.38), channel_id=1, source_target_pairs={{0,5},{1,7},{2,4},{3,6},{4,1},{5,3},{6,0},{7,2},{8,13},{9,15},{10,... | collective-permute-start | bytes 393224 | tf_op jit(solution)/shard_map/ppermute | solution.py:372
  7.2 7.7 %collective-permute-start.8 = (f32[256,128]{1,0:T(8,128)S(1)}, f32[256,128]{1,0:T(8,128)S(1)}, u32[]{:S(2)}, u32[]{:S(2)}) collective-permute-start(f32[256,128]{1,0:T(8,128)S(1)} %bitcast.36), channel_id=1, source_target_pairs={{0,1},{1,3},{2,0},{3,2},{4,5},{5,7},{6,4},{7,6},{8,9},{9,11},{10,8... | collective-permute-start | bytes 393224 | tf_op jit(solution)/shard_map/ppermute | solution.py:372
  7.9 10.0 %collective-permute-start.5 = (f32[256,128]{1,0:T(8,128)S(1)}, f32[256,128]{1,0:T(8,128)S(1)}, u32[]{:S(2)}, u32[]{:S(2)}) collective-permute-start(f32[256,128]{1,0:T(8,128)S(1)} %bitcast.34), channel_id=1, source_target_pairs={{0,4},{1,6},{2,5},{3,7},{4,0},{5,2},{6,1},{7,3},{8,12},{9,14},{10,... | collective-permute-start | bytes 393224 | tf_op jit(solution)/shard_map/ppermute | solution.py:372
  8.1 11.6 %collective-permute-start.4 = (f32[256,128]{1,0:T(8,128)S(1)}, f32[256,128]{1,0:T(8,128)S(1)}, u32[]{:S(2)}, u32[]{:S(2)}) collective-permute-start(f32[256,128]{1,0:T(8,128)S(1)} %bitcast.32), channel_id=1, source_target_pairs={{0,13},{1,15},{2,12},{3,14},{4,9},{5,11},{6,8},{7,10},{8,5},{9,7},... | collective-permute-start | bytes 393224 | tf_op jit(solution)/shard_map/ppermute | solution.py:372
  11.4 11.1 %collective-permute-start.3 = (f32[256,128]{1,0:T(8,128)S(1)}, f32[256,128]{1,0:T(8,128)S(1)}, u32[]{:S(2)}, u32[]{:S(2)}) collective-permute-start(f32[256,128]{1,0:T(8,128)S(1)} %bitcast.29), channel_id=1, source_target_pairs={{0,12},{1,14},{2,13},{3,15},{4,8},{5,10},{6,9},{7,11},{8,4},{9,6},... | collective-permute-start | bytes 393224 | tf_op jit(solution)/shard_map/ppermute | solution.py:372
  14.9 17.9 %collective-permute-start.2 = (f32[256,128]{1,0:T(8,128)S(1)}, f32[256,128]{1,0:T(8,128)S(1)}, u32[]{:S(2)}, u32[]{:S(2)}) collective-permute-start(f32[256,128]{1,0:T(8,128)S(1)} %bitcast.27), channel_id=1, source_target_pairs={{0,9},{1,11},{2,8},{3,10},{4,13},{5,15},{6,12},{7,14},{8,1},{9,3},... | collective-permute-start | bytes 393224 | tf_op jit(solution)/shard_map/ppermute | solution.py:372
  17.8 17.5 %collective-permute-start.1 = (f32[256,128]{1,0:T(8,128)S(1)}, f32[256,128]{1,0:T(8,128)S(1)}, u32[]{:S(2)}, u32[]{:S(2)}) collective-permute-start(f32[256,128]{1,0:T(8,128)S(1)} %bitcast.25), channel_id=1, source_target_pairs={{0,8},{1,10},{2,9},{3,11},{4,12},{5,14},{6,13},{7,15},{8,0},{9,2},... | collective-permute-start | bytes 393224 | tf_op jit(solution)/shard_map/ppermute | solution.py:372
  19.7 15.7 %collective-permute-start.7 = (f32[256,128]{1,0:T(8,128)S(1)}, f32[256,128]{1,0:T(8,128)S(1)}, u32[]{:S(2)}, u32[]{:S(2)}) collective-permute-start(f32[256,128]{1,0:T(8,128)S(1)} %bitcast.24), channel_id=1, source_target_pairs={{0,0},{1,2},{2,1},{3,3},{4,4},{5,6},{6,5},{7,7},{8,8},{9,10},{10,9... | collective-permute-start | bytes 393224 | tf_op jit(solution)/shard_map/ppermute | solution.py:372
  36.1 6.5 %collective-permute-start.9 = (f32[384,128]{1,0:T(8,128)S(1)}, f32[384,128]{1,0:T(8,128)S(1)}, u32[]{:S(2)}, u32[]{:S(2)}) collective-permute-start(f32[384,128]{1,0:T(8,128)S(1)} %get-tuple-element.20), channel_id=1, source_target_pairs={{0,4},{4,0},{1,5},{5,1},{2,6},{6,2},{3,7},{7,3},{8,12},{12,8},{9,1... | collective-permute-start | bytes 589832 | tf_op jit(solution)/shard_map/ppermute | solution.py:394
  36.1 6.5 %collective-permute-start.10 = (f32[384,128]{1,0:T(8,128)S(1)}, f32[384,128]{1,0:T(8,128)S(1)}, u32[]{:S(2)}, u32[]{:S(2)}) collective-permute-start(f32[384,128]{1,0:T(8,128)S(1)} %get-tuple-element.21), channel_id=1, source_target_pairs={{4,8},{8,4},{5,9},{9,5},{6,10},{10,6},{7,11},{11,7},{20,24},{24,20... | collective-permute-start | bytes 589832 | tf_op jit(solution)/shard_map/ppermute | solution.py:395
  36.8 8.1 %collective-permute-start.11 = (f32[384,128]{1,0:T(8,128)S(1)}, f32[384,128]{1,0:T(8,128)S(1)}, u32[]{:S(2)}, u32[]{:S(2)}) collective-permute-start(f32[384,128]{1,0:T(8,128)S(1)} %get-tuple-element.23), channel_id=1, source_target_pairs={{0,2},{2,0},{1,3},{3,1},{4,6},{6,4},{5,7},{7,5},{8,10},{10,8},{9,1... | collective-permute-start | bytes 589832 | tf_op jit(solution)/shard_map/ppermute | solution.py:396
  43.3 3.2 %collective-permute-start.12 = (f32[128,128]{1,0:T(8,128)S(1)}, f32[128,128]{1,0:T(8,128)S(1)}, u32[]{:S(2)}, u32[]{:S(2)}) collective-permute-start(f32[128,128]{1,0:T(8,128)S(1)} %get-tuple-element.24), channel_id=1, source_target_pairs={{0,2},{2,0},{1,3},{3,1},{4,6},{6,4},{5,7},{7,5},{8,10},{10,8},{9,1... | collective-permute-start | bytes 196616 | tf_op jit(solution)/shard_map/ppermute | solution.py:403
  54.5 20.2 %collective-permute-start.13 = (f32[256,128]{1,0:T(8,128)S(1)}, f32[256,128]{1,0:T(8,128)S(1)}, u32[]{:S(2)}, u32[]{:S(2)}) collective-permute-start(f32[256,128]{1,0:T(8,128)S(1)} %get-tuple-element.25), channel_id=1, source_target_pairs={{8,0},{10,1},{9,2},{11,3},{12,4},{14,5},{13,6},{15,7},{0,8},{2,9},... | collective-permute-start | bytes 393224 | tf_op jit(solution)/shard_map/ppermute | solution.py:415
  60.6 14.6 %collective-permute-start.14 = (f32[256,128]{1,0:T(8,128)S(1)}, f32[256,128]{1,0:T(8,128)S(1)}, u32[]{:S(2)}, u32[]{:S(2)}) collective-permute-start(f32[256,128]{1,0:T(8,128)S(1)} %get-tuple-element.26), channel_id=1, source_target_pairs={{9,0},{11,1},{8,2},{10,3},{13,4},{15,5},{12,6},{14,7},{1,8},{3,9},... | collective-permute-start | bytes 393224 | tf_op jit(solution)/shard_map/ppermute | solution.py:415
  60.6 20.6 %collective-permute-start.15 = (f32[256,128]{1,0:T(8,128)S(1)}, f32[256,128]{1,0:T(8,128)S(1)}, u32[]{:S(2)}, u32[]{:S(2)}) collective-permute-start(f32[256,128]{1,0:T(8,128)S(1)} %get-tuple-element.27), channel_id=1, source_target_pairs={{12,0},{14,1},{13,2},{15,3},{8,4},{10,5},{9,6},{11,7},{4,8},{6,9},... | collective-permute-start | bytes 393224 | tf_op jit(solution)/shard_map/ppermute | solution.py:415
  60.9 20.4 %collective-permute-start.16 = (f32[256,128]{1,0:T(8,128)S(1)}, f32[256,128]{1,0:T(8,128)S(1)}, u32[]{:S(2)}, u32[]{:S(2)}) collective-permute-start(f32[256,128]{1,0:T(8,128)S(1)} %get-tuple-element.28), channel_id=1, source_target_pairs={{13,0},{15,1},{12,2},{14,3},{9,4},{11,5},{8,6},{10,7},{5,8},{7,9},... | collective-permute-start | bytes 393224 | tf_op jit(solution)/shard_map/ppermute | solution.py:415
  64.5 16.8 %collective-permute-start.17 = (f32[256,128]{1,0:T(8,128)S(1)}, f32[256,128]{1,0:T(8,128)S(1)}, u32[]{:S(2)}, u32[]{:S(2)}) collective-permute-start(f32[256,128]{1,0:T(8,128)S(1)} %get-tuple-element.29), channel_id=1, source_target_pairs={{4,0},{6,1},{5,2},{7,3},{0,4},{2,5},{1,6},{3,7},{12,8},{14,9},{13,... | collective-permute-start | bytes 393224 | tf_op jit(solution)/shard_map/ppermute | solution.py:415
  74.8 10.5 %copy-start.4 = (f32[256,128]{1,0:T(8,128)}, f32[256,128]{1,0:T(8,128)S(1)}, u32[]{:S(2)}) copy-start(f32[256,128]{1,0:T(8,128)S(1)} %collective-permute-done.13) | copy-start | bytes 393220
  74.8 6.5 %collective-permute-start.18 = (f32[256,128]{1,0:T(8,128)S(1)}, f32[256,128]{1,0:T(8,128)S(1)}, u32[]{:S(2)}, u32[]{:S(2)}) collective-permute-start(f32[256,128]{1,0:T(8,128)S(1)} %get-tuple-element.30), channel_id=1, source_target_pairs={{5,0},{7,1},{4,2},{6,3},{1,4},{3,5},{0,6},{2,7},{13,8},{15,9},{12,... | collective-permute-start | bytes 393224 | tf_op jit(solution)/shard_map/ppermute | solution.py:415
  75.2 10.1 %copy-start.5 = (f32[256,128]{1,0:T(8,128)}, f32[256,128]{1,0:T(8,128)S(1)}, u32[]{:S(2)}) copy-start(f32[256,128]{1,0:T(8,128)S(1)} %collective-permute-done.14) | copy-start | bytes 393220
  75.2 8.8 %collective-permute-start.19 = (f32[256,128]{1,0:T(8,128)S(1)}, f32[256,128]{1,0:T(8,128)S(1)}, u32[]{:S(2)}, u32[]{:S(2)}) collective-permute-start(f32[256,128]{1,0:T(8,128)S(1)} %get-tuple-element.31), channel_id=1, source_target_pairs={{0,0},{2,1},{1,2},{3,3},{4,4},{6,5},{5,6},{7,7},{8,8},{10,9},{9,10... | collective-permute-start | bytes 393224 | tf_op jit(solution)/shard_map/ppermute | solution.py:415
  81.2 4.0 %collective-permute-start.20 = (f32[256,128]{1,0:T(8,128)S(1)}, f32[256,128]{1,0:T(8,128)S(1)}, u32[]{:S(2)}, u32[]{:S(2)}) collective-permute-start(f32[256,128]{1,0:T(8,128)S(1)} %get-tuple-element.32), channel_id=1, source_target_pairs={{1,0},{3,1},{0,2},{2,3},{5,4},{7,5},{4,6},{6,7},{9,8},{11,9},{8,10... | collective-permute-start | bytes 393224 | tf_op jit(solution)/shard_map/ppermute | solution.py:415
  (9 other events, 21.6 us)

commit v2 on v1

--- a/solution.py
+++ b/solution.py
@@ -29,8 +29,8 @@
         self.main = self.rows // TILE
         self.tiles = self.main + 1
         self.ext = self.nz + 2 * GHOST
-        order = [2, 3, 1, 0]
-        self.rounds = [(a, m, c) for a in order for m in range(self.in_half) for c in range(2)]
+        kinds = [(2, 0), (1, 0), (1, 1), (0, 0), (2, 1), (3, 0), (3, 1), (0, 1)]
+        self.rounds = [(a, m, c) for m in range(self.in_half) for a, c in kinds]
 
     def flat(self, hi, zb, s):
         return (hi * self.z_parts + zb) * self.cores + s
@@ -68,19 +68,18 @@
         return ((hi ^ a) * self.in_half + ((zb % self.in_half) ^ m)) * 2 + (s ^ c)
 
 
-def kernel_call(body, outs, args, scalars=True, scratch=(), cost=None):
-    in_specs = [pl.BlockSpec(memory_space=pltpu.VMEM)] * len(args)
-    if scalars:
-        in_specs[0] = pl.BlockSpec(memory_space=pltpu.SMEM)
+def kernel_call(body, outs, args, scratch=(), out_space=pltpu.VMEM, limit=16):
+    in_specs = [pl.BlockSpec(memory_space=pltpu.SMEM)]
+    in_specs += [pl.BlockSpec(memory_space=pltpu.VMEM)] * (len(args) - 1)
     single = isinstance(outs, tuple)
     shapes = [outs] if single else list(outs)
     result = pl.pallas_call(
         body,
         out_shape=[jax.ShapeDtypeStruct(s, jnp.float32) for s in shapes],
         in_specs=in_specs,
-        out_specs=[pl.BlockSpec(memory_space=pltpu.VMEM)] * len(shapes),
+        out_specs=[pl.BlockSpec(memory_space=out_space)] * len(shapes),
         scratch_shapes=list(scratch),
-        compiler_params=pltpu.CompilerParams(vmem_limit_bytes=40 << 20),
+        compiler_params=pltpu.CompilerParams(vmem_limit_bytes=limit << 20),
     )(*args)
     return result[0] if single else result
 
@@ -340,6 +339,18 @@
         out[...] = last[pl.ds(pl.multiple_of(step * size, TILE), size), :]
 
 
+def run_sweeps(plan, place, arrays):
+    size = plan.nz * plan.rows
+    grid = (plan.ext * plan.tiles * plan.steps * TILE, plan.ny)
+    return kernel_call(
+        functools.partial(sweep_kernel, plan),
+        [(size, plan.ny)] * plan.steps,
+        (place, *arrays),
+        scratch=[pltpu.VMEM(grid, jnp.float32)] * 3 + [pltpu.VMEM((plan.steps * size, plan.ny), jnp.float32)],
+        limit=24,
+    )
+
+
 def place_blocks(plan, place, *refs):
     blocks, out, sems = refs[: plan.steps], refs[plan.steps], refs[plan.steps + 1]
     hi, lo = place[0], place[1]
@@ -371,18 +382,6 @@
         block = lax.dynamic_slice(right_side[0], at, (1, plan.nz, plan.rows, ny))
         blocks.append(lax.ppermute(block.reshape(size, ny), FLAT, plan.pairs(a, m, c)))
 
-    packed = kernel_call(
-        functools.partial(pack_coefs, plan),
-        (4 * half_z * plan.tiles * TILE, ny),
-        (place, diffusivity.reshape(half_z * nx, ny), velocity.reshape(3 * half_z * nx, ny)),
-    )
-    other = lax.ppermute(packed, "space", [(i, cores - 1 - i) for i in range(cores)])
-    coefs = kernel_call(
-        functools.partial(make_coefs, plan),
-        (plan.ext * plan.tiles * COEFS * TILE, ny),
-        (place, packed, other),
-    )
-
     sides = 1 if plan.z_parts == 2 else 2
     edge_x = (GHOST * steps * plan.nz, ny)
     edge_z = (GHOST * steps * plan.rows, ny)
@@ -391,9 +390,22 @@
         [(steps * size, ny), edge_x, edge_x] + [edge_z] * sides,
         (place, *blocks),
     )
+    z_in = [lax.ppermute(send, FLAT, plan.z_pairs(first)) for first, send in enumerate(z_sends)]
     even = lax.ppermute(x_even, FLAT, plan.x_pairs(0))
     odd = lax.ppermute(x_odd, FLAT, plan.x_pairs(1))
-    z_in = [lax.ppermute(send, FLAT, plan.z_pairs(first)) for first, send in enumerate(z_sends)]
+    after, field = lax.optimization_barrier((diffusivity, field))
+    packed = kernel_call(
+        functools.partial(pack_coefs, plan),
+        (4 * half_z * plan.tiles * TILE, ny),
+        (place, after.reshape(half_z * nx, ny), velocity.reshape(3 * half_z * nx, ny)),
+    )
+    other = lax.ppermute(packed, "space", [(i, cores - 1 - i) for i in range(cores)])
+    coefs = kernel_call(
+        functools.partial(make_coefs, plan),
+        (plan.ext * plan.tiles * COEFS * TILE, ny),
+        (place, packed, other),
+    )
+
     corner = ((GHOST - 1) * steps * TILE, ny)
     planes, *corners = kernel_call(
         functools.partial(gather_ghosts, plan),
@@ -402,25 +414,19 @@
     )
     c_in = [lax.ppermute(send, FLAT, plan.z_pairs(first)) for first, send in enumerate(corners)]
 
-    grid = (plan.ext * plan.tiles * steps * TILE, ny)
-    solved = kernel_call(
-        functools.partial(sweep_kernel, plan),
-        [(size, ny)] * steps,
-        (place, coefs, field, planes, *z_in, *c_in),
-        scratch=[pltpu.VMEM(grid, jnp.float32)] * 3 + [pltpu.VMEM((steps * size, ny), jnp.float32)],
-    )
+    solved = run_sweeps(plan, place, [coefs, field, planes, *z_in, *c_in])
     back = []
     for block, (a, m, c) in zip(solved, plan.rounds):
         pairs = [(target, source) for source, target in plan.pairs(a, m, c)]
         back.append(lax.ppermute(block, FLAT, pairs).reshape(plan.nz, plan.rows, ny))
 
-    out = pl.pallas_call(
+    out = kernel_call(
         functools.partial(place_blocks, plan),
-        out_shape=jax.ShapeDtypeStruct((parts, half_z, nx, ny), jnp.float32),
-        in_specs=[pl.BlockSpec(memory_space=pltpu.SMEM)] + [pl.BlockSpec(memory_space=pl.ANY)] * steps,
-        out_specs=pl.BlockSpec(memory_space=pl.ANY),
-        scratch_shapes=[pltpu.SemaphoreType.DMA((steps,))],
-    )(place, *back)
+        (parts, half_z, nx, ny),
+        (place, *back),
+        scratch=[pltpu.SemaphoreType.DMA((steps,))],
+        out_space=pl.ANY,
+    )
     return out[None]
 
 

time: 120 us -> 80.7 us (0.67)
  the two profiles are of different devices: /device:TPU:1 before, /device:TPU:8 now
where the time goes in v2:
time: 80.7 us; the launch traced here: 79.6 us
  waiting for transfers between devices  38.1 us (47%)
  starting transfers between devices  25.9 us (32%)
  Pallas kernels  13.2 us (16%)
  local copies, waits for them, and re-layouts  2.23 us (3%)
    ppermute x8, waiting for transfers between devices, local(): lax.ppermute(block.reshape(size, ny), FLAT, plan.pairs(a, m, c))  17.9 us
    pallas_call x6, Pallas kernels, kernel_call(): pl.pallas_call(body, out_shape=[jax.ShapeDtypeStruct(s, jnp.float32) for...  13.2 us
    ppermute x8, waiting for transfers between devices, local(): lax.ppermute(block, FLAT, pairs).reshape(plan.nz, plan.rows, ny)  12.5 us
    ppermute x8, starting transfers between devices, local(): lax.ppermute(block, FLAT, pairs).reshape(plan.nz, plan.rows, ny)  11.8 us
    ppermute x8, starting transfers between devices, local(): lax.ppermute(block.reshape(size, ny), FLAT, plan.pairs(a, m, c))  9.72 us
    ppermute x1, waiting for transfers between devices, local(): even = lax.ppermute(x_even, FLAT, plan.x_pairs(0))  3.47 us
    ppermute x1, starting transfers between devices, local(): odd = lax.ppermute(x_odd, FLAT, plan.x_pairs(1))  2.62 us
    ppermute x2, waiting for transfers between devices, local(): lax.ppermute(send, FLAT, plan.z_pairs(first))  2.36 us
  transfers between devices with their start and end apart: 21, of which 13 were waited for; matrix products, arithmetic and copies ran while one was open for 0% of the time, Pallas kernels for 3%

profile of v2, /device:TPU:8, one launch (start us, length us, event | category | flops | bytes accessed | tf_op | source)
XLA Modules:
  0.0 79.6 jit_solution(4832052386459019194)
XLA Ops:
  0.0 2.2 %constant_dynamic-slice_fusion = (f32[1,1,16,16,128]{4,3,2,1,0:T(8,128)S(1)}, f32[1,1,16,16,128]{4,3,2,1,0:T(8,128)S(1)}, f32[1,1,16,16,128]{4,3,2,1,0:T(8,128)}...) fusion(f32[1,2,16,64,128]{4,3,2,1,0:T(8,128)} %param.3, ...), kind=kLoop, calls=%fused_computation | loop fusion | bytes 2097176 | tf_op jit(solution)/shard_map/dynamic_slice | solution.py:382
  2.2 2.6 %collective-permute-start = (f32[256,128]{1,0:T(8,128)S(1)}, f32[256,128]{1,0:T(8,128)S(1)}, u32[]{:S(2)}, u32[]{:S(2)}) collective-permute-start(f32[256,128]{1,0:T(8,128)S(1)} %bitcast.37), channel_id=1, source_target_pairs={{0,8},{1,10},{2,9},{3,11},{4,12},{5,14},{6,13},{7,15},{8,0},{9,2},... | collective-permute-start | bytes 393224 | tf_op jit(solution)/shard_map/ppermute | solution.py:383
  5.3 1.6 %collective-permute-start.2 = (f32[256,128]{1,0:T(8,128)S(1)}, f32[256,128]{1,0:T(8,128)S(1)}, u32[]{:S(2)}, u32[]{:S(2)}) collective-permute-start(f32[256,128]{1,0:T(8,128)S(1)} %bitcast.35), channel_id=1, source_target_pairs={{0,5},{1,7},{2,4},{3,6},{4,1},{5,3},{6,0},{7,2},{8,13},{9,15},{10,... | collective-permute-start | bytes 393224 | tf_op jit(solution)/shard_map/ppermute | solution.py:383
  6.9 1.6 %collective-permute-start.3 = (f32[256,128]{1,0:T(8,128)}, f32[256,128]{1,0:T(8,128)S(1)}, u32[]{:S(2)}, u32[]{:S(2)}) collective-permute-start(f32[256,128]{1,0:T(8,128)} %bitcast.6), channel_id=1, source_target_pairs={{0,0},{1,2},{2,1},{3,3},{4,4},{5,6},{6,5},{7,7},{8,8},{9,10},{10,9... | collective-permute-start | bytes 393224 | tf_op jit(solution)/shard_map/ppermute | solution.py:383
  8.5 1.9 %collective-permute-start.4 = (f32[256,128]{1,0:T(8,128)}, f32[256,128]{1,0:T(8,128)S(1)}, u32[]{:S(2)}, u32[]{:S(2)}) collective-permute-start(f32[256,128]{1,0:T(8,128)} %bitcast.7), channel_id=1, source_target_pairs={{0,9},{1,11},{2,8},{3,10},{4,13},{5,15},{6,12},{7,14},{8,1},{9,3},... | collective-permute-start | bytes 393224 | tf_op jit(solution)/shard_map/ppermute | solution.py:383
  10.3 1.1 %collective-permute-done.refs_0_ = f32[256,128]{1,0:T(8,128)S(1)} collective-permute-done((f32[256,128]{1,0:T(8,128)S(1)}, f32[256,128]{1,0:T(8,128)S(1)}, u32[]{:S(2)}, u32[]{:S(2)}) %collective-permute-start) | collective-permute-done | bytes 131104 | tf_op jit(solution)/shard_map/ppermute | solution.py:383
  13.1 2.6 %collective-permute-done.2.refs_2_ = f32[256,128]{1,0:T(8,128)S(1)} collective-permute-done((f32[256,128]{1,0:T(8,128)S(1)}, f32[256,128]{1,0:T(8,128)S(1)}, u32[]{:S(2)}, u32[]{:S(2)}) %collective-permute-start.2) | collective-permute-done | bytes 131104 | tf_op jit(solution)/shard_map/ppermute | solution.py:383
  15.7 2.9 %collective-permute-done.4.refs_4_ = f32[256,128]{1,0:T(8,128)S(1)} collective-permute-done((f32[256,128]{1,0:T(8,128)}, f32[256,128]{1,0:T(8,128)S(1)}, u32[]{:S(2)}, u32[]{:S(2)}) %collective-permute-start.4) | collective-permute-done | bytes 131104 | tf_op jit(solution)/shard_map/ppermute | solution.py:383
  18.7 9.3 %collective-permute-done.5.refs_5_ = f32[256,128]{1,0:T(8,128)S(1)} collective-permute-done((f32[256,128]{1,0:T(8,128)S(1)}, f32[256,128]{1,0:T(8,128)S(1)}, u32[]{:S(2)}, u32[]{:S(2)}) %collective-permute-start.5) | collective-permute-done | bytes 131104 | tf_op jit(solution)/shard_map/ppermute | solution.py:383
  27.9 2.0 %collective-permute-done.6.refs_6_ = f32[256,128]{1,0:T(8,128)S(1)} collective-permute-done((f32[256,128]{1,0:T(8,128)S(1)}, f32[256,128]{1,0:T(8,128)S(1)}, u32[]{:S(2)}, u32[]{:S(2)}) %collective-permute-start.6) | collective-permute-done | bytes 131104 | tf_op jit(solution)/shard_map/ppermute | solution.py:383
  31.6 2.6 %collective-permute-start.10 = (f32[384,128]{1,0:T(8,128)S(1)}, f32[384,128]{1,0:T(8,128)S(1)}, u32[]{:S(2)}, u32[]{:S(2)}) collective-permute-start(f32[384,128]{1,0:T(8,128)S(1)} %get-tuple-element.25), channel_id=1, source_target_pairs={{4,8},{8,4},{5,9},{9,5},{6,10},{10,6},{7,11},{11,7},{20,24},{24,20... | collective-permute-start | bytes 589832 | tf_op jit(solution)/shard_map/ppermute | solution.py:395
  34.2 1.1 %collective-permute-start.11 = (f32[384,128]{1,0:T(8,128)S(1)}, f32[384,128]{1,0:T(8,128)S(1)}, u32[]{:S(2)}, u32[]{:S(2)}) collective-permute-start(f32[384,128]{1,0:T(8,128)S(1)} %get-tuple-element.27), channel_id=1, source_target_pairs={{0,2},{2,0},{1,3},{3,1},{4,6},{6,4},{5,7},{7,5},{8,10},{10,8},{9,1... | collective-permute-start | bytes 589832 | tf_op jit(solution)/shard_map/ppermute | solution.py:393
  35.3 3.5 %collective-permute-done.9.even_ref = f32[384,128]{1,0:T(8,128)S(1)} collective-permute-done((f32[384,128]{1,0:T(8,128)S(1)}, f32[384,128]{1,0:T(8,128)S(1)}, u32[]{:S(2)}, u32[]{:S(2)}) %collective-permute-start.9) | collective-permute-done | bytes 196640 | tf_op jit(solution)/shard_map/ppermute | solution.py:394
  38.8 1.9 %collective-permute-done.10.odd_ref = f32[384,128]{1,0:T(8,128)S(1)} collective-permute-done((f32[384,128]{1,0:T(8,128)S(1)}, f32[384,128]{1,0:T(8,128)S(1)}, u32[]{:S(2)}, u32[]{:S(2)}) %collective-permute-start.10) | collective-permute-done | bytes 196640 | tf_op jit(solution)/shard_map/ppermute | solution.py:395
  41.8 1.5 %shard_map.39.coefs = f32[4752,128]{1,0:T(8,128)S(1)} custom-call(s32[3]{0:T(128)S(1)} %pad_add_fusion.place, f32[1536,128]{1,0:T(8,128)S(1)} %shard_map.38.own_ref, f32[1536,128]{1,0:T(8,128)S(1)} %collective-permute-done.8.other_ref), custom_call_target="tpu_custom_call" | custom-call | tf_op jit(solution)/shard_map/pallas_call | solution.py:76
  43.3 2.4 %collective-permute-done.12.refs_1_ = f32[128,128]{1,0:T(8,128)S(1)} collective-permute-done((f32[128,128]{1,0:T(8,128)S(1)}, f32[128,128]{1,0:T(8,128)S(1)}, u32[]{:S(2)}, u32[]{:S(2)}) %collective-permute-start.12) | collective-permute-done | bytes 65568 | tf_op jit(solution)/shard_map/ppermute | solution.py:415
  45.7 8.1 %shard_map.41 = (f32[256,128]{1,0:T(8,128)S(1)}, f32[256,128]{1,0:T(8,128)S(1)}, f32[256,128]{1,0:T(8,128)S(1)}, f32[256,128]{1,0:T(8,128)S(1)}, f32[256,128]{1,...) custom-call(s32[3]{0:T(128)S(1)} %pad_add_fusion.place, ...), custom_call_target="tpu_custom_call" | custom-call | tf_op jit(solution)/shard_map/pallas_call | solution.py:76
  53.8 2.1 %collective-permute-start.14 = (f32[256,128]{1,0:T(8,128)S(1)}, f32[256,128]{1,0:T(8,128)S(1)}, u32[]{:S(2)}, u32[]{:S(2)}) collective-permute-start(f32[256,128]{1,0:T(8,128)S(1)} %get-tuple-element.30), channel_id=1, source_target_pairs={{4,0},{6,1},{5,2},{7,3},{0,4},{2,5},{1,6},{3,7},{12,8},{14,9},{13,... | collective-permute-start | bytes 393224 | tf_op jit(solution)/shard_map/ppermute | solution.py:421
  56.6 5.3 %collective-permute-start.17 = (f32[256,128]{1,0:T(8,128)S(1)}, f32[256,128]{1,0:T(8,128)S(1)}, u32[]{:S(2)}, u32[]{:S(2)}) collective-permute-start(f32[256,128]{1,0:T(8,128)S(1)} %get-tuple-element.33), channel_id=1, source_target_pairs={{9,0},{11,1},{8,2},{10,3},{13,4},{15,5},{12,6},{14,7},{1,8},{3,9},... | collective-permute-start | bytes 393224 | tf_op jit(solution)/shard_map/ppermute | solution.py:421
  63.9 1.3 %collective-permute-done.15 = f32[256,128]{1,0:T(8,128)S(1)} collective-permute-done((f32[256,128]{1,0:T(8,128)S(1)}, f32[256,128]{1,0:T(8,128)S(1)}, u32[]{:S(2)}, u32[]{:S(2)}) %collective-permute-start.15) | collective-permute-done | bytes 131104 | tf_op jit(solution)/shard_map/ppermute | solution.py:421
  65.3 2.2 %collective-permute-start.20 = (f32[256,128]{1,0:T(8,128)S(1)}, f32[256,128]{1,0:T(8,128)S(1)}, u32[]{:S(2)}, u32[]{:S(2)}) collective-permute-start(f32[256,128]{1,0:T(8,128)S(1)} %get-tuple-element.36), channel_id=1, source_target_pairs={{1,0},{3,1},{0,2},{2,3},{5,4},{7,5},{4,6},{6,7},{9,8},{11,9},{8,10... | collective-permute-start | bytes 393224 | tf_op jit(solution)/shard_map/ppermute | solution.py:421
  67.5 6.7 %collective-permute-done.17 = f32[256,128]{1,0:T(8,128)S(1)} collective-permute-done((f32[256,128]{1,0:T(8,128)S(1)}, f32[256,128]{1,0:T(8,128)S(1)}, u32[]{:S(2)}, u32[]{:S(2)}) %collective-permute-start.17) | collective-permute-done | bytes 131104 | tf_op jit(solution)/shard_map/ppermute | solution.py:421
  74.1 3.5 %collective-permute-done.18 = f32[256,128]{1,0:T(8,128)S(1)} collective-permute-done((f32[256,128]{1,0:T(8,128)S(1)}, f32[256,128]{1,0:T(8,128)S(1)}, u32[]{:S(2)}, u32[]{:S(2)}) %collective-permute-start.18) | collective-permute-done | bytes 131104 | tf_op jit(solution)/shard_map/ppermute | solution.py:421
  78.0 1.6 %shard_map.42 = f32[2,16,64,128]{3,2,1,0:T(8,128)} custom-call(s32[3]{0:T(128)S(1)} %pad_add_fusion.place, f32[16,16,128]{2,1,0:T(8,128)S(1)} %bitcast.24, f32[16,16,128]{2,1,0:T(8,128)S(1)} %bitcast.25, f32[16,16,128]{2,1,0:T(8,128)S(1)} %bitcast.26, f32[16,16,128]{2,1,0:T(8,128)S(1)} %bitcast.27, f32[16,16,128]{2,1,0:T(8,128)S(1)} %bitcast.28, ...), custom_call_target="tpu_custom_call" | custom-call | tf_op jit(solution)/shard_map/pallas_call | solution.py:76
  (30 shorter events, 8.1 us)
Async XLA Ops:
  0.0 30.7 %copy-start.1 = (f32[16,64,128]{2,1,0:T(8,128)S(1)}, f32[16,64,128]{2,1,0:T(8,128)}, u32[]{:S(2)}) copy-start(f32[16,64,128]{2,1,0:T(8,128)} %param.4) | copy-start | bytes 1572868
  0.0 30.7 %copy-start = (f32[3,16,64,128]{3,2,1,0:T(8,128)S(1)}, f32[3,16,64,128]{3,2,1,0:T(8,128)}, u32[]{:S(2)}) copy-start(f32[3,16,64,128]{3,2,1,0:T(8,128)} %param.5) | copy-start | bytes 4718596
  2.2 9.2 %collective-permute-start = (f32[256,128]{1,0:T(8,128)S(1)}, f32[256,128]{1,0:T(8,128)S(1)}, u32[]{:S(2)}, u32[]{:S(2)}) collective-permute-start(f32[256,128]{1,0:T(8,128)S(1)} %bitcast.37), channel_id=1, source_target_pairs={{0,8},{1,10},{2,9},{3,11},{4,12},{5,14},{6,13},{7,15},{8,0},{9,2},... | collective-permute-start | bytes 393224 | tf_op jit(solution)/shard_map/ppermute | solution.py:383
  4.8 7.4 %collective-permute-start.1 = (f32[256,128]{1,0:T(8,128)S(1)}, f32[256,128]{1,0:T(8,128)S(1)}, u32[]{:S(2)}, u32[]{:S(2)}) collective-permute-start(f32[256,128]{1,0:T(8,128)S(1)} %bitcast.36), channel_id=1, source_target_pairs={{0,4},{1,6},{2,5},{3,7},{4,0},{5,2},{6,1},{7,3},{8,12},{9,14},{10,... | collective-permute-start | bytes 393224 | tf_op jit(solution)/shard_map/ppermute | solution.py:383
  5.3 10.4 %collective-permute-start.2 = (f32[256,128]{1,0:T(8,128)S(1)}, f32[256,128]{1,0:T(8,128)S(1)}, u32[]{:S(2)}, u32[]{:S(2)}) collective-permute-start(f32[256,128]{1,0:T(8,128)S(1)} %bitcast.35), channel_id=1, source_target_pairs={{0,5},{1,7},{2,4},{3,6},{4,1},{5,3},{6,0},{7,2},{8,13},{9,15},{10,... | collective-permute-start | bytes 393224 | tf_op jit(solution)/shard_map/ppermute | solution.py:383
  6.9 8.8 %collective-permute-start.3 = (f32[256,128]{1,0:T(8,128)}, f32[256,128]{1,0:T(8,128)S(1)}, u32[]{:S(2)}, u32[]{:S(2)}) collective-permute-start(f32[256,128]{1,0:T(8,128)} %bitcast.6), channel_id=1, source_target_pairs={{0,0},{1,2},{2,1},{3,3},{4,4},{5,6},{6,5},{7,7},{8,8},{9,10},{10,9... | collective-permute-start | bytes 393224 | tf_op jit(solution)/shard_map/ppermute | solution.py:383
  8.5 10.2 %collective-permute-start.4 = (f32[256,128]{1,0:T(8,128)}, f32[256,128]{1,0:T(8,128)S(1)}, u32[]{:S(2)}, u32[]{:S(2)}) collective-permute-start(f32[256,128]{1,0:T(8,128)} %bitcast.7), channel_id=1, source_target_pairs={{0,9},{1,11},{2,8},{3,10},{4,13},{5,15},{6,12},{7,14},{8,1},{9,3},... | collective-permute-start | bytes 393224 | tf_op jit(solution)/shard_map/ppermute | solution.py:383
  11.4 16.5 %collective-permute-start.5 = (f32[256,128]{1,0:T(8,128)S(1)}, f32[256,128]{1,0:T(8,128)S(1)}, u32[]{:S(2)}, u32[]{:S(2)}) collective-permute-start(f32[256,128]{1,0:T(8,128)S(1)} %bitcast.34), channel_id=1, source_target_pairs={{0,12},{1,14},{2,13},{3,15},{4,8},{5,10},{6,9},{7,11},{8,4},{9,6},... | collective-permute-start | bytes 393224 | tf_op jit(solution)/shard_map/ppermute | solution.py:383
  12.2 17.8 %collective-permute-start.6 = (f32[256,128]{1,0:T(8,128)S(1)}, f32[256,128]{1,0:T(8,128)S(1)}, u32[]{:S(2)}, u32[]{:S(2)}) collective-permute-start(f32[256,128]{1,0:T(8,128)S(1)} %bitcast.33), channel_id=1, source_target_pairs={{0,13},{1,15},{2,12},{3,14},{4,9},{5,11},{6,8},{7,10},{8,5},{9,7},... | collective-permute-start | bytes 393224 | tf_op jit(solution)/shard_map/ppermute | solution.py:383
  15.6 14.3 %collective-permute-start.7 = (f32[256,128]{1,0:T(8,128)S(1)}, f32[256,128]{1,0:T(8,128)S(1)}, u32[]{:S(2)}, u32[]{:S(2)}) collective-permute-start(f32[256,128]{1,0:T(8,128)S(1)} %bitcast.32), channel_id=1, source_target_pairs={{0,1},{1,3},{2,0},{3,2},{4,5},{5,7},{6,4},{7,6},{8,9},{9,11},{10,8... | collective-permute-start | bytes 393224 | tf_op jit(solution)/shard_map/ppermute | solution.py:383
  31.4 10.4 %collective-permute-start.8 = (f32[1536,128]{1,0:T(8,128)S(1)}, f32[1536,128]{1,0:T(8,128)S(1)}, u32[]{:S(2)}, u32[]{:S(2)}) collective-permute-start(f32[1536,128]{1,0:T(8,128)S(1)} %shard_map.38.own_ref), channel_id=1, source_target_pairs={{0,1},{1,0},{2,3},{3,2},{4,5},{5,4},{6,7},{7,6},{8,9},{9,8},{10,11... | collective-permute-start | bytes 2359304 | tf_op jit(solution)/shard_map/ppermute | solution.py:402
  31.5 7.3 %collective-permute-start.9 = (f32[384,128]{1,0:T(8,128)S(1)}, f32[384,128]{1,0:T(8,128)S(1)}, u32[]{:S(2)}, u32[]{:S(2)}) collective-permute-start(f32[384,128]{1,0:T(8,128)S(1)} %get-tuple-element.24), channel_id=1, source_target_pairs={{0,4},{4,0},{1,5},{5,1},{2,6},{6,2},{3,7},{7,3},{8,12},{12,8},{9,1... | collective-permute-start | bytes 589832 | tf_op jit(solution)/shard_map/ppermute | solution.py:394
  31.6 9.1 %collective-permute-start.10 = (f32[384,128]{1,0:T(8,128)S(1)}, f32[384,128]{1,0:T(8,128)S(1)}, u32[]{:S(2)}, u32[]{:S(2)}) collective-permute-start(f32[384,128]{1,0:T(8,128)S(1)} %get-tuple-element.25), channel_id=1, source_target_pairs={{4,8},{8,4},{5,9},{9,5},{6,10},{10,6},{7,11},{11,7},{20,24},{24,20... | collective-permute-start | bytes 589832 | tf_op jit(solution)/shard_map/ppermute | solution.py:395
  34.2 9.1 %collective-permute-start.11 = (f32[384,128]{1,0:T(8,128)S(1)}, f32[384,128]{1,0:T(8,128)S(1)}, u32[]{:S(2)}, u32[]{:S(2)}) collective-permute-start(f32[384,128]{1,0:T(8,128)S(1)} %get-tuple-element.27), channel_id=1, source_target_pairs={{0,2},{2,0},{1,3},{3,1},{4,6},{6,4},{5,7},{7,5},{8,10},{10,8},{9,1... | collective-permute-start | bytes 589832 | tf_op jit(solution)/shard_map/ppermute | solution.py:393
  41.3 4.3 %collective-permute-start.12 = (f32[128,128]{1,0:T(8,128)S(1)}, f32[128,128]{1,0:T(8,128)S(1)}, u32[]{:S(2)}, u32[]{:S(2)}) collective-permute-start(f32[128,128]{1,0:T(8,128)S(1)} %get-tuple-element.28), channel_id=1, source_target_pairs={{0,2},{2,0},{1,3},{3,1},{4,6},{6,4},{5,7},{7,5},{8,10},{10,8},{9,1... | collective-permute-start | bytes 196616 | tf_op jit(solution)/shard_map/ppermute | solution.py:415
  53.7 8.2 %collective-permute-start.13 = (f32[256,128]{1,0:T(8,128)S(1)}, f32[256,128]{1,0:T(8,128)S(1)}, u32[]{:S(2)}, u32[]{:S(2)}) collective-permute-start(f32[256,128]{1,0:T(8,128)S(1)} %get-tuple-element.29), channel_id=1, source_target_pairs={{8,0},{10,1},{9,2},{11,3},{12,4},{14,5},{13,6},{15,7},{0,8},{2,9},... | collective-permute-start | bytes 393224 | tf_op jit(solution)/shard_map/ppermute | solution.py:421
  53.8 9.3 %collective-permute-start.14 = (f32[256,128]{1,0:T(8,128)S(1)}, f32[256,128]{1,0:T(8,128)S(1)}, u32[]{:S(2)}, u32[]{:S(2)}) collective-permute-start(f32[256,128]{1,0:T(8,128)S(1)} %get-tuple-element.30), channel_id=1, source_target_pairs={{4,0},{6,1},{5,2},{7,3},{0,4},{2,5},{1,6},{3,7},{12,8},{14,9},{13,... | collective-permute-start | bytes 393224 | tf_op jit(solution)/shard_map/ppermute | solution.py:421
  55.9 9.4 %collective-permute-start.15 = (f32[256,128]{1,0:T(8,128)S(1)}, f32[256,128]{1,0:T(8,128)S(1)}, u32[]{:S(2)}, u32[]{:S(2)}) collective-permute-start(f32[256,128]{1,0:T(8,128)S(1)} %get-tuple-element.31), channel_id=1, source_target_pairs={{5,0},{7,1},{4,2},{6,3},{1,4},{3,5},{0,6},{2,7},{13,8},{15,9},{12,... | collective-permute-start | bytes 393224 | tf_op jit(solution)/shard_map/ppermute | solution.py:421
  55.9 11.5 %collective-permute-start.16 = (f32[256,128]{1,0:T(8,128)S(1)}, f32[256,128]{1,0:T(8,128)S(1)}, u32[]{:S(2)}, u32[]{:S(2)}) collective-permute-start(f32[256,128]{1,0:T(8,128)S(1)} %get-tuple-element.32), channel_id=1, source_target_pairs={{0,0},{2,1},{1,2},{3,3},{4,4},{6,5},{5,6},{7,7},{8,8},{10,9},{9,10... | collective-permute-start | bytes 393224 | tf_op jit(solution)/shard_map/ppermute | solution.py:421
  56.6 17.5 %collective-permute-start.17 = (f32[256,128]{1,0:T(8,128)S(1)}, f32[256,128]{1,0:T(8,128)S(1)}, u32[]{:S(2)}, u32[]{:S(2)}) collective-permute-start(f32[256,128]{1,0:T(8,128)S(1)} %get-tuple-element.33), channel_id=1, source_target_pairs={{9,0},{11,1},{8,2},{10,3},{13,4},{15,5},{12,6},{14,7},{1,8},{3,9},... | collective-permute-start | bytes 393224 | tf_op jit(solution)/shard_map/ppermute | solution.py:421
  61.9 15.7 %collective-permute-start.18 = (f32[256,128]{1,0:T(8,128)S(1)}, f32[256,128]{1,0:T(8,128)S(1)}, u32[]{:S(2)}, u32[]{:S(2)}) collective-permute-start(f32[256,128]{1,0:T(8,128)S(1)} %get-tuple-element.34), channel_id=1, source_target_pairs={{12,0},{14,1},{13,2},{15,3},{8,4},{10,5},{9,6},{11,7},{4,8},{6,9},... | collective-permute-start | bytes 393224 | tf_op jit(solution)/shard_map/ppermute | solution.py:421
  63.1 14.9 %collective-permute-start.19 = (f32[256,128]{1,0:T(8,128)S(1)}, f32[256,128]{1,0:T(8,128)S(1)}, u32[]{:S(2)}, u32[]{:S(2)}) collective-permute-start(f32[256,128]{1,0:T(8,128)S(1)} %get-tuple-element.35), channel_id=1, source_target_pairs={{13,0},{15,1},{12,2},{14,3},{9,4},{11,5},{8,6},{10,7},{5,8},{7,9},... | collective-permute-start | bytes 393224 | tf_op jit(solution)/shard_map/ppermute | solution.py:421
  65.3 12.8 %collective-permute-start.20 = (f32[256,128]{1,0:T(8,128)S(1)}, f32[256,128]{1,0:T(8,128)S(1)}, u32[]{:S(2)}, u32[]{:S(2)}) collective-permute-start(f32[256,128]{1,0:T(8,128)S(1)} %get-tuple-element.36), channel_id=1, source_target_pairs={{1,0},{3,1},{0,2},{2,3},{5,4},{7,5},{4,6},{6,7},{9,8},{11,9},{8,10... | collective-permute-start | bytes 393224 | tf_op jit(solution)/shard_map/ppermute | solution.py:421

commit v3 on v0

v3 whole, which is shorter than its diff:
```python
import functools

import jax
import jax.numpy as jnp
from jax import lax
from jax.experimental import pallas as pl
from jax.experimental.pallas import tpu as pltpu
from jax.sharding import PartitionSpec as P

SWEEPS = 4
GHOST = SWEEPS - 1
QUARTERS = 4
TILE = 8
COEFS = 9
RAW = 4

alpha_circ = 0.1
inv_step = 2.0

FLAT = ("tm", "space")


class Plan:
    def __init__(self, steps, cores, half_z, nx, ny):
        self.steps, self.cores, self.half_z, self.nx, self.ny = steps, cores, half_z, nx, ny
        self.per_quarter = steps // QUARTERS
        self.in_half = self.per_quarter // 2
        self.z_parts = self.in_half * cores
        self.nz = half_z // self.in_half
        self.rows = nx // QUARTERS
        self.main = self.rows // TILE
        self.tiles = self.main + 1
        self.ext = self.nz + 2 * GHOST
        self.sides = 1 if self.z_parts == 2 else 2
        self.z_tiles = GHOST * self.main + GHOST - 1
        self.raw_tiles = GHOST * self.tiles * RAW
        kinds = [(2, 0), (1, 0), (1, 1), (0, 1), (2, 1), (3, 0), (3, 1), (0, 0)]
        self.rounds = [a * self.per_quarter + m * 2 + c for m in range(self.in_half) for a, c in kinds]

    def direct(self, r):
        return r // self.per_quarter < 2

    def pairs(self, r):
        return [(i, i ^ r) for i in range(self.steps)]

    def x_pairs(self, first):
        result = []
        for hi in range(first, QUARTERS - 1, 2):
            for lo in range(self.per_quarter):
                one = hi * self.per_quarter + lo
                result += [(one, one + self.per_quarter), (one + self.per_quarter, one)]
        return result

    def z_pairs(self, first):
        def flat(hi, zb, part):
            return (hi * self.per_quarter + zb % self.in_half * 2 + part) * self.cores + zb // self.in_half

        result = []
        for zb in range(first, self.z_parts - 1, 2):
            for hi in range(QUARTERS):
                for part in range(2):
                    one, two = flat(hi, zb, part), flat(hi, zb + 1, part)
                    result += [(one, two), (two, one)]
        return result


class Place:
    def __init__(self, plan, ref):
        self.t, self.s = ref[0], ref[1]
        self.hi, self.lo = self.t // plan.per_quarter, self.t % plan.per_quarter
        self.zm, self.part = self.lo // 2, self.lo % 2
        self.zb = self.s * plan.in_half + self.zm
        self.hi_odd, self.zb_odd = self.hi % 2 == 1, self.zb % 2 == 1


def kernel_call(body, outs, args, scratch=(), out_space=pltpu.VMEM, limit=16, aliases=None):
    in_specs = [pl.BlockSpec(memory_space=pltpu.SMEM)]
    in_specs += [pl.BlockSpec(memory_space=pltpu.VMEM)] * (len(args) - 1)
    single = isinstance(outs, tuple)
    shapes = [outs] if single else list(outs)
    result = pl.pallas_call(
        body,
        out_shape=[jax.ShapeDtypeStruct(s, jnp.float32) for s in shapes],
        in_specs=in_specs,
        out_specs=[pl.BlockSpec(memory_space=out_space)] * len(shapes),
        scratch_shapes=list(scratch),
        input_output_aliases=aliases or {},
        compiler_params=pltpu.CompilerParams(vmem_limit_bytes=limit << 20),
    )(*args)
    return result[0] if single else result


def rows_at(index, count=1):
    return pl.ds(pl.multiple_of(index * TILE, TILE), count * TILE)


def sublane(plan):
    return lax.broadcasted_iota(jnp.int32, (TILE, plan.ny), 0)


def lane(plan):
    return lax.broadcasted_iota(jnp.int32, (TILE, plan.ny), 1)


def near_tiles(plan, hi):
    per = plan.nx // TILE
    own = [hi * plan.main + k for k in range(plan.main)]
    return own, jnp.minimum(own[-1] + 1, per - 1), jnp.maximum(own[0] - 1, 0)


def write_coefs(plan, hi, inside, k, values, store):
    row, col = sublane(plan), lane(plan)
    d, vz, vx, vy = values
    if k < plan.main:
        x = row + k * TILE
    else:
        x = jnp.where(row < GHOST, row + plan.rows, row - TILE)
    x = x + hi * plan.rows
    keep = (x >= 0) & (x < plan.nx)
    if k == plan.main:
        keep = keep & ((row < GHOST) | (row >= TILE - GHOST))
    if inside is not None:
        keep = keep & inside
    total = inv_step + 6.0 * d + (jnp.abs(vz) + jnp.abs(vx) + jnp.abs(vy))
    w = jnp.where(keep, 1.0 / total, 0.0)
    c = inv_step * w
    power = c
    for _ in range(plan.steps.bit_length() - 1):
        power = power * power
    wrap = alpha_circ / (1.0 - alpha_circ * power)
    low = [w * (d + jnp.maximum(v, 0.0)) for v in (vz, vx, vy)]
    high = [w * (d + jnp.maximum(-v, 0.0)) for v in (vz, vx, vy)]
    low[2] = jnp.where(col == 0, 0.0, low[2])
    high[2] = jnp.where(col == plan.ny - 1, 0.0, high[2])
    for n, value in enumerate([w, c, wrap] + low + high):
        store(n, value)


def make_coefs(plan, place_ref, d_ref, v_ref, out_ref, *raw_refs):
    place = Place(plan, place_ref)
    per = plan.nx // TILE
    row = sublane(plan)
    own, over, under = near_tiles(plan, place.hi)

    def read(z):
        z = place.zm * plan.nz + z
        found = []
        for n in range(RAW):
            ref, base = (d_ref, z * per) if n == 0 else (v_ref, ((n - 1) * plan.half_z + z) * per)
            edge = jnp.where(row < TILE // 2, ref[rows_at(base + over), :], ref[rows_at(base + under), :])
            found.append([ref[rows_at(base + at), :] for at in own] + [edge])
        return [[tiles[k] for tiles in found] for k in range(plan.tiles)]

    def layer(z, _):
        for k, values in enumerate(read(z)):

            def store(n, value, k=k):
                out_ref[rows_at(((z + GHOST) * plan.tiles + k) * COEFS + n), :] = value

            write_coefs(plan, place.hi, None, k, values, store)
        return 0

    lax.fori_loop(0, plan.nz, layer, 0)
    for side, raw in enumerate(raw_refs):
        up = jnp.logical_not(place.zb_odd) if side == 0 else place.zb_odd
        for n in range(GHOST):
            for k, values in enumerate(read(jnp.where(up, plan.nz - GHOST + n, n))):
                for at, value in enumerate(values):
                    raw[rows_at((n * plan.tiles + k) * RAW + at), :] = value


def pack_blocks(plan, place_ref, right, *outs):
    place = Place(plan, place_ref)
    per = plan.nx // TILE
    row = sublane(plan)
    for out, r in zip(outs, plan.rounds):
        target = place.t ^ r
        quarter, lo = target // plan.per_quarter, target % plan.per_quarter
        first = lo % 2 * plan.half_z + lo // 2 * plan.nz
        own, over, under = near_tiles(plan, quarter)
        for z in range(plan.nz):
            base = (first + z) * per
            for k, at in enumerate(own):
                out[rows_at(z * plan.main + k), :] = right[rows_at(base + at), :]
            if plan.direct(r):
                edge = jnp.where(row < TILE // 2, right[rows_at(base + over), :], right[rows_at(base + under), :])
                out[rows_at(plan.nz * plan.main + z), :] = edge


def edge_rows(plan, place_ref, *refs):
    place = Place(plan, place_ref)
    blocks, (x_even, x_odd) = refs[: plan.steps], refs[plan.steps :]
    half = plan.steps // 2
    for block, r in zip(blocks, plan.rounds):
        step = (place.t ^ r) % half
        for n in range(GHOST):
            low = block[pl.ds(n, plan.nz, stride=plan.rows), :]
            high = block[pl.ds(plan.rows - GHOST + n, plan.nz, stride=plan.rows), :]
            at = pl.ds((n * half + step) * plan.nz, plan.nz)
            if plan.direct(r):
                x_odd[at, :] = jnp.where(place.hi_odd, high, low)
            else:
                x_even[at, :] = jnp.where(place.hi_odd, low, high)


def gather_steps(plan, place_ref, *refs):
    place = Place(plan, place_ref)
    blocks, field = refs[: plan.steps], refs[plan.steps]
    size = plan.nz * plan.rows
    for block, r in zip(blocks, plan.rounds):
        at = pl.multiple_of((place.t ^ r) * size, TILE)
        field[pl.ds(at, size), :] = block[pl.ds(0, size), :]


def gather_ghosts(plan, place_ref, field, even_ref, odd_ref, *refs):
    place = Place(plan, place_ref)
    direct = [r for r in plan.rounds if plan.direct(r)]
    blocks, refs = refs[: len(direct)], refs[len(direct) :]
    raws, refs = refs[: plan.sides], refs[plan.sides :]
    ghost, z_sends, planes = refs[0], refs[1:-1], refs[-1]
    half = plan.steps // 2
    count = half * plan.nz
    size = plan.nz * plan.rows
    for block, r in zip(blocks, direct):
        at = pl.multiple_of((place.t ^ r) * plan.nz * TILE, TILE)
        ghost[pl.ds(at, plan.nz * TILE), :] = block[pl.ds(size, plan.nz * TILE), :]
    for n in range(GHOST):
        even, odd = even_ref[pl.ds(n * count, count), :], odd_ref[pl.ds(n * count, count), :]
        planes[pl.ds(n * count, count), :] = jnp.where(place.hi_odd, odd, even)
        planes[pl.ds((TILE - GHOST + n) * count, count), :] = jnp.where(place.hi_odd, even, odd)
    for n in range(GHOST, TILE - GHOST):
        planes[pl.ds(n * count, count), :] = jnp.zeros((count, plan.ny), jnp.float32)
    first = (1 - place.hi // 2) * count
    for n in range(count):
        ghost[rows_at(first + n), :] = planes[pl.ds(n, TILE, stride=count), :]
    deep, tiles = GHOST - 1, plan.z_tiles
    for side, (raw, z_send) in enumerate(zip(raws, z_sends)):
        up = jnp.logical_not(place.zb_odd) if side == 0 else place.zb_odd
        for t in range(plan.steps):
            for n in range(GHOST):
                z = t * plan.nz + jnp.where(up, plan.nz - GHOST + n, n)
                for k in range(plan.main):
                    z_send[rows_at(t * tiles + n * plan.main + k), :] = field[rows_at(z * plan.main + k), :]
            for n in range(deep):
                z = t * plan.nz + jnp.where(up, plan.nz - deep + n, n)
                z_send[rows_at(t * tiles + GHOST * plan.main + n), :] = ghost[rows_at(z), :]
        z_send[rows_at(plan.steps * tiles, plan.raw_tiles), :] = raw[...]


class Sweeps:
    def __init__(self, plan, place, coefs, source, ping, pong, last):
        self.plan, self.coefs = plan, coefs
        self.source, self.buffers, self.last = source, (ping, pong), last
        self.has_low, self.has_high = place.zb > 0, place.zb < plan.z_parts - 1
        self.low_at, self.high_at = GHOST, GHOST + plan.nz

    def spot(self, e, k, t):
        return rows_at((e * self.plan.tiles + k) * self.plan.steps + t)

    def coef(self, e, k, n):
        return self.coefs[rows_at((e * self.plan.tiles + k) * COEFS + n), :]

    def first(self, e, k, values):
        w, c, wrap = (self.coef(e, k, n) for n in range(3))
        partial = []
        for t, value in enumerate(values):
            value = w * value
            self.source[self.spot(e, k, t), :] = value
            if t:
                value = value + c * partial[-1]
            partial.append(value)
        carry = c * (wrap * partial[-1])
        for t, value in enumerate(partial):
            self.buffers[0][self.spot(e, k, t), :] = value + carry
            carry = c * carry

    def sweep(self, number, start, stop):
        plan, steps, tiles, ny = self.plan, self.plan.steps, self.plan.tiles, self.plan.ny
        old, new = self.buffers[(number - 1) % 2], self.buffers[number % 2]
        final = number == SWEEPS - 1
        wide = plan.main if final else tiles
        row = sublane(plan)
        spot, coef = self.spot, self.coef

        def layer(e, _):
            c = [coef(e, k, 1) for k in range(wide)]
            near = [[coef(e, k, n) for n in range(3, COEFS)] for k in range(wide)]
            partial = [[] for _ in range(wide)]
            for t in range(steps):
                here = [old[spot(e, k, t), :] for k in range(tiles)]
                down = [pltpu.roll(value, 1, 0) for value in here]
                up = [pltpu.roll(value, TILE - 1, 0) for value in here]
                for k in range(wide):
                    z_low, x_low, y_low, z_high, x_high, y_high = near[k]
                    below = jnp.where(row == 0, down[k - 1], down[k])
                    above = jnp.where(row == TILE - 1, up[(k + 1) % tiles], up[k])
                    total = self.source[spot(e, k, t), :] + z_low * old[spot(e - 1, k, t), :]
                    total = total + z_high * old[spot(e + 1, k, t), :]
                    total = total + (x_low * below + x_high * above)
                    total = total + (
                        y_low * pltpu.roll(here[k], 1, 1) + y_high * pltpu.roll(here[k], ny - 1, 1)
                    )
                    if t:
                        total = total + c[k] * partial[k][-1]
                    partial[k].append(total)
            for k in range(wide):
                carry = c[k] * (coef(e, k, 2) * partial[k][-1])
                for t in range(steps):
                    value = partial[k][t] + carry
                    carry = c[k] * carry
                    if final:
                        self.last[rows_at((t * plan.nz + e - GHOST) * plan.main + k), :] = value
                    else:
                        new[spot(e, k, t), :] = value
            return 0

        lax.fori_loop(start, stop, layer, 0)


def all_sweeps(plan, place_ref, coefs_in, field, ghost, *refs):
    place = Place(plan, place_ref)
    sides, steps, main = plan.sides, plan.steps, plan.main
    z_in, refs = refs[:sides], refs[sides:]
    outs, (coefs, source, ping, pong, last) = refs[:steps], refs[steps:]
    work = Sweeps(plan, place, coefs, source, ping, pong, last)
    deep = GHOST - 1
    empty = jnp.zeros((TILE, plan.ny), jnp.float32)

    def own_layer(z, _):
        for k in range(main):
            work.first(z + GHOST, k, [field[rows_at((t * plan.nz + z) * main + k), :] for t in range(steps)])
        work.first(z + GHOST, main, [ghost[rows_at(t * plan.nz + z), :] for t in range(steps)])
        return 0

    lax.fori_loop(0, plan.nz, own_layer, 0)

    def ghost_layers(at, upper, z_ref):
        for n in range(GHOST):
            e = at + n
            for k in range(plan.tiles):
                raw = steps * plan.z_tiles + (n * plan.tiles + k) * RAW

                def store(number, value, k=k, e=e):
                    coefs[rows_at((e * plan.tiles + k) * COEFS + number), :] = value

                write_coefs(plan, place.hi, None, k, [z_ref[rows_at(raw + m), :] for m in range(RAW)], store)
            for k in range(main):
                tile = n * main + k
                work.first(e, k, [z_ref[rows_at(t * plan.z_tiles + tile), :] for t in range(steps)])
            c_at = n if upper else n - (GHOST - deep)
            if 0 <= c_at < deep:
                tile = GHOST * main + c_at
                work.first(e, main, [z_ref[rows_at(t * plan.z_tiles + tile), :] for t in range(steps)])
            else:
                for t in range(steps):
                    ping[work.spot(e, main, t), :] = empty
                    source[work.spot(e, main, t), :] = empty

    for odd in (False, True):

        @pl.when(work.has_low & (place.zb_odd == odd))
        def _(odd=odd):
            ghost_layers(0, False, z_in[0 if odd else sides - 1])

        @pl.when(work.has_high & (place.zb_odd == odd))
        def _(odd=odd):
            ghost_layers(work.high_at, True, z_in[sides - 1 if odd else 0])

    for outside, e in ((work.has_low, work.low_at - 1), (work.has_high, work.high_at)):

        @pl.when(jnp.logical_not(outside))
        def _(e=e):
            for k in range(plan.tiles):
                for t in range(steps):
                    for buffer in work.buffers:
                        buffer[work.spot(e, k, t), :] = empty

    for number in range(1, SWEEPS):
        reach = SWEEPS - 1 - number
        start = work.low_at - jnp.where(work.has_low, reach, 0)
        stop = work.high_at + jnp.where(work.has_high, reach, 0)
        work.sweep(number, start, stop)

    size = plan.nz * plan.rows
    for out, r in zip(outs, plan.rounds):
        out[...] = last[pl.ds(pl.multiple_of((place.t ^ r) * size, TILE), size), :]


def run_sweeps(plan, place, coefs, field, ghost, z_in):
    size = plan.nz * plan.rows
    grid = pltpu.VMEM((plan.ext * plan.tiles * plan.steps * TILE, plan.ny), jnp.float32)
    outs = kernel_call(
        functools.partial(all_sweeps, plan),
        [(size, plan.ny)] * plan.steps + [coefs.shape],
        (place, coefs, field, ghost, *z_in),
        scratch=[grid] * 3 + [pltpu.VMEM((plan.steps * size, plan.ny), jnp.float32)],
        aliases={1: plan.steps},
        limit=24,
    )
    return outs[: plan.steps]


def place_blocks(plan, place_ref, *refs):
    place = Place(plan, place_ref)
    blocks, out, sems = refs[: plan.steps], refs[plan.steps], refs[plan.steps + 1]
    copies = []
    for n, (block, r) in enumerate(zip(blocks, plan.rounds)):
        source = place.t ^ r
        quarter, lo = source // plan.per_quarter, source % plan.per_quarter
        z = pl.multiple_of(lo // 2 * plan.nz, plan.nz)
        x = pl.multiple_of(quarter * plan.rows, plan.rows)
        target = out.at[lo % 2, pl.ds(z, plan.nz), pl.ds(x, plan.rows), :]
        copies.append(pltpu.make_async_copy(block, target, sems.at[n]))
    for copy in copies:
        copy.start()
    for copy in copies:
        copy.wait()


def local(right_side, diffusivity, velocity):
    steps, cores = lax.axis_size("tm"), lax.axis_size("space")
    _, parts, half_z, nx, ny = right_side.shape
    plan = Plan(steps, cores, half_z, nx, ny)
    place = jnp.stack([lax.axis_index("tm"), lax.axis_index("space")]).astype(jnp.int32)
    size = plan.nz * plan.rows
    half_x = steps // 2 * plan.nz

    def call(body, outs, arrays, **options):
        return kernel_call(functools.partial(body, plan), outs, (place, *arrays), **options)

    def turned(arrays):
        return [array if r == 0 else lax.ppermute(array, "tm", plan.pairs(r)) for array, r in zip(arrays, plan.rounds)]

    with_ghosts = (size + plan.nz * TILE, ny)
    blocks = turned(
        call(
            pack_blocks,
            [with_ghosts if plan.direct(r) else (size, ny) for r in plan.rounds],
            (right_side.reshape(parts * half_z * nx, ny),),
        )
    )
    blocks = lax.optimization_barrier(blocks)
    x_even, x_odd = call(edge_rows, [(GHOST * half_x, ny)] * 2, blocks)
    even = lax.ppermute(x_even, "tm", plan.x_pairs(0))
    odd = lax.ppermute(x_odd, "tm", plan.x_pairs(1))
    diffusivity, velocity, *blocks = lax.optimization_barrier((diffusivity, velocity, *blocks))
    field = call(gather_steps, (steps * size, ny), blocks)
    coefs, *raws = call(
        make_coefs,
        [(plan.ext * plan.tiles * COEFS * TILE, ny)] + [(plan.raw_tiles * TILE, ny)] * plan.sides,
        (diffusivity.reshape(half_z * nx, ny), velocity.reshape(3 * half_z * nx, ny)),
    )
    direct = [block for block, r in zip(blocks, plan.rounds) if plan.direct(r)]
    ghost, *z_sends = call(
        gather_ghosts,
        [(steps * plan.nz * TILE, ny)] + [((steps * plan.z_tiles + plan.raw_tiles) * TILE, ny)] * plan.sides,
        (field, even, odd, *direct, *raws),
        scratch=[pltpu.VMEM((half_x * TILE, ny), jnp.float32)],
    )
    z_in = [lax.ppermute(send, FLAT, plan.z_pairs(first)) for first, send in enumerate(z_sends)]
    solved = run_sweeps(plan, place, coefs, field, ghost, z_in)
    back = [block.reshape(plan.nz, plan.rows, ny) for block in turned(solved)]
    out = call(
        place_blocks,
        (parts, half_z, nx, ny),
        back,
        scratch=[pltpu.SemaphoreType.DMA((steps,))],
        out_space=pl.ANY,
    )
    return out[None]


def solution(mesh):
    placed = (
        P(("group", "tm"), None, "space", None, None),
        P("space", None, None),
        P(None, "space", None, None),
    )
    return jax.shard_map(
        local,
        mesh=mesh,
        in_specs=placed,
        out_specs=P(("group", "tm"), None, "space", None, None),
        check_vma=False,
    )
```

time: 229 us -> 74.7 us (0.33); the launches traced: 226 us -> 74.5 us
  waiting for transfers between devices: 185 us -> 37.7 us
  other arithmetic: 18.3 us -> 0.07 us
  Pallas kernels: 0 us -> 13.4 us
    ppermute x12 -> x17, waiting for transfers between devices: 185 us -> 37.7 us  [the longest x14 34.8 us: turned(): lax.ppermute(array, 'tm', plan.pairs(r))]
    pallas_call x0 -> x7, Pallas kernels: none -> 13.4 us  [kernel_call(): pl.pallas_call(body, out_shape=[jax.ShapeDtypeStruct(s, jnp.float32) for...]
    select_n x8 -> x0, other arithmetic: 5.11 us -> none  [the longest x2 3.4 us: butterfly_inverse(): grid_field = jnp.where(is_upper, kept_part - turned, kept_part + turned)]
    add x3 -> x0, other arithmetic: 3.58 us -> none  [jacobi_step(): combined = source + nearby]
    ppermute x12 -> x17, starting transfers between devices: 20.1 us -> 21.9 us  [the longest x14 17.2 us: turned(): lax.ppermute(array, 'tm', plan.pairs(r))]
  transfers between devices with their start and end apart: 12 -> 17, of which waited for: 9 -> 12; matrix products, arithmetic and copies ran while one was open for 1% -> 0% of each run, Pallas kernels for 0% -> 2%
where the time goes in v3:
time: 74.7 us; the launch traced here: 74.5 us
  waiting for transfers between devices  37.7 us (50%)
  starting transfers between devices  21.9 us (29%)
  Pallas kernels  13.4 us (18%)
  local copies, waits for them, and re-layouts  1.34 us (2%)
    ppermute x14, waiting for transfers between devices, turned(): lax.ppermute(array, 'tm', plan.pairs(r))  34.8 us
    ppermute x14, starting transfers between devices, turned(): lax.ppermute(array, 'tm', plan.pairs(r))  17.2 us
    pallas_call x7, Pallas kernels, kernel_call(): pl.pallas_call(body, out_shape=[jax.ShapeDtypeStruct(s, jnp.float32) for...  13.4 us
    ppermute x1, starting transfers between devices, local(): odd = lax.ppermute(x_odd, 'tm', plan.x_pairs(1))  4.54 us
    ppermute x1, waiting for transfers between devices, local(): lax.ppermute(send, FLAT, plan.z_pairs(first))  1.73 us
  transfers between devices with their start and end apart: 17, of which 12 were waited for; matrix products, arithmetic and copies ran while one was open for 0% of the time, Pallas kernels for 2%

profile of v3, /device:TPU:8, one launch (start us, length us, event | category | flops | bytes accessed | tf_op | source)
XLA Modules:
  0.0 74.5 jit_solution(17624234126654659122)
XLA Ops:
  0.1 1.3 %copy-done.1 = f32[1,2,16,64,128]{4,3,2,1,0:T(8,128)S(1)} copy-done((f32[1,2,16,64,128]{4,3,2,1,0:T(8,128)S(1)}, f32[1,2,16,64,128]{4,3,2,1,0:T(8,128)}, u32[]{:S(2)}) %copy-start.1) | copy-done | bytes 1048600
  2.1 2.7 %collective-permute-start = (f32[256,128]{1,0:T(8,128)S(1)}, f32[256,128]{1,0:T(8,128)S(1)}, u32[]{:S(2)}, u32[]{:S(2)}) collective-permute-start(f32[256,128]{1,0:T(8,128)S(1)} %get-tuple-element.45), channel_id=1, source_target_pairs={{0,8},{2,10},{4,12},{6,14},{8,0},{10,2},{12,4},{14,6},{1,9},{3,11}... | collective-permute-start | bytes 393224 | tf_op jit(solution)/shard_map/ppermute | solution.py:432
  4.8 1.3 %collective-permute-start.4 = (f32[256,128]{1,0:T(8,128)S(1)}, f32[256,128]{1,0:T(8,128)S(1)}, u32[]{:S(2)}, u32[]{:S(2)}) collective-permute-start(f32[256,128]{1,0:T(8,128)S(1)} %get-tuple-element.49), channel_id=1, source_target_pairs={{0,10},{2,8},{4,14},{6,12},{8,2},{10,0},{12,6},{14,4},{1,11},{3,9}... | collective-permute-start | bytes 393224 | tf_op jit(solution)/shard_map/ppermute | solution.py:432
  6.5 1.5 %collective-permute-start.2 = (f32[384,128]{1,0:T(8,128)S(1)}, f32[384,128]{1,0:T(8,128)S(1)}, u32[]{:S(2)}, u32[]{:S(2)}) collective-permute-start(f32[384,128]{1,0:T(8,128)S(1)} %get-tuple-element.47), channel_id=1, source_target_pairs={{0,6},{2,4},{4,2},{6,0},{8,14},{10,12},{12,10},{14,8},{1,7},{3,5},... | collective-permute-start | bytes 589832 | tf_op jit(solution)/shard_map/ppermute | solution.py:432
  8.1 1.5 %collective-permute-start.3 = (f32[384,128]{1,0:T(8,128)S(1)}, f32[384,128]{1,0:T(8,128)S(1)}, u32[]{:S(2)}, u32[]{:S(2)}) collective-permute-start(f32[384,128]{1,0:T(8,128)S(1)} %get-tuple-element.48), channel_id=1, source_target_pairs={{0,2},{2,0},{4,6},{6,4},{8,10},{10,8},{12,14},{14,12},{1,3},{3,1},... | collective-permute-start | bytes 589832 | tf_op jit(solution)/shard_map/ppermute | solution.py:432
  9.6 3.6 %collective-permute-done.refs_0_ = f32[256,128]{1,0:T(8,128)S(1)} collective-permute-done((f32[256,128]{1,0:T(8,128)S(1)}, f32[256,128]{1,0:T(8,128)S(1)}, u32[]{:S(2)}, u32[]{:S(2)}) %collective-permute-start) | collective-permute-done | bytes 131104 | tf_op jit(solution)/shard_map/ppermute | solution.py:432
  13.2 2.9 %collective-permute-done.4.refs_4_ = f32[256,128]{1,0:T(8,128)S(1)} collective-permute-done((f32[256,128]{1,0:T(8,128)S(1)}, f32[256,128]{1,0:T(8,128)S(1)}, u32[]{:S(2)}, u32[]{:S(2)}) %collective-permute-start.4) | collective-permute-done | bytes 131104 | tf_op jit(solution)/shard_map/ppermute | solution.py:432
  16.3 3.5 %collective-permute-done.5.refs_5_ = f32[256,128]{1,0:T(8,128)S(1)} collective-permute-done((f32[256,128]{1,0:T(8,128)S(1)}, f32[256,128]{1,0:T(8,128)S(1)}, u32[]{:S(2)}, u32[]{:S(2)}) %collective-permute-start.5) | collective-permute-done | bytes 131104 | tf_op jit(solution)/shard_map/ppermute | solution.py:432
  19.8 8.2 %collective-permute-done.6.refs_6_ = f32[256,128]{1,0:T(8,128)S(1)} collective-permute-done((f32[256,128]{1,0:T(8,128)S(1)}, f32[256,128]{1,0:T(8,128)S(1)}, u32[]{:S(2)}, u32[]{:S(2)}) %collective-permute-start.6) | collective-permute-done | bytes 131104 | tf_op jit(solution)/shard_map/ppermute | solution.py:432
  28.7 4.5 %collective-permute-start.8 = (f32[192,128]{1,0:T(8,128)S(1)}, f32[192,128]{1,0:T(8,128)S(1)}, u32[]{:S(2)}, u32[]{:S(2)}) collective-permute-start(f32[192,128]{1,0:T(8,128)S(1)} %get-tuple-element.73), channel_id=1, source_target_pairs={{4,8},{8,4},{6,10},{10,6},{5,9},{9,5},{7,11},{11,7},{20,24},{24,20... | collective-permute-start | bytes 294920 | tf_op jit(solution)/shard_map/ppermute | solution.py:445
  33.3 1.1 %shard_map.38 = (f32[4752,128]{1,0:T(8,128)S(1)}, f32[288,128]{1,0:T(8,128)S(1)}) custom-call(s32[2]{0:T(128)S(1)} %pad_add_fusion.place_ref, f32[1024,128]{1,0:T(8,128)S(1)} %bitcast.16, f32[3072,128]{1,0:T(8,128)S(1)} %bitcast.14), custom_call_target="tpu_custom_call" | custom-call | tf_op jit(solution)/shard_map/pallas_call | solution.py:81
  35.0 1.2 %collective-permute-done.8.odd_ref = f32[192,128]{1,0:T(8,128)S(1)} collective-permute-done((f32[192,128]{1,0:T(8,128)S(1)}, f32[192,128]{1,0:T(8,128)S(1)}, u32[]{:S(2)}, u32[]{:S(2)}) %collective-permute-start.8) | collective-permute-done | bytes 98336 | tf_op jit(solution)/shard_map/ppermute | solution.py:445
  37.1 1.7 %collective-permute-done.9.refs_0_ = f32[800,128]{1,0:T(8,128)S(1)} collective-permute-done((f32[800,128]{1,0:T(8,128)S(1)}, f32[800,128]{1,0:T(8,128)S(1)}, u32[]{:S(2)}, u32[]{:S(2)}) %collective-permute-start.9) | collective-permute-done | bytes 409632 | tf_op jit(solution)/shard_map/ppermute | solution.py:460
  38.8 8.0 %shard_map.42 = (f32[256,128]{1,0:T(8,128)S(1)}, f32[256,128]{1,0:T(8,128)S(1)}, f32[256,128]{1,0:T(8,128)S(1)}, f32[256,128]{1,0:T(8,128)S(1)}, f32[256,128]{1,...) custom-call(s32[2]{0:T(128)S(1)} %pad_add_fusion.place_ref, ...), custom_call_target="tpu_custom_call", output_to_operand_aliasing={{8}: (1, {})} | custom-call | tf_op jit(solution)/shard_map/pallas_call | solution.py:81
  46.8 3.2 %collective-permute-start.11 = (f32[256,128]{1,0:T(8,128)S(1)}, f32[256,128]{1,0:T(8,128)S(1)}, u32[]{:S(2)}, u32[]{:S(2)}) collective-permute-start(f32[256,128]{1,0:T(8,128)S(1)} %get-tuple-element.78), channel_id=1, source_target_pairs={{0,4},{2,6},{4,0},{6,2},{8,12},{10,14},{12,8},{14,10},{1,5},{3,7},... | collective-permute-start | bytes 393224 | tf_op jit(solution)/shard_map/ppermute | solution.py:432
  50.0 0.9 %collective-permute-start.12 = (f32[256,128]{1,0:T(8,128)S(1)}, f32[256,128]{1,0:T(8,128)S(1)}, u32[]{:S(2)}, u32[]{:S(2)}) collective-permute-start(f32[256,128]{1,0:T(8,128)S(1)} %get-tuple-element.79), channel_id=1, source_target_pairs={{0,6},{2,4},{4,2},{6,0},{8,14},{10,12},{12,10},{14,8},{1,7},{3,5},... | collective-permute-start | bytes 393224 | tf_op jit(solution)/shard_map/ppermute | solution.py:432
  51.5 2.4 %collective-permute-start.14 = (f32[256,128]{1,0:T(8,128)S(1)}, f32[256,128]{1,0:T(8,128)S(1)}, u32[]{:S(2)}, u32[]{:S(2)}) collective-permute-start(f32[256,128]{1,0:T(8,128)S(1)} %get-tuple-element.81), channel_id=1, source_target_pairs={{0,10},{2,8},{4,14},{6,12},{8,2},{10,0},{12,6},{14,4},{1,11},{3,9}... | collective-permute-start | bytes 393224 | tf_op jit(solution)/shard_map/ppermute | solution.py:432
  54.1 1.7 %collective-permute-start.15 = (f32[256,128]{1,0:T(8,128)S(1)}, f32[256,128]{1,0:T(8,128)S(1)}, u32[]{:S(2)}, u32[]{:S(2)}) collective-permute-start(f32[256,128]{1,0:T(8,128)S(1)} %get-tuple-element.82), channel_id=1, source_target_pairs={{0,12},{2,14},{4,8},{6,10},{8,4},{10,6},{12,0},{14,2},{1,13},{3,15... | collective-permute-start | bytes 393224 | tf_op jit(solution)/shard_map/ppermute | solution.py:432
  55.9 1.5 %collective-permute-done.11 = f32[256,128]{1,0:T(8,128)S(1)} collective-permute-done((f32[256,128]{1,0:T(8,128)S(1)}, f32[256,128]{1,0:T(8,128)S(1)}, u32[]{:S(2)}, u32[]{:S(2)}) %collective-permute-start.11) | collective-permute-done | bytes 131104 | tf_op jit(solution)/shard_map/ppermute | solution.py:432
  58.1 3.3 %collective-permute-done.12 = f32[256,128]{1,0:T(8,128)S(1)} collective-permute-done((f32[256,128]{1,0:T(8,128)S(1)}, f32[256,128]{1,0:T(8,128)S(1)}, u32[]{:S(2)}, u32[]{:S(2)}) %collective-permute-start.12) | collective-permute-done | bytes 131104 | tf_op jit(solution)/shard_map/ppermute | solution.py:432
  61.4 2.1 %collective-permute-done.14 = f32[256,128]{1,0:T(8,128)S(1)} collective-permute-done((f32[256,128]{1,0:T(8,128)S(1)}, f32[256,128]{1,0:T(8,128)S(1)}, u32[]{:S(2)}, u32[]{:S(2)}) %collective-permute-start.14) | collective-permute-done | bytes 131104 | tf_op jit(solution)/shard_map/ppermute | solution.py:432
  63.5 7.5 %collective-permute-done.15 = f32[256,128]{1,0:T(8,128)S(1)} collective-permute-done((f32[256,128]{1,0:T(8,128)S(1)}, f32[256,128]{1,0:T(8,128)S(1)}, u32[]{:S(2)}, u32[]{:S(2)}) %collective-permute-start.15) | collective-permute-done | bytes 131104 | tf_op jit(solution)/shard_map/ppermute | solution.py:432
  71.0 2.0 %collective-permute-done.16 = f32[256,128]{1,0:T(8,128)S(1)} collective-permute-done((f32[256,128]{1,0:T(8,128)S(1)}, f32[256,128]{1,0:T(8,128)S(1)}, u32[]{:S(2)}, u32[]{:S(2)}) %collective-permute-start.16) | collective-permute-done | bytes 131104 | tf_op jit(solution)/shard_map/ppermute | solution.py:432
  73.0 1.6 %shard_map.43 = f32[2,16,64,128]{3,2,1,0:T(8,128)} custom-call(s32[2]{0:T(128)S(1)} %pad_add_fusion.place_ref, f32[16,16,128]{2,1,0:T(8,128)S(1)} %bitcast.18, f32[16,16,128]{2,1,0:T(8,128)S(1)} %bitcast.19, f32[16,16,128]{2,1,0:T(8,128)S(1)} %bitcast.20, f32[16,16,128]{2,1,0:T(8,128)S(1)} %bitcast.21, f32[16,16,128]{2,1,0:T(8,128)S(1)} %bitcast.22, ...), custom_call_target="tpu_custom_call" | custom-call | tf_op jit(solution)/shard_map/pallas_call | solution.py:81
  (24 shorter events, 5.3 us)
Async XLA Ops:
  0.0 33.3 %copy-start = (f32[3,16,64,128]{3,2,1,0:T(8,128)S(1)}, f32[3,16,64,128]{3,2,1,0:T(8,128)}, u32[]{:S(2)}) copy-start(f32[3,16,64,128]{3,2,1,0:T(8,128)} %param.5) | copy-start | bytes 4718596
  0.1 1.3 %copy-start.1 = (f32[1,2,16,64,128]{4,3,2,1,0:T(8,128)S(1)}, f32[1,2,16,64,128]{4,3,2,1,0:T(8,128)}, u32[]{:S(2)}) copy-start(f32[1,2,16,64,128]{4,3,2,1,0:T(8,128)} %param.3) | copy-start | bytes 3145732
  1.4 31.9 %copy-start.2 = (f32[16,64,128]{2,1,0:T(8,128)S(1)}, f32[16,64,128]{2,1,0:T(8,128)}, u32[]{:S(2)}) copy-start(f32[16,64,128]{2,1,0:T(8,128)} %param.4) | copy-start | bytes 1572868
  2.1 11.1 %collective-permute-start = (f32[256,128]{1,0:T(8,128)S(1)}, f32[256,128]{1,0:T(8,128)S(1)}, u32[]{:S(2)}, u32[]{:S(2)}) collective-permute-start(f32[256,128]{1,0:T(8,128)S(1)} %get-tuple-element.45), channel_id=1, source_target_pairs={{0,8},{2,10},{4,12},{6,14},{8,0},{10,2},{12,4},{14,6},{1,9},{3,11}... | collective-permute-start | bytes 393224 | tf_op jit(solution)/shard_map/ppermute | solution.py:432
  4.8 11.3 %collective-permute-start.4 = (f32[256,128]{1,0:T(8,128)S(1)}, f32[256,128]{1,0:T(8,128)S(1)}, u32[]{:S(2)}, u32[]{:S(2)}) collective-permute-start(f32[256,128]{1,0:T(8,128)S(1)} %get-tuple-element.49), channel_id=1, source_target_pairs={{0,10},{2,8},{4,14},{6,12},{8,2},{10,0},{12,6},{14,4},{1,11},{3,9}... | collective-permute-start | bytes 393224 | tf_op jit(solution)/shard_map/ppermute | solution.py:432
  6.1 21.9 %collective-permute-start.1 = (f32[384,128]{1,0:T(8,128)S(1)}, f32[384,128]{1,0:T(8,128)S(1)}, u32[]{:S(2)}, u32[]{:S(2)}) collective-permute-start(f32[384,128]{1,0:T(8,128)S(1)} %get-tuple-element.46), channel_id=1, source_target_pairs={{0,4},{2,6},{4,0},{6,2},{8,12},{10,14},{12,8},{14,10},{1,5},{3,7},... | collective-permute-start | bytes 589832 | tf_op jit(solution)/shard_map/ppermute | solution.py:432
  6.5 21.4 %collective-permute-start.2 = (f32[384,128]{1,0:T(8,128)S(1)}, f32[384,128]{1,0:T(8,128)S(1)}, u32[]{:S(2)}, u32[]{:S(2)}) collective-permute-start(f32[384,128]{1,0:T(8,128)S(1)} %get-tuple-element.47), channel_id=1, source_target_pairs={{0,6},{2,4},{4,2},{6,0},{8,14},{10,12},{12,10},{14,8},{1,7},{3,5},... | collective-permute-start | bytes 589832 | tf_op jit(solution)/shard_map/ppermute | solution.py:432
  8.1 19.9 %collective-permute-start.3 = (f32[384,128]{1,0:T(8,128)S(1)}, f32[384,128]{1,0:T(8,128)S(1)}, u32[]{:S(2)}, u32[]{:S(2)}) collective-permute-start(f32[384,128]{1,0:T(8,128)S(1)} %get-tuple-element.48), channel_id=1, source_target_pairs={{0,2},{2,0},{4,6},{6,4},{8,10},{10,8},{12,14},{14,12},{1,3},{3,1},... | collective-permute-start | bytes 589832 | tf_op jit(solution)/shard_map/ppermute | solution.py:432
  13.2 6.6 %collective-permute-start.5 = (f32[256,128]{1,0:T(8,128)S(1)}, f32[256,128]{1,0:T(8,128)S(1)}, u32[]{:S(2)}, u32[]{:S(2)}) collective-permute-start(f32[256,128]{1,0:T(8,128)S(1)} %get-tuple-element.50), channel_id=1, source_target_pairs={{0,12},{2,14},{4,8},{6,10},{8,4},{10,6},{12,0},{14,2},{1,13},{3,15... | collective-permute-start | bytes 393224 | tf_op jit(solution)/shard_map/ppermute | solution.py:432
  16.0 11.9 %collective-permute-start.6 = (f32[256,128]{1,0:T(8,128)S(1)}, f32[256,128]{1,0:T(8,128)S(1)}, u32[]{:S(2)}, u32[]{:S(2)}) collective-permute-start(f32[256,128]{1,0:T(8,128)S(1)} %get-tuple-element.51), channel_id=1, source_target_pairs={{0,14},{2,12},{4,10},{6,8},{8,6},{10,4},{12,2},{14,0},{1,15},{3,13... | collective-permute-start | bytes 393224 | tf_op jit(solution)/shard_map/ppermute | solution.py:432
  28.6 6.4 %collective-permute-start.7 = (f32[192,128]{1,0:T(8,128)S(1)}, f32[192,128]{1,0:T(8,128)S(1)}, u32[]{:S(2)}, u32[]{:S(2)}) collective-permute-start(f32[192,128]{1,0:T(8,128)S(1)} %get-tuple-element.72), channel_id=1, source_target_pairs={{0,4},{4,0},{2,6},{6,2},{8,12},{12,8},{10,14},{14,10},{1,5},{5,1},... | collective-permute-start | bytes 294920 | tf_op jit(solution)/shard_map/ppermute | solution.py:444
  28.7 7.5 %collective-permute-start.8 = (f32[192,128]{1,0:T(8,128)S(1)}, f32[192,128]{1,0:T(8,128)S(1)}, u32[]{:S(2)}, u32[]{:S(2)}) collective-permute-start(f32[192,128]{1,0:T(8,128)S(1)} %get-tuple-element.73), channel_id=1, source_target_pairs={{4,8},{8,4},{6,10},{10,6},{5,9},{9,5},{7,11},{11,7},{20,24},{24,20... | collective-permute-start | bytes 294920 | tf_op jit(solution)/shard_map/ppermute | solution.py:445
  37.0 1.8 %collective-permute-start.9 = (f32[800,128]{1,0:T(8,128)S(1)}, f32[800,128]{1,0:T(8,128)S(1)}, u32[]{:S(2)}, u32[]{:S(2)}) collective-permute-start(f32[800,128]{1,0:T(8,128)S(1)} %get-tuple-element.76), channel_id=1, source_target_pairs={{0,1},{1,0},{2,3},{3,2},{4,5},{5,4},{6,7},{7,6},{8,9},{9,8},{10,11... | collective-permute-start | bytes 1228808 | tf_op jit(solution)/shard_map/ppermute | solution.py:460
  46.8 7.4 %collective-permute-start.10 = (f32[256,128]{1,0:T(8,128)S(1)}, f32[256,128]{1,0:T(8,128)S(1)}, u32[]{:S(2)}, u32[]{:S(2)}) collective-permute-start(f32[256,128]{1,0:T(8,128)S(1)} %get-tuple-element.77), channel_id=1, source_target_pairs={{0,8},{2,10},{4,12},{6,14},{8,0},{10,2},{12,4},{14,6},{1,9},{3,11}... | collective-permute-start | bytes 393224 | tf_op jit(solution)/shard_map/ppermute | solution.py:432
  46.8 10.5 %collective-permute-start.11 = (f32[256,128]{1,0:T(8,128)S(1)}, f32[256,128]{1,0:T(8,128)S(1)}, u32[]{:S(2)}, u32[]{:S(2)}) collective-permute-start(f32[256,128]{1,0:T(8,128)S(1)} %get-tuple-element.78), channel_id=1, source_target_pairs={{0,4},{2,6},{4,0},{6,2},{8,12},{10,14},{12,8},{14,10},{1,5},{3,7},... | collective-permute-start | bytes 393224 | tf_op jit(solution)/shard_map/ppermute | solution.py:432
  50.0 11.4 %collective-permute-start.12 = (f32[256,128]{1,0:T(8,128)S(1)}, f32[256,128]{1,0:T(8,128)S(1)}, u32[]{:S(2)}, u32[]{:S(2)}) collective-permute-start(f32[256,128]{1,0:T(8,128)S(1)} %get-tuple-element.79), channel_id=1, source_target_pairs={{0,6},{2,4},{4,2},{6,0},{8,14},{10,12},{12,10},{14,8},{1,7},{3,5},... | collective-permute-start | bytes 393224 | tf_op jit(solution)/shard_map/ppermute | solution.py:432
  50.9 10.5 %collective-permute-start.13 = (f32[256,128]{1,0:T(8,128)S(1)}, f32[256,128]{1,0:T(8,128)S(1)}, u32[]{:S(2)}, u32[]{:S(2)}) collective-permute-start(f32[256,128]{1,0:T(8,128)S(1)} %get-tuple-element.80), channel_id=1, source_target_pairs={{0,2},{2,0},{4,6},{6,4},{8,10},{10,8},{12,14},{14,12},{1,3},{3,1},... | collective-permute-start | bytes 393224 | tf_op jit(solution)/shard_map/ppermute | solution.py:432
  51.5 12.0 %collective-permute-start.14 = (f32[256,128]{1,0:T(8,128)S(1)}, f32[256,128]{1,0:T(8,128)S(1)}, u32[]{:S(2)}, u32[]{:S(2)}) collective-permute-start(f32[256,128]{1,0:T(8,128)S(1)} %get-tuple-element.81), channel_id=1, source_target_pairs={{0,10},{2,8},{4,14},{6,12},{8,2},{10,0},{12,6},{14,4},{1,11},{3,9}... | collective-permute-start | bytes 393224 | tf_op jit(solution)/shard_map/ppermute | solution.py:432
  54.1 16.9 %collective-permute-start.15 = (f32[256,128]{1,0:T(8,128)S(1)}, f32[256,128]{1,0:T(8,128)S(1)}, u32[]{:S(2)}, u32[]{:S(2)}) collective-permute-start(f32[256,128]{1,0:T(8,128)S(1)} %get-tuple-element.82), channel_id=1, source_target_pairs={{0,12},{2,14},{4,8},{6,10},{8,4},{10,6},{12,0},{14,2},{1,13},{3,15... | collective-permute-start | bytes 393224 | tf_op jit(solution)/shard_map/ppermute | solution.py:432
  57.4 15.6 %collective-permute-start.16 = (f32[256,128]{1,0:T(8,128)S(1)}, f32[256,128]{1,0:T(8,128)S(1)}, u32[]{:S(2)}, u32[]{:S(2)}) collective-permute-start(f32[256,128]{1,0:T(8,128)S(1)} %get-tuple-element.83), channel_id=1, source_target_pairs={{0,14},{2,12},{4,10},{6,8},{8,6},{10,4},{12,2},{14,0},{1,15},{3,13... | collective-permute-start | bytes 393224 | tf_op jit(solution)/shard_map/ppermute | solution.py:432

commit v4 on v3

--- a/solution.py
+++ b/solution.py
@@ -13,6 +13,7 @@
 TILE = 8
 COEFS = 9
 RAW = 4
+GROUP = 6
 
 alpha_circ = 0.1
 inv_step = 2.0
@@ -40,6 +41,9 @@
     def direct(self, r):
         return r // self.per_quarter < 2
 
+    def stride(self, r):
+        return self.rows + TILE if self.direct(r) else self.rows
+
     def pairs(self, r):
         return [(i, i ^ r) for i in range(self.steps)]
 
@@ -73,15 +77,14 @@
         self.hi_odd, self.zb_odd = self.hi % 2 == 1, self.zb % 2 == 1
 
 
-def kernel_call(body, outs, args, scratch=(), out_space=pltpu.VMEM, limit=16, aliases=None):
-    in_specs = [pl.BlockSpec(memory_space=pltpu.SMEM)]
-    in_specs += [pl.BlockSpec(memory_space=pltpu.VMEM)] * (len(args) - 1)
+def kernel_call(body, outs, args, scratch=(), spaces=None, out_space=pltpu.VMEM, limit=16, aliases=None):
+    spaces = [pltpu.SMEM] + (spaces or [pltpu.VMEM] * (len(args) - 1))
     single = isinstance(outs, tuple)
     shapes = [outs] if single else list(outs)
     result = pl.pallas_call(
         body,
         out_shape=[jax.ShapeDtypeStruct(s, jnp.float32) for s in shapes],
-        in_specs=in_specs,
+        in_specs=[pl.BlockSpec(memory_space=space) for space in spaces],
         out_specs=[pl.BlockSpec(memory_space=out_space)] * len(shapes),
         scratch_shapes=list(scratch),
         input_output_aliases=aliases or {},
@@ -169,22 +172,23 @@
                     raw[rows_at((n * plan.tiles + k) * RAW + at), :] = value
 
 
-def pack_blocks(plan, place_ref, right, *outs):
+def pack_blocks(plan, rounds, place_ref, right, *outs):
     place = Place(plan, place_ref)
     per = plan.nx // TILE
     row = sublane(plan)
-    for out, r in zip(outs, plan.rounds):
+    for out, r in zip(outs, rounds):
         target = place.t ^ r
         quarter, lo = target // plan.per_quarter, target % plan.per_quarter
         first = lo % 2 * plan.half_z + lo // 2 * plan.nz
         own, over, under = near_tiles(plan, quarter)
+        tiles = plan.stride(r) // TILE
         for z in range(plan.nz):
             base = (first + z) * per
             for k, at in enumerate(own):
-                out[rows_at(z * plan.main + k), :] = right[rows_at(base + at), :]
+                out[rows_at(z * tiles + k), :] = right[rows_at(base + at), :]
             if plan.direct(r):
                 edge = jnp.where(row < TILE // 2, right[rows_at(base + over), :], right[rows_at(base + under), :])
-                out[rows_at(plan.nz * plan.main + z), :] = edge
+                out[rows_at(z * tiles + plan.main), :] = edge
 
 
 def edge_rows(plan, place_ref, *refs):
@@ -193,9 +197,10 @@
     half = plan.steps // 2
     for block, r in zip(blocks, plan.rounds):
         step = (place.t ^ r) % half
+        stride = plan.stride(r)
         for n in range(GHOST):
-            low = block[pl.ds(n, plan.nz, stride=plan.rows), :]
-            high = block[pl.ds(plan.rows - GHOST + n, plan.nz, stride=plan.rows), :]
+            low = block[pl.ds(n, plan.nz, stride=stride), :]
+            high = block[pl.ds(plan.rows - GHOST + n, plan.nz, stride=stride), :]
             at = pl.ds((n * half + step) * plan.nz, plan.nz)
             if plan.direct(r):
                 x_odd[at, :] = jnp.where(place.hi_odd, high, low)
@@ -208,8 +213,10 @@
     blocks, field = refs[: plan.steps], refs[plan.steps]
     size = plan.nz * plan.rows
     for block, r in zip(blocks, plan.rounds):
-        at = pl.multiple_of((place.t ^ r) * size, TILE)
-        field[pl.ds(at, size), :] = block[pl.ds(0, size), :]
+        at = (place.t ^ r) * size
+        for z in range(plan.nz):
+            to = pl.ds(pl.multiple_of(at + z * plan.rows, TILE), plan.rows)
+            field[to, :] = block[pl.ds(z * plan.stride(r), plan.rows), :]
 
 
 def gather_ghosts(plan, place_ref, field, even_ref, odd_ref, *refs):
@@ -220,10 +227,10 @@
     ghost, z_sends, planes = refs[0], refs[1:-1], refs[-1]
     half = plan.steps // 2
     count = half * plan.nz
-    size = plan.nz * plan.rows
     for block, r in zip(blocks, direct):
-        at = pl.multiple_of((place.t ^ r) * plan.nz * TILE, TILE)
-        ghost[pl.ds(at, plan.nz * TILE), :] = block[pl.ds(size, plan.nz * TILE), :]
+        at = (place.t ^ r) * plan.nz
+        for z in range(plan.nz):
+            ghost[rows_at(at + z), :] = block[pl.ds(z * plan.stride(r) + plan.rows, TILE), :]
     for n in range(GHOST):
         even, odd = even_ref[pl.ds(n * count, count), :], odd_ref[pl.ds(n * count, count), :]
         planes[pl.ds(n * count, count), :] = jnp.where(place.hi_odd, odd, even)
@@ -282,39 +289,58 @@
         row = sublane(plan)
         spot, coef = self.spot, self.coef
 
-        def layer(e, _):
-            c = [coef(e, k, 1) for k in range(wide)]
-            near = [[coef(e, k, n) for n in range(3, COEFS)] for k in range(wide)]
-            partial = [[] for _ in range(wide)]
-            for t in range(steps):
-                here = [old[spot(e, k, t), :] for k in range(tiles)]
-                down = [pltpu.roll(value, 1, 0) for value in here]
-                up = [pltpu.roll(value, TILE - 1, 0) for value in here]
-                for k in range(wide):
-                    z_low, x_low, y_low, z_high, x_high, y_high = near[k]
-                    below = jnp.where(row == 0, down[k - 1], down[k])
-                    above = jnp.where(row == TILE - 1, up[(k + 1) % tiles], up[k])
-                    total = self.source[spot(e, k, t), :] + z_low * old[spot(e - 1, k, t), :]
-                    total = total + z_high * old[spot(e + 1, k, t), :]
-                    total = total + (x_low * below + x_high * above)
-                    total = total + (
-                        y_low * pltpu.roll(here[k], 1, 1) + y_high * pltpu.roll(here[k], ny - 1, 1)
-                    )
-                    if t:
-                        total = total + c[k] * partial[k][-1]
-                    partial[k].append(total)
-            for k in range(wide):
-                carry = c[k] * (coef(e, k, 2) * partial[k][-1])
+        def layers(e, count):
+            parts = [(e + g, k) for g in range(count) for k in range(wide)]
+            c = [coef(at, k, 1) for at, k in parts]
+            near = [[coef(at, k, n) for n in range(3, COEFS)] for at, k in parts]
+            partial = [[] for _ in parts]
+            for g in range(count):
+                at = e + g
                 for t in range(steps):
-                    value = partial[k][t] + carry
-                    carry = c[k] * carry
+                    here = [old[spot(at, k, t), :] for k in range(tiles)]
+                    down = [pltpu.roll(value, 1, 0) for value in here]
+                    up = [pltpu.roll(value, TILE - 1, 0) for value in here]
+                    for k in range(wide):
+                        n = g * wide + k
+                        z_low, x_low, y_low, z_high, x_high, y_high = near[n]
+                        below = jnp.where(row == 0, down[k - 1], down[k])
+                        above = jnp.where(row == TILE - 1, up[(k + 1) % tiles], up[k])
+                        total = self.source[spot(at, k, t), :] + z_low * old[spot(at - 1, k, t), :]
+                        total = total + z_high * old[spot(at + 1, k, t), :]
+                        total = total + (x_low * below + x_high * above)
+                        total = total + (
+                            y_low * pltpu.roll(here[k], 1, 1) + y_high * pltpu.roll(here[k], ny - 1, 1)
+                        )
+                        if t:
+                            total = total + c[n] * partial[n][-1]
+                        partial[n].append(total)
+            for n, (at, k) in enumerate(parts):
+                carry = c[n] * (coef(at, k, 2) * partial[n][-1])
+                for t in range(steps):
+                    value = partial[n][t] + carry
+                    carry = c[n] * carry
                     if final:
-                        self.last[rows_at((t * plan.nz + e - GHOST) * plan.main + k), :] = value
+                        self.last[rows_at((t * plan.nz + at - GHOST) * plan.main + k), :] = value
                     else:
-                        new[spot(e, k, t), :] = value
-            return 0
-
-        lax.fori_loop(start, stop, layer, 0)
+                        new[spot(at, k, t), :] = value
+
+        if plan.sides == 1:
+            total = plan.nz + SWEEPS - 1 - number
+
+            def several(i, _):
+                layers(start + i * GROUP, GROUP)
+                return 0
+
+            lax.fori_loop(0, total // GROUP, several, 0)
+            if total % GROUP:
+                layers(start + total // GROUP * GROUP, total % GROUP)
+        else:
+
+            def one(e, _):
+                layers(e, 1)
+                return 0
+
+            lax.fori_loop(start, stop, one, 0)
 
 
 def all_sweeps(plan, place_ref, coefs_in, field, ghost, *refs):
@@ -326,13 +352,15 @@
     deep = GHOST - 1
     empty = jnp.zeros((TILE, plan.ny), jnp.float32)
 
-    def own_layer(z, _):
-        for k in range(main):
-            work.first(z + GHOST, k, [field[rows_at((t * plan.nz + z) * main + k), :] for t in range(steps)])
-        work.first(z + GHOST, main, [ghost[rows_at(t * plan.nz + z), :] for t in range(steps)])
+    def own_layers(i, _):
+        for n in range(4):
+            z = i * 4 + n
+            for k in range(main):
+                work.first(z + GHOST, k, [field[rows_at((t * plan.nz + z) * main + k), :] for t in range(steps)])
+            work.first(z + GHOST, main, [ghost[rows_at(t * plan.nz + z), :] for t in range(steps)])
         return 0
 
-    lax.fori_loop(0, plan.nz, own_layer, 0)
+    lax.fori_loop(0, plan.nz // 4, own_layers, 0)
 
     def ghost_layers(at, upper, z_ref):
         for n in range(GHOST):
@@ -402,7 +430,7 @@
 
 def place_blocks(plan, place_ref, *refs):
     place = Place(plan, place_ref)
-    blocks, out, sems = refs[: plan.steps], refs[plan.steps], refs[plan.steps + 1]
+    blocks, (out, sems) = refs[: plan.steps], refs[plan.steps :]
     copies = []
     for n, (block, r) in enumerate(zip(blocks, plan.rounds)):
         source = place.t ^ r
@@ -425,20 +453,20 @@
     size = plan.nz * plan.rows
     half_x = steps // 2 * plan.nz
 
-    def call(body, outs, arrays, **options):
-        return kernel_call(functools.partial(body, plan), outs, (place, *arrays), **options)
+    def call(body, outs, arrays, rounds=None, **options):
+        body = functools.partial(body, plan) if rounds is None else functools.partial(body, plan, rounds)
+        return kernel_call(body, outs, (place, *arrays), **options)
 
     def turned(arrays):
         return [array if r == 0 else lax.ppermute(array, "tm", plan.pairs(r)) for array, r in zip(arrays, plan.rounds)]
 
-    with_ghosts = (size + plan.nz * TILE, ny)
-    blocks = turned(
-        call(
-            pack_blocks,
-            [with_ghosts if plan.direct(r) else (size, ny) for r in plan.rounds],
-            (right_side.reshape(parts * half_z * nx, ny),),
-        )
-    )
+    sends = call(
+        pack_blocks,
+        [(plan.nz * plan.stride(r), ny) for r in plan.rounds],
+        (right_side.reshape(parts * half_z * nx, ny),),
+        rounds=plan.rounds,
+    )
+    blocks = turned(sends)
     blocks = lax.optimization_barrier(blocks)
     x_even, x_odd = call(edge_rows, [(GHOST * half_x, ny)] * 2, blocks)
     even = lax.ppermute(x_even, "tm", plan.x_pairs(0))

time: 74.7 us -> 71.2 us (0.953)
  Pallas kernels: 13.4 us -> 9.96 us
    pallas_call x7, Pallas kernels: 13.4 us -> 9.96 us  [kernel_call(): pl.pallas_call(body, out_shape=[jax.ShapeDtypeStruct(s, jnp.float32) for...]
where the time goes in v4:
time: 71.2 us; the launch traced here: 71.1 us
  waiting for transfers between devices  37.7 us (53%)
  starting transfers between devices  21.9 us (31%)
  Pallas kernels  9.96 us (14%)
  local copies, waits for them, and re-layouts  1.34 us (2%)
    ppermute x14, waiting for transfers between devices, turned(): lax.ppermute(array, 'tm', plan.pairs(r))  34.8 us
    ppermute x14, starting transfers between devices, turned(): lax.ppermute(array, 'tm', plan.pairs(r))  17.2 us
    pallas_call x7, Pallas kernels, kernel_call(): pl.pallas_call(body, out_shape=[jax.ShapeDtypeStruct(s, jnp.float32) for...  9.96 us
    ppermute x1, starting transfers between devices, local(): odd = lax.ppermute(x_odd, 'tm', plan.x_pairs(1))  4.54 us
    ppermute x1, waiting for transfers between devices, local(): lax.ppermute(send, FLAT, plan.z_pairs(first))  1.73 us
  transfers between devices with their start and end apart: 17, of which 12 were waited for; matrix products, arithmetic and copies ran while one was open for 0% of the time, Pallas kernels for 2%

profile of v4, /device:TPU:8, one launch (start us, length us, event | category | flops | bytes accessed | tf_op | source)
XLA Modules:
  0.0 71.1 jit_solution(16252192352762883048)
XLA Ops:
  0.1 1.3 %copy-done.1 = f32[1,2,16,64,128]{4,3,2,1,0:T(8,128)S(1)} copy-done((f32[1,2,16,64,128]{4,3,2,1,0:T(8,128)S(1)}, f32[1,2,16,64,128]{4,3,2,1,0:T(8,128)}, u32[]{:S(2)}) %copy-start.1) | copy-done | bytes 1048600
  2.1 2.7 %collective-permute-start = (f32[256,128]{1,0:T(8,128)S(1)}, f32[256,128]{1,0:T(8,128)S(1)}, u32[]{:S(2)}, u32[]{:S(2)}) collective-permute-start(f32[256,128]{1,0:T(8,128)S(1)} %get-tuple-element.45), channel_id=1, source_target_pairs={{0,8},{2,10},{4,12},{6,14},{8,0},{10,2},{12,4},{14,6},{1,9},{3,11}... | collective-permute-start | bytes 393224 | tf_op jit(solution)/shard_map/ppermute | solution.py:461
  4.8 1.3 %collective-permute-start.4 = (f32[256,128]{1,0:T(8,128)S(1)}, f32[256,128]{1,0:T(8,128)S(1)}, u32[]{:S(2)}, u32[]{:S(2)}) collective-permute-start(f32[256,128]{1,0:T(8,128)S(1)} %get-tuple-element.49), channel_id=1, source_target_pairs={{0,10},{2,8},{4,14},{6,12},{8,2},{10,0},{12,6},{14,4},{1,11},{3,9}... | collective-permute-start | bytes 393224 | tf_op jit(solution)/shard_map/ppermute | solution.py:461
  6.5 1.5 %collective-permute-start.2 = (f32[384,128]{1,0:T(8,128)S(1)}, f32[384,128]{1,0:T(8,128)S(1)}, u32[]{:S(2)}, u32[]{:S(2)}) collective-permute-start(f32[384,128]{1,0:T(8,128)S(1)} %get-tuple-element.47), channel_id=1, source_target_pairs={{0,6},{2,4},{4,2},{6,0},{8,14},{10,12},{12,10},{14,8},{1,7},{3,5},... | collective-permute-start | bytes 589832 | tf_op jit(solution)/shard_map/ppermute | solution.py:461
  8.1 1.5 %collective-permute-start.3 = (f32[384,128]{1,0:T(8,128)S(1)}, f32[384,128]{1,0:T(8,128)S(1)}, u32[]{:S(2)}, u32[]{:S(2)}) collective-permute-start(f32[384,128]{1,0:T(8,128)S(1)} %get-tuple-element.48), channel_id=1, source_target_pairs={{0,2},{2,0},{4,6},{6,4},{8,10},{10,8},{12,14},{14,12},{1,3},{3,1},... | collective-permute-start | bytes 589832 | tf_op jit(solution)/shard_map/ppermute | solution.py:461
  9.6 3.6 %collective-permute-done.refs_0_ = f32[256,128]{1,0:T(8,128)S(1)} collective-permute-done((f32[256,128]{1,0:T(8,128)S(1)}, f32[256,128]{1,0:T(8,128)S(1)}, u32[]{:S(2)}, u32[]{:S(2)}) %collective-permute-start) | collective-permute-done | bytes 131104 | tf_op jit(solution)/shard_map/ppermute | solution.py:461
  13.2 2.9 %collective-permute-done.4.refs_4_ = f32[256,128]{1,0:T(8,128)S(1)} collective-permute-done((f32[256,128]{1,0:T(8,128)S(1)}, f32[256,128]{1,0:T(8,128)S(1)}, u32[]{:S(2)}, u32[]{:S(2)}) %collective-permute-start.4) | collective-permute-done | bytes 131104 | tf_op jit(solution)/shard_map/ppermute | solution.py:461
  16.3 3.5 %collective-permute-done.5.refs_5_ = f32[256,128]{1,0:T(8,128)S(1)} collective-permute-done((f32[256,128]{1,0:T(8,128)S(1)}, f32[256,128]{1,0:T(8,128)S(1)}, u32[]{:S(2)}, u32[]{:S(2)}) %collective-permute-start.5) | collective-permute-done | bytes 131104 | tf_op jit(solution)/shard_map/ppermute | solution.py:461
  19.8 8.2 %collective-permute-done.6.refs_6_ = f32[256,128]{1,0:T(8,128)S(1)} collective-permute-done((f32[256,128]{1,0:T(8,128)S(1)}, f32[256,128]{1,0:T(8,128)S(1)}, u32[]{:S(2)}, u32[]{:S(2)}) %collective-permute-start.6) | collective-permute-done | bytes 131104 | tf_op jit(solution)/shard_map/ppermute | solution.py:461
  28.7 4.5 %collective-permute-start.8 = (f32[192,128]{1,0:T(8,128)S(1)}, f32[192,128]{1,0:T(8,128)S(1)}, u32[]{:S(2)}, u32[]{:S(2)}) collective-permute-start(f32[192,128]{1,0:T(8,128)S(1)} %get-tuple-element.73), channel_id=1, source_target_pairs={{4,8},{8,4},{6,10},{10,6},{5,9},{9,5},{7,11},{11,7},{20,24},{24,20... | collective-permute-start | bytes 294920 | tf_op jit(solution)/shard_map/ppermute | solution.py:473
  33.3 1.1 %shard_map.38 = (f32[4752,128]{1,0:T(8,128)S(1)}, f32[288,128]{1,0:T(8,128)S(1)}) custom-call(s32[2]{0:T(128)S(1)} %pad_add_fusion.place_ref, f32[1024,128]{1,0:T(8,128)S(1)} %bitcast.16, f32[3072,128]{1,0:T(8,128)S(1)} %bitcast.14), custom_call_target="tpu_custom_call" | custom-call | tf_op jit(solution)/shard_map/pallas_call | solution.py:84
  35.0 1.2 %collective-permute-done.8.odd_ref = f32[192,128]{1,0:T(8,128)S(1)} collective-permute-done((f32[192,128]{1,0:T(8,128)S(1)}, f32[192,128]{1,0:T(8,128)S(1)}, u32[]{:S(2)}, u32[]{:S(2)}) %collective-permute-start.8) | collective-permute-done | bytes 98336 | tf_op jit(solution)/shard_map/ppermute | solution.py:473
  37.0 1.7 %collective-permute-done.9.refs_0_ = f32[800,128]{1,0:T(8,128)S(1)} collective-permute-done((f32[800,128]{1,0:T(8,128)S(1)}, f32[800,128]{1,0:T(8,128)S(1)}, u32[]{:S(2)}, u32[]{:S(2)}) %collective-permute-start.9) | collective-permute-done | bytes 409632 | tf_op jit(solution)/shard_map/ppermute | solution.py:488
  38.8 4.5 %shard_map.42 = (f32[256,128]{1,0:T(8,128)S(1)}, f32[256,128]{1,0:T(8,128)S(1)}, f32[256,128]{1,0:T(8,128)S(1)}, f32[256,128]{1,0:T(8,128)S(1)}, f32[256,128]{1,...) custom-call(s32[2]{0:T(128)S(1)} %pad_add_fusion.place_ref, ...), custom_call_target="tpu_custom_call", output_to_operand_aliasing={{8}: (1, {})} | custom-call | tf_op jit(solution)/shard_map/pallas_call | solution.py:84
  43.4 3.2 %collective-permute-start.11 = (f32[256,128]{1,0:T(8,128)S(1)}, f32[256,128]{1,0:T(8,128)S(1)}, u32[]{:S(2)}, u32[]{:S(2)}) collective-permute-start(f32[256,128]{1,0:T(8,128)S(1)} %get-tuple-element.78), channel_id=1, source_target_pairs={{0,4},{2,6},{4,0},{6,2},{8,12},{10,14},{12,8},{14,10},{1,5},{3,7},... | collective-permute-start | bytes 393224 | tf_op jit(solution)/shard_map/ppermute | solution.py:461
  46.6 0.9 %collective-permute-start.12 = (f32[256,128]{1,0:T(8,128)S(1)}, f32[256,128]{1,0:T(8,128)S(1)}, u32[]{:S(2)}, u32[]{:S(2)}) collective-permute-start(f32[256,128]{1,0:T(8,128)S(1)} %get-tuple-element.79), channel_id=1, source_target_pairs={{0,6},{2,4},{4,2},{6,0},{8,14},{10,12},{12,10},{14,8},{1,7},{3,5},... | collective-permute-start | bytes 393224 | tf_op jit(solution)/shard_map/ppermute | solution.py:461
  48.0 2.4 %collective-permute-start.14 = (f32[256,128]{1,0:T(8,128)S(1)}, f32[256,128]{1,0:T(8,128)S(1)}, u32[]{:S(2)}, u32[]{:S(2)}) collective-permute-start(f32[256,128]{1,0:T(8,128)S(1)} %get-tuple-element.81), channel_id=1, source_target_pairs={{0,10},{2,8},{4,14},{6,12},{8,2},{10,0},{12,6},{14,4},{1,11},{3,9}... | collective-permute-start | bytes 393224 | tf_op jit(solution)/shard_map/ppermute | solution.py:461
  50.7 1.8 %collective-permute-start.15 = (f32[256,128]{1,0:T(8,128)S(1)}, f32[256,128]{1,0:T(8,128)S(1)}, u32[]{:S(2)}, u32[]{:S(2)}) collective-permute-start(f32[256,128]{1,0:T(8,128)S(1)} %get-tuple-element.82), channel_id=1, source_target_pairs={{0,12},{2,14},{4,8},{6,10},{8,4},{10,6},{12,0},{14,2},{1,13},{3,15... | collective-permute-start | bytes 393224 | tf_op jit(solution)/shard_map/ppermute | solution.py:461
  52.4 1.5 %collective-permute-done.11 = f32[256,128]{1,0:T(8,128)S(1)} collective-permute-done((f32[256,128]{1,0:T(8,128)S(1)}, f32[256,128]{1,0:T(8,128)S(1)}, u32[]{:S(2)}, u32[]{:S(2)}) %collective-permute-start.11) | collective-permute-done | bytes 131104 | tf_op jit(solution)/shard_map/ppermute | solution.py:461
  54.6 3.3 %collective-permute-done.12 = f32[256,128]{1,0:T(8,128)S(1)} collective-permute-done((f32[256,128]{1,0:T(8,128)S(1)}, f32[256,128]{1,0:T(8,128)S(1)}, u32[]{:S(2)}, u32[]{:S(2)}) %collective-permute-start.12) | collective-permute-done | bytes 131104 | tf_op jit(solution)/shard_map/ppermute | solution.py:461
  57.9 2.1 %collective-permute-done.14 = f32[256,128]{1,0:T(8,128)S(1)} collective-permute-done((f32[256,128]{1,0:T(8,128)S(1)}, f32[256,128]{1,0:T(8,128)S(1)}, u32[]{:S(2)}, u32[]{:S(2)}) %collective-permute-start.14) | collective-permute-done | bytes 131104 | tf_op jit(solution)/shard_map/ppermute | solution.py:461
  60.1 7.5 %collective-permute-done.15 = f32[256,128]{1,0:T(8,128)S(1)} collective-permute-done((f32[256,128]{1,0:T(8,128)S(1)}, f32[256,128]{1,0:T(8,128)S(1)}, u32[]{:S(2)}, u32[]{:S(2)}) %collective-permute-start.15) | collective-permute-done | bytes 131104 | tf_op jit(solution)/shard_map/ppermute | solution.py:461
  67.5 2.0 %collective-permute-done.16 = f32[256,128]{1,0:T(8,128)S(1)} collective-permute-done((f32[256,128]{1,0:T(8,128)S(1)}, f32[256,128]{1,0:T(8,128)S(1)}, u32[]{:S(2)}, u32[]{:S(2)}) %collective-permute-start.16) | collective-permute-done | bytes 131104 | tf_op jit(solution)/shard_map/ppermute | solution.py:461
  69.5 1.6 %shard_map.43 = f32[2,16,64,128]{3,2,1,0:T(8,128)} custom-call(s32[2]{0:T(128)S(1)} %pad_add_fusion.place_ref, f32[16,16,128]{2,1,0:T(8,128)S(1)} %bitcast.18, f32[16,16,128]{2,1,0:T(8,128)S(1)} %bitcast.19, f32[16,16,128]{2,1,0:T(8,128)S(1)} %bitcast.20, f32[16,16,128]{2,1,0:T(8,128)S(1)} %bitcast.21, f32[16,16,128]{2,1,0:T(8,128)S(1)} %bitcast.22, ...), custom_call_target="tpu_custom_call" | custom-call | tf_op jit(solution)/shard_map/pallas_call | solution.py:84
  (24 shorter events, 5.3 us)
Async XLA Ops:
  0.0 33.2 %copy-start = (f32[3,16,64,128]{3,2,1,0:T(8,128)S(1)}, f32[3,16,64,128]{3,2,1,0:T(8,128)}, u32[]{:S(2)}) copy-start(f32[3,16,64,128]{3,2,1,0:T(8,128)} %param.5) | copy-start | bytes 4718596
  0.1 1.3 %copy-start.1 = (f32[1,2,16,64,128]{4,3,2,1,0:T(8,128)S(1)}, f32[1,2,16,64,128]{4,3,2,1,0:T(8,128)}, u32[]{:S(2)}) copy-start(f32[1,2,16,64,128]{4,3,2,1,0:T(8,128)} %param.3) | copy-start | bytes 3145732
  1.4 31.8 %copy-start.2 = (f32[16,64,128]{2,1,0:T(8,128)S(1)}, f32[16,64,128]{2,1,0:T(8,128)}, u32[]{:S(2)}) copy-start(f32[16,64,128]{2,1,0:T(8,128)} %param.4) | copy-start | bytes 1572868
  2.1 11.1 %collective-permute-start = (f32[256,128]{1,0:T(8,128)S(1)}, f32[256,128]{1,0:T(8,128)S(1)}, u32[]{:S(2)}, u32[]{:S(2)}) collective-permute-start(f32[256,128]{1,0:T(8,128)S(1)} %get-tuple-element.45), channel_id=1, source_target_pairs={{0,8},{2,10},{4,12},{6,14},{8,0},{10,2},{12,4},{14,6},{1,9},{3,11}... | collective-permute-start | bytes 393224 | tf_op jit(solution)/shard_map/ppermute | solution.py:461
  4.8 11.3 %collective-permute-start.4 = (f32[256,128]{1,0:T(8,128)S(1)}, f32[256,128]{1,0:T(8,128)S(1)}, u32[]{:S(2)}, u32[]{:S(2)}) collective-permute-start(f32[256,128]{1,0:T(8,128)S(1)} %get-tuple-element.49), channel_id=1, source_target_pairs={{0,10},{2,8},{4,14},{6,12},{8,2},{10,0},{12,6},{14,4},{1,11},{3,9}... | collective-permute-start | bytes 393224 | tf_op jit(solution)/shard_map/ppermute | solution.py:461
  6.1 21.9 %collective-permute-start.1 = (f32[384,128]{1,0:T(8,128)S(1)}, f32[384,128]{1,0:T(8,128)S(1)}, u32[]{:S(2)}, u32[]{:S(2)}) collective-permute-start(f32[384,128]{1,0:T(8,128)S(1)} %get-tuple-element.46), channel_id=1, source_target_pairs={{0,4},{2,6},{4,0},{6,2},{8,12},{10,14},{12,8},{14,10},{1,5},{3,7},... | collective-permute-start | bytes 589832 | tf_op jit(solution)/shard_map/ppermute | solution.py:461
  6.5 21.4 %collective-permute-start.2 = (f32[384,128]{1,0:T(8,128)S(1)}, f32[384,128]{1,0:T(8,128)S(1)}, u32[]{:S(2)}, u32[]{:S(2)}) collective-permute-start(f32[384,128]{1,0:T(8,128)S(1)} %get-tuple-element.47), channel_id=1, source_target_pairs={{0,6},{2,4},{4,2},{6,0},{8,14},{10,12},{12,10},{14,8},{1,7},{3,5},... | collective-permute-start | bytes 589832 | tf_op jit(solution)/shard_map/ppermute | solution.py:461
  8.1 19.9 %collective-permute-start.3 = (f32[384,128]{1,0:T(8,128)S(1)}, f32[384,128]{1,0:T(8,128)S(1)}, u32[]{:S(2)}, u32[]{:S(2)}) collective-permute-start(f32[384,128]{1,0:T(8,128)S(1)} %get-tuple-element.48), channel_id=1, source_target_pairs={{0,2},{2,0},{4,6},{6,4},{8,10},{10,8},{12,14},{14,12},{1,3},{3,1},... | collective-permute-start | bytes 589832 | tf_op jit(solution)/shard_map/ppermute | solution.py:461
  13.2 6.6 %collective-permute-start.5 = (f32[256,128]{1,0:T(8,128)S(1)}, f32[256,128]{1,0:T(8,128)S(1)}, u32[]{:S(2)}, u32[]{:S(2)}) collective-permute-start(f32[256,128]{1,0:T(8,128)S(1)} %get-tuple-element.50), channel_id=1, source_target_pairs={{0,12},{2,14},{4,8},{6,10},{8,4},{10,6},{12,0},{14,2},{1,13},{3,15... | collective-permute-start | bytes 393224 | tf_op jit(solution)/shard_map/ppermute | solution.py:461
  16.0 11.9 %collective-permute-start.6 = (f32[256,128]{1,0:T(8,128)S(1)}, f32[256,128]{1,0:T(8,128)S(1)}, u32[]{:S(2)}, u32[]{:S(2)}) collective-permute-start(f32[256,128]{1,0:T(8,128)S(1)} %get-tuple-element.51), channel_id=1, source_target_pairs={{0,14},{2,12},{4,10},{6,8},{8,6},{10,4},{12,2},{14,0},{1,15},{3,13... | collective-permute-start | bytes 393224 | tf_op jit(solution)/shard_map/ppermute | solution.py:461
  28.6 6.4 %collective-permute-start.7 = (f32[192,128]{1,0:T(8,128)S(1)}, f32[192,128]{1,0:T(8,128)S(1)}, u32[]{:S(2)}, u32[]{:S(2)}) collective-permute-start(f32[192,128]{1,0:T(8,128)S(1)} %get-tuple-element.72), channel_id=1, source_target_pairs={{0,4},{4,0},{2,6},{6,2},{8,12},{12,8},{10,14},{14,10},{1,5},{5,1},... | collective-permute-start | bytes 294920 | tf_op jit(solution)/shard_map/ppermute | solution.py:472
  28.7 7.5 %collective-permute-start.8 = (f32[192,128]{1,0:T(8,128)S(1)}, f32[192,128]{1,0:T(8,128)S(1)}, u32[]{:S(2)}, u32[]{:S(2)}) collective-permute-start(f32[192,128]{1,0:T(8,128)S(1)} %get-tuple-element.73), channel_id=1, source_target_pairs={{4,8},{8,4},{6,10},{10,6},{5,9},{9,5},{7,11},{11,7},{20,24},{24,20... | collective-permute-start | bytes 294920 | tf_op jit(solution)/shard_map/ppermute | solution.py:473
  37.0 1.8 %collective-permute-start.9 = (f32[800,128]{1,0:T(8,128)S(1)}, f32[800,128]{1,0:T(8,128)S(1)}, u32[]{:S(2)}, u32[]{:S(2)}) collective-permute-start(f32[800,128]{1,0:T(8,128)S(1)} %get-tuple-element.76), channel_id=1, source_target_pairs={{0,1},{1,0},{2,3},{3,2},{4,5},{5,4},{6,7},{7,6},{8,9},{9,8},{10,11... | collective-permute-start | bytes 1228808 | tf_op jit(solution)/shard_map/ppermute | solution.py:488
  43.3 7.4 %collective-permute-start.10 = (f32[256,128]{1,0:T(8,128)S(1)}, f32[256,128]{1,0:T(8,128)S(1)}, u32[]{:S(2)}, u32[]{:S(2)}) collective-permute-start(f32[256,128]{1,0:T(8,128)S(1)} %get-tuple-element.77), channel_id=1, source_target_pairs={{0,8},{2,10},{4,12},{6,14},{8,0},{10,2},{12,4},{14,6},{1,9},{3,11}... | collective-permute-start | bytes 393224 | tf_op jit(solution)/shard_map/ppermute | solution.py:461
  43.4 10.5 %collective-permute-start.11 = (f32[256,128]{1,0:T(8,128)S(1)}, f32[256,128]{1,0:T(8,128)S(1)}, u32[]{:S(2)}, u32[]{:S(2)}) collective-permute-start(f32[256,128]{1,0:T(8,128)S(1)} %get-tuple-element.78), channel_id=1, source_target_pairs={{0,4},{2,6},{4,0},{6,2},{8,12},{10,14},{12,8},{14,10},{1,5},{3,7},... | collective-permute-start | bytes 393224 | tf_op jit(solution)/shard_map/ppermute | solution.py:461
  46.6 11.4 %collective-permute-start.12 = (f32[256,128]{1,0:T(8,128)S(1)}, f32[256,128]{1,0:T(8,128)S(1)}, u32[]{:S(2)}, u32[]{:S(2)}) collective-permute-start(f32[256,128]{1,0:T(8,128)S(1)} %get-tuple-element.79), channel_id=1, source_target_pairs={{0,6},{2,4},{4,2},{6,0},{8,14},{10,12},{12,10},{14,8},{1,7},{3,5},... | collective-permute-start | bytes 393224 | tf_op jit(solution)/shard_map/ppermute | solution.py:461
  47.5 10.5 %collective-permute-start.13 = (f32[256,128]{1,0:T(8,128)S(1)}, f32[256,128]{1,0:T(8,128)S(1)}, u32[]{:S(2)}, u32[]{:S(2)}) collective-permute-start(f32[256,128]{1,0:T(8,128)S(1)} %get-tuple-element.80), channel_id=1, source_target_pairs={{0,2},{2,0},{4,6},{6,4},{8,10},{10,8},{12,14},{14,12},{1,3},{3,1},... | collective-permute-start | bytes 393224 | tf_op jit(solution)/shard_map/ppermute | solution.py:461
  48.0 12.0 %collective-permute-start.14 = (f32[256,128]{1,0:T(8,128)S(1)}, f32[256,128]{1,0:T(8,128)S(1)}, u32[]{:S(2)}, u32[]{:S(2)}) collective-permute-start(f32[256,128]{1,0:T(8,128)S(1)} %get-tuple-element.81), channel_id=1, source_target_pairs={{0,10},{2,8},{4,14},{6,12},{8,2},{10,0},{12,6},{14,4},{1,11},{3,9}... | collective-permute-start | bytes 393224 | tf_op jit(solution)/shard_map/ppermute | solution.py:461
  50.7 16.9 %collective-permute-start.15 = (f32[256,128]{1,0:T(8,128)S(1)}, f32[256,128]{1,0:T(8,128)S(1)}, u32[]{:S(2)}, u32[]{:S(2)}) collective-permute-start(f32[256,128]{1,0:T(8,128)S(1)} %get-tuple-element.82), channel_id=1, source_target_pairs={{0,12},{2,14},{4,8},{6,10},{8,4},{10,6},{12,0},{14,2},{1,13},{3,15... | collective-permute-start | bytes 393224 | tf_op jit(solution)/shard_map/ppermute | solution.py:461
  53.9 15.6 %collective-permute-start.16 = (f32[256,128]{1,0:T(8,128)S(1)}, f32[256,128]{1,0:T(8,128)S(1)}, u32[]{:S(2)}, u32[]{:S(2)}) collective-permute-start(f32[256,128]{1,0:T(8,128)S(1)} %get-tuple-element.83), channel_id=1, source_target_pairs={{0,14},{2,12},{4,10},{6,8},{8,6},{10,4},{12,2},{14,0},{1,15},{3,13... | collective-permute-start | bytes 393224 | tf_op jit(solution)/shard_map/ppermute | solution.py:461

commit v5 on v4

--- a/solution.py
+++ b/solution.py
@@ -38,6 +38,26 @@
         kinds = [(2, 0), (1, 0), (1, 1), (0, 1), (2, 1), (3, 0), (3, 1), (0, 0)]
         self.rounds = [a * self.per_quarter + m * 2 + c for m in range(self.in_half) for a, c in kinds]
 
+        self.back, self.ties = self.return_order()
+
+    def return_order(self):
+        pieces = len(self.pieces())
+        near = [r for r in self.rounds if self.direct(r)]
+        far = [r for r in self.rounds if not self.direct(r)]
+        if pieces == 1:
+            return [[(r, None) for r in far + near]], ()
+        far = far[2:] + far[:2]
+        back = [[(r, 0) for r in far], [(r, 1) for r in far] + [(r, None) for r in near]]
+        return back, [(2 * len(far) + n, len(far) - 1) for n in range(len(near) - 1)]
+
+    def pieces(self):
+        if self.sides == 1 and self.nz >= 4 * GHOST:
+            return [self.nz // 2, self.nz // 2]
+        return [self.nz]
+
+    def layers(self, piece):
+        return self.nz if piece is None else self.pieces()[piece]
+
     def direct(self, r):
         return r // self.per_quarter < 2
 
@@ -75,6 +95,14 @@
         self.zm, self.part = self.lo // 2, self.lo % 2
         self.zb = self.s * plan.in_half + self.zm
         self.hi_odd, self.zb_odd = self.hi % 2 == 1, self.zb % 2 == 1
+        self.up = self.zb == 0
+
+    def piece(self, plan, number):
+        sizes = plan.pieces()
+        before = sum(sizes[:number])
+        if len(sizes) == 1:
+            return 0
+        return jnp.where(self.up, before, plan.nz - before - sizes[number])
 
 
 def kernel_call(body, outs, args, scratch=(), spaces=None, out_space=pltpu.VMEM, limit=16, aliases=None):
@@ -281,7 +309,7 @@
             self.buffers[0][self.spot(e, k, t), :] = value + carry
             carry = c * carry
 
-    def sweep(self, number, start, stop):
+    def sweep(self, number, start, stop, total=None):
         plan, steps, tiles, ny = self.plan, self.plan.steps, self.plan.tiles, self.plan.ny
         old, new = self.buffers[(number - 1) % 2], self.buffers[number % 2]
         final = number == SWEEPS - 1
@@ -324,8 +352,7 @@
                     else:
                         new[spot(at, k, t), :] = value
 
-        if plan.sides == 1:
-            total = plan.nz + SWEEPS - 1 - number
+        if total is not None:
 
             def several(i, _):
                 layers(start + i * GROUP, GROUP)
@@ -343,24 +370,28 @@
             lax.fori_loop(start, stop, one, 0)
 
 
-def all_sweeps(plan, place_ref, coefs_in, field, ghost, *refs):
-    place = Place(plan, place_ref)
-    sides, steps, main = plan.sides, plan.steps, plan.main
-    z_in, refs = refs[:sides], refs[sides:]
-    outs, (coefs, source, ping, pong, last) = refs[:steps], refs[steps:]
-    work = Sweeps(plan, place, coefs, source, ping, pong, last)
-    deep = GHOST - 1
+def first_pass(plan, work, field, ghost, start, count):
+    steps, main = plan.steps, plan.main
+
+    def layer(z):
+        for k in range(main):
+            work.first(z + GHOST, k, [field[rows_at((t * plan.nz + z) * main + k), :] for t in range(steps)])
+        work.first(z + GHOST, main, [ghost[rows_at(t * plan.nz + z), :] for t in range(steps)])
+
+    def several(i, _):
+        for n in range(4):
+            layer(start + i * 4 + n)
+        return 0
+
+    lax.fori_loop(0, count // 4, several, 0)
+    for n in range(count // 4 * 4, count):
+        layer(start + n)
+
+
+def ghost_pass(plan, place, work, z_in):
+    steps, main, sides, deep = plan.steps, plan.main, plan.sides, GHOST - 1
+    coefs, source, ping = work.coefs, work.source, work.buffers[0]
     empty = jnp.zeros((TILE, plan.ny), jnp.float32)
-
-    def own_layers(i, _):
-        for n in range(4):
-            z = i * 4 + n
-            for k in range(main):
-                work.first(z + GHOST, k, [field[rows_at((t * plan.nz + z) * main + k), :] for t in range(steps)])
-            work.first(z + GHOST, main, [ghost[rows_at(t * plan.nz + z), :] for t in range(steps)])
-        return 0
-
-    lax.fori_loop(0, plan.nz // 4, own_layers, 0)
 
     def ghost_layers(at, upper, z_ref):
         for n in range(GHOST):
@@ -394,50 +425,105 @@
         def _(odd=odd):
             ghost_layers(work.high_at, True, z_in[sides - 1 if odd else 0])
 
+
+def no_ghosts(plan, work):
+    empty = jnp.zeros((TILE, plan.ny), jnp.float32)
     for outside, e in ((work.has_low, work.low_at - 1), (work.has_high, work.high_at)):
 
         @pl.when(jnp.logical_not(outside))
         def _(e=e):
             for k in range(plan.tiles):
-                for t in range(steps):
+                for t in range(plan.steps):
                     for buffer in work.buffers:
                         buffer[work.spot(e, k, t), :] = empty
 
+
+def write_piece(plan, place, last, outs, number):
+    for out, (r, piece) in zip(outs, plan.back[number]):
+        start = 0 if piece is None else place.piece(plan, piece)
+        at = ((place.t ^ r) * plan.nz + start) * plan.rows
+        out[...] = last[pl.ds(pl.multiple_of(at, TILE), out.shape[0]), :]
+
+
+def all_sweeps(plan, place_ref, coefs_in, field, ghost, *refs):
+    place = Place(plan, place_ref)
+    z_in, refs = refs[: plan.sides], refs[plan.sides :]
+    outs, (coefs, source, ping, pong, last) = refs[:-5], refs[-5:]
+    work = Sweeps(plan, place, coefs, source, ping, pong, last)
+    first_pass(plan, work, field, ghost, 0, plan.nz)
+    ghost_pass(plan, place, work, z_in)
+    no_ghosts(plan, work)
     for number in range(1, SWEEPS):
         reach = SWEEPS - 1 - number
         start = work.low_at - jnp.where(work.has_low, reach, 0)
         stop = work.high_at + jnp.where(work.has_high, reach, 0)
         work.sweep(number, start, stop)
-
-    size = plan.nz * plan.rows
-    for out, r in zip(outs, plan.rounds):
-        out[...] = last[pl.ds(pl.multiple_of((place.t ^ r) * size, TILE), size), :]
-
-
-def run_sweeps(plan, place, coefs, field, ghost, z_in):
-    size = plan.nz * plan.rows
-    grid = pltpu.VMEM((plan.ext * plan.tiles * plan.steps * TILE, plan.ny), jnp.float32)
-    outs = kernel_call(
-        functools.partial(all_sweeps, plan),
-        [(size, plan.ny)] * plan.steps + [coefs.shape],
-        (place, coefs, field, ghost, *z_in),
-        scratch=[grid] * 3 + [pltpu.VMEM((plan.steps * size, plan.ny), jnp.float32)],
-        aliases={1: plan.steps},
+    write_piece(plan, place, last, outs, 0)
+
+
+def far_sweeps(plan, place_ref, coefs, field, ghost, *refs):
+    place = Place(plan, place_ref)
+    outs, (source, ping, pong, last) = refs[:-4], refs[-4:]
+    work = Sweeps(plan, place, coefs, source, ping, pong, last)
+    count = plan.pieces()[0]
+    first_pass(plan, work, field, ghost, jnp.where(place.up, 0, plan.nz - count - GHOST), count + GHOST)
+    no_ghosts(plan, work)
+    for number in range(1, SWEEPS):
+        total = count + SWEEPS - 1 - number
+        start = jnp.where(place.up, work.low_at, work.high_at - total)
+        work.sweep(number, start, start + total, total)
+    write_piece(plan, place, last, outs, 0)
+
+
+def near_sweeps(plan, place_ref, field, ghost, z_in, coefs_in, source_in, ping_in, pong_in, last_in, *refs):
+    place = Place(plan, place_ref)
+    outs, (coefs, source, ping, pong, last) = refs[:-5], refs[-5:]
+    work = Sweeps(plan, place, coefs, source, ping, pong, last)
+    first, count = plan.pieces()
+    left = plan.nz - first - GHOST
+    first_pass(plan, work, field, ghost, jnp.where(place.up, plan.nz - left, 0), left)
+    ghost_pass(plan, place, work, [z_in])
+    for number in range(1, SWEEPS):
+        reach = SWEEPS - 1 - number
+        start = jnp.where(place.up, work.low_at + first + reach, work.low_at - reach)
+        work.sweep(number, start, start + count, count)
+    write_piece(plan, place, last, outs, 1)
+
+
+def run_sweeps(plan, call, coefs, field, ghost, z_of):
+    grid = (plan.ext * plan.tiles * plan.steps * TILE, plan.ny)
+    whole = (plan.steps * plan.nz * plan.rows, plan.ny)
+    shapes = [[(plan.layers(piece) * plan.rows, plan.ny) for r, piece in blocks] for blocks in plan.back]
+    if len(shapes) == 1:
+        scratch = [pltpu.VMEM(shape, jnp.float32) for shape in [grid] * 3 + [whole]]
+        inputs = (coefs, field, ghost, *z_of())
+        found = call(
+            all_sweeps, shapes[0] + [coefs.shape], inputs, scratch=scratch, aliases={1: len(shapes[0])}, limit=24
+        )
+        return [found[:-1]]
+    *done, source, ping, pong, last = call(
+        far_sweeps, shapes[0] + [grid] * 3 + [whole], (coefs, field, ghost), limit=24
+    )
+    rest = call(
+        near_sweeps,
+        shapes[1] + [coefs.shape] + [grid] * 3 + [whole],
+        (field, ghost, *z_of(), coefs, source, ping, pong, last),
+        aliases={4 + n: len(shapes[1]) + n for n in range(5)},
         limit=24,
     )
-    return outs[: plan.steps]
+    return [done, rest[:-5]]
 
 
 def place_blocks(plan, place_ref, *refs):
     place = Place(plan, place_ref)
-    blocks, (out, sems) = refs[: plan.steps], refs[plan.steps :]
+    blocks, (out, sems) = refs[:-2], refs[-2:]
     copies = []
-    for n, (block, r) in enumerate(zip(blocks, plan.rounds)):
+    for n, (block, (r, piece)) in enumerate(zip(blocks, sum(plan.back, []))):
         source = place.t ^ r
         quarter, lo = source // plan.per_quarter, source % plan.per_quarter
-        z = pl.multiple_of(lo // 2 * plan.nz, plan.nz)
+        z = lo // 2 * plan.nz + (0 if piece is None else place.piece(plan, piece))
         x = pl.multiple_of(quarter * plan.rows, plan.rows)
-        target = out.at[lo % 2, pl.ds(z, plan.nz), pl.ds(x, plan.rows), :]
+        target = out.at[lo % 2, pl.ds(z, plan.layers(piece)), pl.ds(x, plan.rows), :]
         copies.append(pltpu.make_async_copy(block, target, sems.at[n]))
     for copy in copies:
         copy.start()
@@ -453,20 +539,26 @@
     size = plan.nz * plan.rows
     half_x = steps // 2 * plan.nz
 
-    def call(body, outs, arrays, rounds=None, **options):
-        body = functools.partial(body, plan) if rounds is None else functools.partial(body, plan, rounds)
+    def call(body, outs, arrays, extra=None, **options):
+        body = functools.partial(body, plan) if extra is None else functools.partial(body, plan, extra)
         return kernel_call(body, outs, (place, *arrays), **options)
 
-    def turned(arrays):
-        return [array if r == 0 else lax.ppermute(array, "tm", plan.pairs(r)) for array, r in zip(arrays, plan.rounds)]
+    def turned(arrays, rounds, ties=(), known=()):
+        found = list(known)
+        for n, (array, r) in enumerate(zip(arrays, rounds), len(found)):
+            for late, early in ties:
+                if n == late:
+                    array, found[early] = lax.optimization_barrier((array, found[early]))
+            found.append(array if r == 0 else lax.ppermute(array, "tm", plan.pairs(r)))
+        return found
 
     sends = call(
         pack_blocks,
         [(plan.nz * plan.stride(r), ny) for r in plan.rounds],
         (right_side.reshape(parts * half_z * nx, ny),),
-        rounds=plan.rounds,
-    )
-    blocks = turned(sends)
+        extra=plan.rounds,
+    )
+    blocks = turned(sends, plan.rounds)
     blocks = lax.optimization_barrier(blocks)
     x_even, x_odd = call(edge_rows, [(GHOST * half_x, ny)] * 2, blocks)
     even = lax.ppermute(x_even, "tm", plan.x_pairs(0))
@@ -485,15 +577,23 @@
         (field, even, odd, *direct, *raws),
         scratch=[pltpu.VMEM((half_x * TILE, ny), jnp.float32)],
     )
-    z_in = [lax.ppermute(send, FLAT, plan.z_pairs(first)) for first, send in enumerate(z_sends)]
-    solved = run_sweeps(plan, place, coefs, field, ghost, z_in)
-    back = [block.reshape(plan.nz, plan.rows, ny) for block in turned(solved)]
+
+    def z_of():
+        return [lax.ppermute(send, FLAT, plan.z_pairs(first)) for first, send in enumerate(z_sends)]
+
+    solved = run_sweeps(plan, call, coefs, field, ghost, z_of)
+    back = []
+    for found, blocks in zip(solved, plan.back):
+        back = turned(found, [r for r, piece in blocks], plan.ties, back)
+    back = [
+        block.reshape(plan.layers(piece), plan.rows, ny) for block, (r, piece) in zip(back, sum(plan.back, []))
+    ]
     out = call(
         place_blocks,
         (parts, half_z, nx, ny),
         back,
-        scratch=[pltpu.SemaphoreType.DMA((steps,))],
-        out_space=pl.ANY,
+        scratch=[pltpu.SemaphoreType.DMA((len(back),))],
+        out_space=pltpu.HBM,
     )
     return out[None]
 

time: 71.2 us -> 69.9 us (0.982)
  waiting for transfers between devices: 37.7 us -> 27.9 us
  starting transfers between devices: 21.9 us -> 29.2 us
  Pallas kernels: 9.96 us -> 10.9 us
    ppermute x15 -> x19, waiting for transfers between devices: 36.5 us -> 26.7 us  [the longest x18 26.7 us: turned(): found.append(array if r == 0 else lax.ppermute(array, 'tm', plan.pairs(r)))]
    ppermute x15 -> x19, starting transfers between devices: 17.3 us -> 24.5 us  [the longest x18 24.5 us: turned(): found.append(array if r == 0 else lax.ppermute(array, 'tm', plan.pairs(r)))]
    pallas_call x7 -> x8, Pallas kernels: 9.96 us -> 10.9 us  [kernel_call(): pl.pallas_call(body, out_shape=[jax.ShapeDtypeStruct(s, jnp.float32) for...]
  transfers between devices with their start and end apart: 17 -> 21, of which waited for: 12 -> 9; matrix products, arithmetic and copies ran while one was open for 0% -> 0% of each run, Pallas kernels for 2% -> 10%
where the time goes in v5:
time: 69.9 us; the launch traced here: 69.4 us
  starting transfers between devices  29.2 us (42%)
  waiting for transfers between devices  27.9 us (40%)
  Pallas kernels  10.9 us (16%)
  local copies, waits for them, and re-layouts  1.34 us (2%)
    ppermute x18, waiting for transfers between devices, turned(): found.append(array if r == 0 else lax.ppermute(array, 'tm', plan.pairs(r)))  26.7 us
    ppermute x18, starting transfers between devices, turned(): found.append(array if r == 0 else lax.ppermute(array, 'tm', plan.pairs(r)))  24.5 us
    pallas_call x8, Pallas kernels, kernel_call(): pl.pallas_call(body, out_shape=[jax.ShapeDtypeStruct(s, jnp.float32) for...  10.9 us
    ppermute x1, starting transfers between devices, local(): odd = lax.ppermute(x_odd, 'tm', plan.x_pairs(1))  4.54 us
  transfers between devices with their start and end apart: 21, of which 9 were waited for; matrix products, arithmetic and copies ran while one was open for 0% of the time, Pallas kernels for 10%

profile of v5, /device:TPU:8, one launch (start us, length us, event | category | flops | bytes accessed | tf_op | source)
XLA Modules:
  0.0 69.4 jit_solution(131173066603725986)
XLA Ops:
  0.1 1.3 %copy-done.1 = f32[1,2,16,64,128]{4,3,2,1,0:T(8,128)S(1)} copy-done((f32[1,2,16,64,128]{4,3,2,1,0:T(8,128)S(1)}, f32[1,2,16,64,128]{4,3,2,1,0:T(8,128)}, u32[]{:S(2)}) %copy-start.1) | copy-done | bytes 1048600
  2.1 2.7 %collective-permute-start = (f32[256,128]{1,0:T(8,128)S(1)}, f32[256,128]{1,0:T(8,128)S(1)}, u32[]{:S(2)}, u32[]{:S(2)}) collective-permute-start(f32[256,128]{1,0:T(8,128)S(1)} %get-tuple-element.59), channel_id=1, source_target_pairs={{0,8},{2,10},{4,12},{6,14},{8,0},{10,2},{12,4},{14,6},{1,9},{3,11}... | collective-permute-start | bytes 393224 | tf_op jit(solution)/shard_map/ppermute | solution.py:552
  4.8 1.3 %collective-permute-start.4 = (f32[256,128]{1,0:T(8,128)S(1)}, f32[256,128]{1,0:T(8,128)S(1)}, u32[]{:S(2)}, u32[]{:S(2)}) collective-permute-start(f32[256,128]{1,0:T(8,128)S(1)} %get-tuple-element.63), channel_id=1, source_target_pairs={{0,10},{2,8},{4,14},{6,12},{8,2},{10,0},{12,6},{14,4},{1,11},{3,9}... | collective-permute-start | bytes 393224 | tf_op jit(solution)/shard_map/ppermute | solution.py:552
  6.5 1.5 %collective-permute-start.2 = (f32[384,128]{1,0:T(8,128)S(1)}, f32[384,128]{1,0:T(8,128)S(1)}, u32[]{:S(2)}, u32[]{:S(2)}) collective-permute-start(f32[384,128]{1,0:T(8,128)S(1)} %get-tuple-element.61), channel_id=1, source_target_pairs={{0,6},{2,4},{4,2},{6,0},{8,14},{10,12},{12,10},{14,8},{1,7},{3,5},... | collective-permute-start | bytes 589832 | tf_op jit(solution)/shard_map/ppermute | solution.py:552
  8.1 1.5 %collective-permute-start.3 = (f32[384,128]{1,0:T(8,128)S(1)}, f32[384,128]{1,0:T(8,128)S(1)}, u32[]{:S(2)}, u32[]{:S(2)}) collective-permute-start(f32[384,128]{1,0:T(8,128)S(1)} %get-tuple-element.62), channel_id=1, source_target_pairs={{0,2},{2,0},{4,6},{6,4},{8,10},{10,8},{12,14},{14,12},{1,3},{3,1},... | collective-permute-start | bytes 589832 | tf_op jit(solution)/shard_map/ppermute | solution.py:552
  9.6 3.6 %collective-permute-done.refs_0_ = f32[256,128]{1,0:T(8,128)S(1)} collective-permute-done((f32[256,128]{1,0:T(8,128)S(1)}, f32[256,128]{1,0:T(8,128)S(1)}, u32[]{:S(2)}, u32[]{:S(2)}) %collective-permute-start) | collective-permute-done | bytes 131104 | tf_op jit(solution)/shard_map/ppermute | solution.py:552
  13.2 2.9 %collective-permute-done.4.refs_4_ = f32[256,128]{1,0:T(8,128)S(1)} collective-permute-done((f32[256,128]{1,0:T(8,128)S(1)}, f32[256,128]{1,0:T(8,128)S(1)}, u32[]{:S(2)}, u32[]{:S(2)}) %collective-permute-start.4) | collective-permute-done | bytes 131104 | tf_op jit(solution)/shard_map/ppermute | solution.py:552
  16.3 3.5 %collective-permute-done.5.refs_5_ = f32[256,128]{1,0:T(8,128)S(1)} collective-permute-done((f32[256,128]{1,0:T(8,128)S(1)}, f32[256,128]{1,0:T(8,128)S(1)}, u32[]{:S(2)}, u32[]{:S(2)}) %collective-permute-start.5) | collective-permute-done | bytes 131104 | tf_op jit(solution)/shard_map/ppermute | solution.py:552
  19.8 8.2 %collective-permute-done.6.refs_6_ = f32[256,128]{1,0:T(8,128)S(1)} collective-permute-done((f32[256,128]{1,0:T(8,128)S(1)}, f32[256,128]{1,0:T(8,128)S(1)}, u32[]{:S(2)}, u32[]{:S(2)}) %collective-permute-start.6) | collective-permute-done | bytes 131104 | tf_op jit(solution)/shard_map/ppermute | solution.py:552
  28.7 4.5 %collective-permute-start.8 = (f32[192,128]{1,0:T(8,128)S(1)}, f32[192,128]{1,0:T(8,128)S(1)}, u32[]{:S(2)}, u32[]{:S(2)}) collective-permute-start(f32[192,128]{1,0:T(8,128)S(1)} %get-tuple-element.87), channel_id=1, source_target_pairs={{4,8},{8,4},{6,10},{10,6},{5,9},{9,5},{7,11},{11,7},{20,24},{24,20... | collective-permute-start | bytes 294920 | tf_op jit(solution)/shard_map/ppermute | solution.py:565
  33.3 1.1 %shard_map.38 = (f32[4752,128]{1,0:T(8,128)S(1)}, f32[288,128]{1,0:T(8,128)S(1)}) custom-call(s32[2]{0:T(128)S(1)} %pad_add_fusion.place_ref, f32[1024,128]{1,0:T(8,128)S(1)} %bitcast.20, f32[3072,128]{1,0:T(8,128)S(1)} %bitcast.18), custom_call_target="tpu_custom_call" | custom-call | tf_op jit(solution)/shard_map/pallas_call | solution.py:112
  35.0 1.2 %collective-permute-done.8.odd_ref = f32[192,128]{1,0:T(8,128)S(1)} collective-permute-done((f32[192,128]{1,0:T(8,128)S(1)}, f32[192,128]{1,0:T(8,128)S(1)}, u32[]{:S(2)}, u32[]{:S(2)}) %collective-permute-start.8) | collective-permute-done | bytes 98336 | tf_op jit(solution)/shard_map/ppermute | solution.py:565
  37.0 2.8 %shard_map.42 = (f32[128,128]{1,0:T(8,128)S(1)}, f32[128,128]{1,0:T(8,128)S(1)}, f32[128,128]{1,0:T(8,128)S(1)}, f32[128,128]{1,0:T(8,128)S(1)}, f32[4224,128]{1...) custom-call(s32[2]{0:T(128)S(1)} %pad_add_fusion.place_ref, ...), custom_call_target="tpu_custom_call" | custom-call | tf_op jit(solution)/shard_map/pallas_call | solution.py:112
  40.1 1.6 %collective-permute-start.9 = (f32[128,128]{1,0:T(8,128)S(1)}, f32[128,128]{1,0:T(8,128)S(1)}, u32[]{:S(2)}, u32[]{:S(2)}) collective-permute-start(f32[128,128]{1,0:T(8,128)S(1)} %get-tuple-element.90), channel_id=1, source_target_pairs={{0,12},{2,14},{4,8},{6,10},{8,4},{10,6},{12,0},{14,2},{1,13},{3,15... | collective-permute-start | bytes 196616 | tf_op jit(solution)/shard_map/ppermute | solution.py:552
  41.7 1.0 %collective-permute-start.10 = (f32[128,128]{1,0:T(8,128)S(1)}, f32[128,128]{1,0:T(8,128)S(1)}, u32[]{:S(2)}, u32[]{:S(2)}) collective-permute-start(f32[128,128]{1,0:T(8,128)S(1)} %get-tuple-element.91), channel_id=1, source_target_pairs={{0,14},{2,12},{4,10},{6,8},{8,6},{10,4},{12,2},{14,0},{1,15},{3,13... | collective-permute-start | bytes 196616 | tf_op jit(solution)/shard_map/ppermute | solution.py:552
  42.7 4.9 %collective-permute-start.11 = (f32[128,128]{1,0:T(8,128)S(1)}, f32[128,128]{1,0:T(8,128)S(1)}, u32[]{:S(2)}, u32[]{:S(2)}) collective-permute-start(f32[128,128]{1,0:T(8,128)S(1)} %get-tuple-element.92), channel_id=1, source_target_pairs={{0,8},{2,10},{4,12},{6,14},{8,0},{10,2},{12,4},{14,6},{1,9},{3,11}... | collective-permute-start | bytes 196616 | tf_op jit(solution)/shard_map/ppermute | solution.py:552
  47.5 2.6 %shard_map.43 = (f32[128,128]{1,0:T(8,128)S(1)}, f32[128,128]{1,0:T(8,128)S(1)}, f32[128,128]{1,0:T(8,128)S(1)}, f32[128,128]{1,0:T(8,128)S(1)}, f32[256,128]{1,...) custom-call(s32[2]{0:T(128)S(1)} %pad_add_fusion.place_ref, ...), custom_call_target="tpu_custom_call", output_to_operand_aliasing={{8}: (4, {}), {9}: (5, {}), {10}: (6, {}), {11}: (7, {}), {... | custom-call | tf_op jit(solution)/shard_map/pallas_call | solution.py:112
  50.1 1.8 %collective-permute-start.14 = (f32[128,128]{1,0:T(8,128)S(1)}, f32[128,128]{1,0:T(8,128)S(1)}, u32[]{:S(2)}, u32[]{:S(2)}) collective-permute-start(f32[128,128]{1,0:T(8,128)S(1)} %get-tuple-element.105), channel_id=1, source_target_pairs={{0,12},{2,14},{4,8},{6,10},{8,4},{10,6},{12,0},{14,2},{1,13},{3,15... | collective-permute-start | bytes 196616 | tf_op jit(solution)/shard_map/ppermute | solution.py:552
  53.9 2.8 %collective-permute-start.19 = (f32[256,128]{1,0:T(8,128)S(1)}, f32[256,128]{1,0:T(8,128)S(1)}, u32[]{:S(2)}, u32[]{:S(2)}) collective-permute-start(f32[256,128]{1,0:T(8,128)S(1)} %get-tuple-element.110), channel_id=1, source_target_pairs={{0,6},{2,4},{4,2},{6,0},{8,14},{10,12},{12,10},{14,8},{1,7},{3,5},... | collective-permute-start | bytes 393224 | tf_op jit(solution)/shard_map/ppermute | solution.py:552
  56.7 2.0 %collective-permute-start.18 = (f32[256,128]{1,0:T(8,128)S(1)}, f32[256,128]{1,0:T(8,128)S(1)}, u32[]{:S(2)}, u32[]{:S(2)}) collective-permute-start(f32[256,128]{1,0:T(8,128)S(1)} %get-tuple-element.109), channel_id=1, source_target_pairs={{0,4},{2,6},{4,0},{6,2},{8,12},{10,14},{12,8},{14,10},{1,5},{3,7},... | collective-permute-start | bytes 393224 | tf_op jit(solution)/shard_map/ppermute | solution.py:552
  58.7 3.0 %collective-permute-done.15 = f32[128,128]{1,0:T(8,128)S(1)} collective-permute-done((f32[128,128]{1,0:T(8,128)S(1)}, f32[128,128]{1,0:T(8,128)S(1)}, u32[]{:S(2)}, u32[]{:S(2)}) %collective-permute-start.15) | collective-permute-done | bytes 65568 | tf_op jit(solution)/shard_map/ppermute | solution.py:552
  62.5 1.6 %collective-permute-done.16 = f32[128,128]{1,0:T(8,128)S(1)} collective-permute-done((f32[128,128]{1,0:T(8,128)S(1)}, f32[128,128]{1,0:T(8,128)S(1)}, u32[]{:S(2)}, u32[]{:S(2)}) %collective-permute-start.16) | collective-permute-done | bytes 65568 | tf_op jit(solution)/shard_map/ppermute | solution.py:552
  64.1 3.6 %collective-permute-done.17 = f32[128,128]{1,0:T(8,128)S(1)} collective-permute-done((f32[128,128]{1,0:T(8,128)S(1)}, f32[128,128]{1,0:T(8,128)S(1)}, u32[]{:S(2)}, u32[]{:S(2)}) %collective-permute-start.17) | collective-permute-done | bytes 65568 | tf_op jit(solution)/shard_map/ppermute | solution.py:552
  67.8 1.6 %shard_map.44 = f32[2,16,64,128]{3,2,1,0:T(8,128)} custom-call(s32[2]{0:T(128)S(1)} %pad_add_fusion.place_ref, f32[8,16,128]{2,1,0:T(8,128)S(1)} %bitcast.26, f32[8,16,128]{2,1,0:T(8,128)S(1)} %bitcast.27, f32[8,16,128]{2,1,0:T(8,128)S(1)} %bitcast.28, f32[8,16,128]{2,1,0:T(8,128)S(1)} %bitcast.25, f32[8,16,128]{2,1,0:T(8,128)S(1)} %bitcast.29, ...), custom_call_target="tpu_custom_call" | custom-call | tf_op jit(solution)/shard_map/pallas_call | solution.py:112
  (33 shorter events, 6.6 us)
Async XLA Ops:
  0.0 33.2 %copy-start = (f32[3,16,64,128]{3,2,1,0:T(8,128)S(1)}, f32[3,16,64,128]{3,2,1,0:T(8,128)}, u32[]{:S(2)}) copy-start(f32[3,16,64,128]{3,2,1,0:T(8,128)} %param.5) | copy-start | bytes 4718596
  0.1 1.3 %copy-start.1 = (f32[1,2,16,64,128]{4,3,2,1,0:T(8,128)S(1)}, f32[1,2,16,64,128]{4,3,2,1,0:T(8,128)}, u32[]{:S(2)}) copy-start(f32[1,2,16,64,128]{4,3,2,1,0:T(8,128)} %param.3) | copy-start | bytes 3145732
  1.4 31.8 %copy-start.2 = (f32[16,64,128]{2,1,0:T(8,128)S(1)}, f32[16,64,128]{2,1,0:T(8,128)}, u32[]{:S(2)}) copy-start(f32[16,64,128]{2,1,0:T(8,128)} %param.4) | copy-start | bytes 1572868
  2.1 11.1 %collective-permute-start = (f32[256,128]{1,0:T(8,128)S(1)}, f32[256,128]{1,0:T(8,128)S(1)}, u32[]{:S(2)}, u32[]{:S(2)}) collective-permute-start(f32[256,128]{1,0:T(8,128)S(1)} %get-tuple-element.59), channel_id=1, source_target_pairs={{0,8},{2,10},{4,12},{6,14},{8,0},{10,2},{12,4},{14,6},{1,9},{3,11}... | collective-permute-start | bytes 393224 | tf_op jit(solution)/shard_map/ppermute | solution.py:552
  4.8 11.3 %collective-permute-start.4 = (f32[256,128]{1,0:T(8,128)S(1)}, f32[256,128]{1,0:T(8,128)S(1)}, u32[]{:S(2)}, u32[]{:S(2)}) collective-permute-start(f32[256,128]{1,0:T(8,128)S(1)} %get-tuple-element.63), channel_id=1, source_target_pairs={{0,10},{2,8},{4,14},{6,12},{8,2},{10,0},{12,6},{14,4},{1,11},{3,9}... | collective-permute-start | bytes 393224 | tf_op jit(solution)/shard_map/ppermute | solution.py:552
  6.1 21.9 %collective-permute-start.1 = (f32[384,128]{1,0:T(8,128)S(1)}, f32[384,128]{1,0:T(8,128)S(1)}, u32[]{:S(2)}, u32[]{:S(2)}) collective-permute-start(f32[384,128]{1,0:T(8,128)S(1)} %get-tuple-element.60), channel_id=1, source_target_pairs={{0,4},{2,6},{4,0},{6,2},{8,12},{10,14},{12,8},{14,10},{1,5},{3,7},... | collective-permute-start | bytes 589832 | tf_op jit(solution)/shard_map/ppermute | solution.py:552
  6.5 21.4 %collective-permute-start.2 = (f32[384,128]{1,0:T(8,128)S(1)}, f32[384,128]{1,0:T(8,128)S(1)}, u32[]{:S(2)}, u32[]{:S(2)}) collective-permute-start(f32[384,128]{1,0:T(8,128)S(1)} %get-tuple-element.61), channel_id=1, source_target_pairs={{0,6},{2,4},{4,2},{6,0},{8,14},{10,12},{12,10},{14,8},{1,7},{3,5},... | collective-permute-start | bytes 589832 | tf_op jit(solution)/shard_map/ppermute | solution.py:552
  8.1 19.9 %collective-permute-start.3 = (f32[384,128]{1,0:T(8,128)S(1)}, f32[384,128]{1,0:T(8,128)S(1)}, u32[]{:S(2)}, u32[]{:S(2)}) collective-permute-start(f32[384,128]{1,0:T(8,128)S(1)} %get-tuple-element.62), channel_id=1, source_target_pairs={{0,2},{2,0},{4,6},{6,4},{8,10},{10,8},{12,14},{14,12},{1,3},{3,1},... | collective-permute-start | bytes 589832 | tf_op jit(solution)/shard_map/ppermute | solution.py:552
  13.2 6.6 %collective-permute-start.5 = (f32[256,128]{1,0:T(8,128)S(1)}, f32[256,128]{1,0:T(8,128)S(1)}, u32[]{:S(2)}, u32[]{:S(2)}) collective-permute-start(f32[256,128]{1,0:T(8,128)S(1)} %get-tuple-element.64), channel_id=1, source_target_pairs={{0,12},{2,14},{4,8},{6,10},{8,4},{10,6},{12,0},{14,2},{1,13},{3,15... | collective-permute-start | bytes 393224 | tf_op jit(solution)/shard_map/ppermute | solution.py:552
  16.0 11.9 %collective-permute-start.6 = (f32[256,128]{1,0:T(8,128)S(1)}, f32[256,128]{1,0:T(8,128)S(1)}, u32[]{:S(2)}, u32[]{:S(2)}) collective-permute-start(f32[256,128]{1,0:T(8,128)S(1)} %get-tuple-element.65), channel_id=1, source_target_pairs={{0,14},{2,12},{4,10},{6,8},{8,6},{10,4},{12,2},{14,0},{1,15},{3,13... | collective-permute-start | bytes 393224 | tf_op jit(solution)/shard_map/ppermute | solution.py:552
  28.6 6.4 %collective-permute-start.7 = (f32[192,128]{1,0:T(8,128)S(1)}, f32[192,128]{1,0:T(8,128)S(1)}, u32[]{:S(2)}, u32[]{:S(2)}) collective-permute-start(f32[192,128]{1,0:T(8,128)S(1)} %get-tuple-element.86), channel_id=1, source_target_pairs={{0,4},{4,0},{2,6},{6,2},{8,12},{12,8},{10,14},{14,10},{1,5},{5,1},... | collective-permute-start | bytes 294920 | tf_op jit(solution)/shard_map/ppermute | solution.py:564
  28.7 7.5 %collective-permute-start.8 = (f32[192,128]{1,0:T(8,128)S(1)}, f32[192,128]{1,0:T(8,128)S(1)}, u32[]{:S(2)}, u32[]{:S(2)}) collective-permute-start(f32[192,128]{1,0:T(8,128)S(1)} %get-tuple-element.87), channel_id=1, source_target_pairs={{4,8},{8,4},{6,10},{10,6},{5,9},{9,5},{7,11},{11,7},{20,24},{24,20... | collective-permute-start | bytes 294920 | tf_op jit(solution)/shard_map/ppermute | solution.py:565
  37.0 10.6 %collective-permute-start.12 = (f32[800,128]{1,0:T(8,128)S(1)}, f32[800,128]{1,0:T(8,128)S(1)}, u32[]{:S(2)}, u32[]{:S(2)}) collective-permute-start(f32[800,128]{1,0:T(8,128)S(1)} %get-tuple-element.93), channel_id=1, source_target_pairs={{0,1},{1,0},{2,3},{3,2},{4,5},{5,4},{6,7},{7,6},{8,9},{9,8},{10,11... | collective-permute-start | bytes 1228808 | tf_op jit(solution)/shard_map/ppermute | solution.py:582
  39.8 10.3 %collective-permute-start.13 = (f32[128,128]{1,0:T(8,128)S(1)}, f32[128,128]{1,0:T(8,128)S(1)}, u32[]{:S(2)}, u32[]{:S(2)}) collective-permute-start(f32[128,128]{1,0:T(8,128)S(1)} %get-tuple-element.101), channel_id=1, source_target_pairs={{0,10},{2,8},{4,14},{6,12},{8,2},{10,0},{12,6},{14,4},{1,11},{3,9}... | collective-permute-start | bytes 196616 | tf_op jit(solution)/shard_map/ppermute | solution.py:552
  40.1 12.8 %collective-permute-start.9 = (f32[128,128]{1,0:T(8,128)S(1)}, f32[128,128]{1,0:T(8,128)S(1)}, u32[]{:S(2)}, u32[]{:S(2)}) collective-permute-start(f32[128,128]{1,0:T(8,128)S(1)} %get-tuple-element.90), channel_id=1, source_target_pairs={{0,12},{2,14},{4,8},{6,10},{8,4},{10,6},{12,0},{14,2},{1,13},{3,15... | collective-permute-start | bytes 196616 | tf_op jit(solution)/shard_map/ppermute | solution.py:552
  41.7 12.2 %collective-permute-start.10 = (f32[128,128]{1,0:T(8,128)S(1)}, f32[128,128]{1,0:T(8,128)S(1)}, u32[]{:S(2)}, u32[]{:S(2)}) collective-permute-start(f32[128,128]{1,0:T(8,128)S(1)} %get-tuple-element.91), channel_id=1, source_target_pairs={{0,14},{2,12},{4,10},{6,8},{8,6},{10,4},{12,2},{14,0},{1,15},{3,13... | collective-permute-start | bytes 196616 | tf_op jit(solution)/shard_map/ppermute | solution.py:552
  42.7 14.0 %collective-permute-start.11 = (f32[128,128]{1,0:T(8,128)S(1)}, f32[128,128]{1,0:T(8,128)S(1)}, u32[]{:S(2)}, u32[]{:S(2)}) collective-permute-start(f32[128,128]{1,0:T(8,128)S(1)} %get-tuple-element.92), channel_id=1, source_target_pairs={{0,8},{2,10},{4,12},{6,14},{8,0},{10,2},{12,4},{14,6},{1,9},{3,11}... | collective-permute-start | bytes 196616 | tf_op jit(solution)/shard_map/ppermute | solution.py:552
  50.1 8.5 %collective-permute-start.14 = (f32[128,128]{1,0:T(8,128)S(1)}, f32[128,128]{1,0:T(8,128)S(1)}, u32[]{:S(2)}, u32[]{:S(2)}) collective-permute-start(f32[128,128]{1,0:T(8,128)S(1)} %get-tuple-element.105), channel_id=1, source_target_pairs={{0,12},{2,14},{4,8},{6,10},{8,4},{10,6},{12,0},{14,2},{1,13},{3,15... | collective-permute-start | bytes 196616 | tf_op jit(solution)/shard_map/ppermute | solution.py:552
  51.9 9.8 %collective-permute-start.15 = (f32[128,128]{1,0:T(8,128)S(1)}, f32[128,128]{1,0:T(8,128)S(1)}, u32[]{:S(2)}, u32[]{:S(2)}) collective-permute-start(f32[128,128]{1,0:T(8,128)S(1)} %get-tuple-element.106), channel_id=1, source_target_pairs={{0,14},{2,12},{4,10},{6,8},{8,6},{10,4},{12,2},{14,0},{1,15},{3,13... | collective-permute-start | bytes 196616 | tf_op jit(solution)/shard_map/ppermute | solution.py:552
  52.9 14.9 %collective-permute-start.20 = (f32[256,128]{1,0:T(8,128)S(1)}, f32[256,128]{1,0:T(8,128)S(1)}, u32[]{:S(2)}, u32[]{:S(2)}) collective-permute-start(f32[256,128]{1,0:T(8,128)S(1)} %get-tuple-element.111), channel_id=1, source_target_pairs={{0,2},{2,0},{4,6},{6,4},{8,10},{10,8},{12,14},{14,12},{1,3},{3,1},... | collective-permute-start | bytes 393224 | tf_op jit(solution)/shard_map/ppermute | solution.py:552
  53.9 13.9 %collective-permute-start.19 = (f32[256,128]{1,0:T(8,128)S(1)}, f32[256,128]{1,0:T(8,128)S(1)}, u32[]{:S(2)}, u32[]{:S(2)}) collective-permute-start(f32[256,128]{1,0:T(8,128)S(1)} %get-tuple-element.110), channel_id=1, source_target_pairs={{0,6},{2,4},{4,2},{6,0},{8,14},{10,12},{12,10},{14,8},{1,7},{3,5},... | collective-permute-start | bytes 393224 | tf_op jit(solution)/shard_map/ppermute | solution.py:552
  56.7 11.1 %collective-permute-start.18 = (f32[256,128]{1,0:T(8,128)S(1)}, f32[256,128]{1,0:T(8,128)S(1)}, u32[]{:S(2)}, u32[]{:S(2)}) collective-permute-start(f32[256,128]{1,0:T(8,128)S(1)} %get-tuple-element.109), channel_id=1, source_target_pairs={{0,4},{2,6},{4,0},{6,2},{8,12},{10,14},{12,8},{14,10},{1,5},{3,7},... | collective-permute-start | bytes 393224 | tf_op jit(solution)/shard_map/ppermute | solution.py:552
  58.7 5.5 %collective-permute-start.16 = (f32[128,128]{1,0:T(8,128)S(1)}, f32[128,128]{1,0:T(8,128)S(1)}, u32[]{:S(2)}, u32[]{:S(2)}) collective-permute-start(f32[128,128]{1,0:T(8,128)S(1)} %get-tuple-element.107), channel_id=1, source_target_pairs={{0,8},{2,10},{4,12},{6,14},{8,0},{10,2},{12,4},{14,6},{1,9},{3,11}... | collective-permute-start | bytes 196616 | tf_op jit(solution)/shard_map/ppermute | solution.py:552
  61.7 6.1 %collective-permute-start.17 = (f32[128,128]{1,0:T(8,128)S(1)}, f32[128,128]{1,0:T(8,128)S(1)}, u32[]{:S(2)}, u32[]{:S(2)}) collective-permute-start(f32[128,128]{1,0:T(8,128)S(1)} %get-tuple-element.108), channel_id=1, source_target_pairs={{0,10},{2,8},{4,14},{6,12},{8,2},{10,0},{12,6},{14,4},{1,11},{3,9}... | collective-permute-start | bytes 196616 | tf_op jit(solution)/shard_map/ppermute | solution.py:552

commit v6 on v5

--- a/solution.py
+++ b/solution.py
@@ -35,6 +35,7 @@
         self.sides = 1 if self.z_parts == 2 else 2
         self.z_tiles = GHOST * self.main + GHOST - 1
         self.raw_tiles = GHOST * self.tiles * RAW
+        self.ghost_inputs = 2 + steps // 2 + self.sides
         kinds = [(2, 0), (1, 0), (1, 1), (0, 1), (2, 1), (3, 0), (3, 1), (0, 0)]
         self.rounds = [a * self.per_quarter + m * 2 + c for m in range(self.in_half) for a, c in kinds]
 
@@ -236,18 +237,29 @@
                 x_even[at, :] = jnp.where(place.hi_odd, low, high)
 
 
-def gather_steps(plan, place_ref, *refs):
-    place = Place(plan, place_ref)
-    blocks, field = refs[: plan.steps], refs[plan.steps]
+def first_own(plan, place_ref, coefs, *refs):
+    place = Place(plan, place_ref)
+    blocks, (source, ping, field) = refs[: plan.steps], refs[plan.steps :]
     size = plan.nz * plan.rows
     for block, r in zip(blocks, plan.rounds):
         at = (place.t ^ r) * size
         for z in range(plan.nz):
             to = pl.ds(pl.multiple_of(at + z * plan.rows, TILE), plan.rows)
             field[to, :] = block[pl.ds(z * plan.stride(r), plan.rows), :]
-
-
-def gather_ghosts(plan, place_ref, field, even_ref, odd_ref, *refs):
+    work = Sweeps(plan, place, coefs, source, ping, None, None)
+
+    def several(i, _):
+        for n in range(4):
+            z = i * 4 + n
+            for k in range(plan.main):
+                tiles = [field[rows_at((t * plan.nz + z) * plan.main + k), :] for t in range(plan.steps)]
+                work.first(z + GHOST, k, tiles)
+        return 0
+
+    lax.fori_loop(0, plan.nz // 4, several, 0)
+
+
+def gather_ghosts(plan, place_ref, source, even_ref, odd_ref, *refs):
     place = Place(plan, place_ref)
     direct = [r for r in plan.rounds if plan.direct(r)]
     blocks, refs = refs[: len(direct)], refs[len(direct) :]
@@ -273,9 +285,10 @@
         up = jnp.logical_not(place.zb_odd) if side == 0 else place.zb_odd
         for t in range(plan.steps):
             for n in range(GHOST):
-                z = t * plan.nz + jnp.where(up, plan.nz - GHOST + n, n)
+                e = GHOST + jnp.where(up, plan.nz - GHOST + n, n)
                 for k in range(plan.main):
-                    z_send[rows_at(t * tiles + n * plan.main + k), :] = field[rows_at(z * plan.main + k), :]
+                    to = rows_at(t * tiles + n * plan.main + k)
+                    z_send[to, :] = source[rows_at((e * plan.tiles + k) * plan.steps + t), :]
             for n in range(deep):
                 z = t * plan.nz + jnp.where(up, plan.nz - deep + n, n)
                 z_send[rows_at(t * tiles + GHOST * plan.main + n), :] = ghost[rows_at(z), :]
@@ -295,11 +308,11 @@
     def coef(self, e, k, n):
         return self.coefs[rows_at((e * self.plan.tiles + k) * COEFS + n), :]
 
-    def first(self, e, k, values):
+    def first(self, e, k, values, scaled=False):
         w, c, wrap = (self.coef(e, k, n) for n in range(3))
         partial = []
         for t, value in enumerate(values):
-            value = w * value
+            value = value if scaled else w * value
             self.source[self.spot(e, k, t), :] = value
             if t:
                 value = value + c * partial[-1]
@@ -370,13 +383,9 @@
             lax.fori_loop(start, stop, one, 0)
 
 
-def first_pass(plan, work, field, ghost, start, count):
-    steps, main = plan.steps, plan.main
-
+def first_pass(plan, work, ghost, start, count):
     def layer(z):
-        for k in range(main):
-            work.first(z + GHOST, k, [field[rows_at((t * plan.nz + z) * main + k), :] for t in range(steps)])
-        work.first(z + GHOST, main, [ghost[rows_at(t * plan.nz + z), :] for t in range(steps)])
+        work.first(z + GHOST, plan.main, [ghost[rows_at(t * plan.nz + z), :] for t in range(plan.steps)])
 
     def several(i, _):
         for n in range(4):
@@ -405,7 +414,7 @@
                 write_coefs(plan, place.hi, None, k, [z_ref[rows_at(raw + m), :] for m in range(RAW)], store)
             for k in range(main):
                 tile = n * main + k
-                work.first(e, k, [z_ref[rows_at(t * plan.z_tiles + tile), :] for t in range(steps)])
+                work.first(e, k, [z_ref[rows_at(t * plan.z_tiles + tile), :] for t in range(steps)], True)
             c_at = n if upper else n - (GHOST - deep)
             if 0 <= c_at < deep:
                 tile = GHOST * main + c_at
@@ -445,12 +454,12 @@
         out[...] = last[pl.ds(pl.multiple_of(at, TILE), out.shape[0]), :]
 
 
-def all_sweeps(plan, place_ref, coefs_in, field, ghost, *refs):
+def all_sweeps(plan, place_ref, coefs_in, source_in, ping_in, ghost, *refs):
     place = Place(plan, place_ref)
     z_in, refs = refs[: plan.sides], refs[plan.sides :]
     outs, (coefs, source, ping, pong, last) = refs[:-5], refs[-5:]
     work = Sweeps(plan, place, coefs, source, ping, pong, last)
-    first_pass(plan, work, field, ghost, 0, plan.nz)
+    first_pass(plan, work, ghost, 0, plan.nz)
     ghost_pass(plan, place, work, z_in)
     no_ghosts(plan, work)
     for number in range(1, SWEEPS):
@@ -461,12 +470,14 @@
     write_piece(plan, place, last, outs, 0)
 
 
-def far_sweeps(plan, place_ref, coefs, field, ghost, *refs):
-    place = Place(plan, place_ref)
-    outs, (source, ping, pong, last) = refs[:-4], refs[-4:]
+def far_sweeps(plan, place_ref, coefs, source_in, ping_in, *refs):
+    place = Place(plan, place_ref)
+    given, refs = refs[: plan.ghost_inputs], refs[plan.ghost_inputs :]
+    outs, (source, ping, pong, last, ghost, z_send, planes) = refs[:-7], refs[-7:]
+    gather_ghosts(plan, place_ref, source, *given, ghost, z_send, planes)
     work = Sweeps(plan, place, coefs, source, ping, pong, last)
     count = plan.pieces()[0]
-    first_pass(plan, work, field, ghost, jnp.where(place.up, 0, plan.nz - count - GHOST), count + GHOST)
+    first_pass(plan, work, ghost, jnp.where(place.up, 0, plan.nz - count - GHOST), count + GHOST)
     no_ghosts(plan, work)
     for number in range(1, SWEEPS):
         total = count + SWEEPS - 1 - number
@@ -475,13 +486,13 @@
     write_piece(plan, place, last, outs, 0)
 
 
-def near_sweeps(plan, place_ref, field, ghost, z_in, coefs_in, source_in, ping_in, pong_in, last_in, *refs):
+def near_sweeps(plan, place_ref, ghost, z_in, coefs_in, source_in, ping_in, pong_in, last_in, *refs):
     place = Place(plan, place_ref)
     outs, (coefs, source, ping, pong, last) = refs[:-5], refs[-5:]
     work = Sweeps(plan, place, coefs, source, ping, pong, last)
     first, count = plan.pieces()
     left = plan.nz - first - GHOST
-    first_pass(plan, work, field, ghost, jnp.where(place.up, plan.nz - left, 0), left)
+    first_pass(plan, work, ghost, jnp.where(place.up, plan.nz - left, 0), left)
     ghost_pass(plan, place, work, [z_in])
     for number in range(1, SWEEPS):
         reach = SWEEPS - 1 - number
@@ -490,25 +501,44 @@
     write_piece(plan, place, last, outs, 1)
 
 
-def run_sweeps(plan, call, coefs, field, ghost, z_of):
-    grid = (plan.ext * plan.tiles * plan.steps * TILE, plan.ny)
-    whole = (plan.steps * plan.nz * plan.rows, plan.ny)
-    shapes = [[(plan.layers(piece) * plan.rows, plan.ny) for r, piece in blocks] for blocks in plan.back]
+def run_sweeps(plan, call, coefs, source, ping, ghost_inputs):
+    steps, ny = plan.steps, plan.ny
+    grid = (plan.ext * plan.tiles * steps * TILE, ny)
+    whole = (steps * plan.nz * plan.rows, ny)
+    ghost = (steps * plan.nz * TILE, ny)
+    z_send = ((steps * plan.z_tiles + plan.raw_tiles) * TILE, ny)
+    planes = pltpu.VMEM((steps // 2 * plan.nz * TILE, ny), jnp.float32)
+    shapes = [[(plan.layers(piece) * plan.rows, ny) for r, piece in blocks] for blocks in plan.back]
+
+    def along_z(sends):
+        return [lax.ppermute(send, FLAT, plan.z_pairs(first)) for first, send in enumerate(sends)]
+
     if len(shapes) == 1:
-        scratch = [pltpu.VMEM(shape, jnp.float32) for shape in [grid] * 3 + [whole]]
-        inputs = (coefs, field, ghost, *z_of())
+        ghost, *z_sends = call(
+            gather_ghosts, [ghost] + [z_send] * plan.sides, (source, *ghost_inputs), scratch=[planes]
+        )
         found = call(
-            all_sweeps, shapes[0] + [coefs.shape], inputs, scratch=scratch, aliases={1: len(shapes[0])}, limit=24
+            all_sweeps,
+            shapes[0] + [coefs.shape, grid, grid],
+            (coefs, source, ping, ghost, *along_z(z_sends)),
+            scratch=[pltpu.VMEM(shape, jnp.float32) for shape in (grid, whole)],
+            aliases={1 + n: len(shapes[0]) + n for n in range(3)},
+            limit=24,
         )
-        return [found[:-1]]
-    *done, source, ping, pong, last = call(
-        far_sweeps, shapes[0] + [grid] * 3 + [whole], (coefs, field, ghost), limit=24
+        return [found[:-3]]
+    *done, source, ping, pong, last, ghost, z_send = call(
+        far_sweeps,
+        shapes[0] + [grid] * 3 + [whole, ghost, z_send],
+        (coefs, source, ping, *ghost_inputs),
+        scratch=[planes],
+        aliases={2 + n: len(shapes[0]) + n for n in range(2)},
+        limit=24,
     )
     rest = call(
         near_sweeps,
         shapes[1] + [coefs.shape] + [grid] * 3 + [whole],
-        (field, ghost, *z_of(), coefs, source, ping, pong, last),
-        aliases={4 + n: len(shapes[1]) + n for n in range(5)},
+        (ghost, *along_z([z_send]), coefs, source, ping, pong, last),
+        aliases={3 + n: len(shapes[1]) + n for n in range(5)},
         limit=24,
     )
     return [done, rest[:-5]]
@@ -564,24 +594,17 @@
     even = lax.ppermute(x_even, "tm", plan.x_pairs(0))
     odd = lax.ppermute(x_odd, "tm", plan.x_pairs(1))
     diffusivity, velocity, *blocks = lax.optimization_barrier((diffusivity, velocity, *blocks))
-    field = call(gather_steps, (steps * size, ny), blocks)
     coefs, *raws = call(
         make_coefs,
         [(plan.ext * plan.tiles * COEFS * TILE, ny)] + [(plan.raw_tiles * TILE, ny)] * plan.sides,
         (diffusivity.reshape(half_z * nx, ny), velocity.reshape(3 * half_z * nx, ny)),
     )
     direct = [block for block, r in zip(blocks, plan.rounds) if plan.direct(r)]
-    ghost, *z_sends = call(
-        gather_ghosts,
-        [(steps * plan.nz * TILE, ny)] + [((steps * plan.z_tiles + plan.raw_tiles) * TILE, ny)] * plan.sides,
-        (field, even, odd, *direct, *raws),
-        scratch=[pltpu.VMEM((half_x * TILE, ny), jnp.float32)],
-    )
-
-    def z_of():
-        return [lax.ppermute(send, FLAT, plan.z_pairs(first)) for first, send in enumerate(z_sends)]
-
-    solved = run_sweeps(plan, call, coefs, field, ghost, z_of)
+    grid = (plan.ext * plan.tiles * steps * TILE, ny)
+    source, ping = call(
+        first_own, [grid, grid], (coefs, *blocks), scratch=[pltpu.VMEM((steps * size, ny), jnp.float32)]
+    )
+    solved = run_sweeps(plan, call, coefs, source, ping, (even, odd, *direct, *raws))
     back = []
     for found, blocks in zip(solved, plan.back):
         back = turned(found, [r for r, piece in blocks], plan.ties, back)

time: 69.9 us -> 69.1 us (0.989)
    pallas_call x8 -> x7, Pallas kernels: 10.9 us -> 10.3 us  [kernel_call(): pl.pallas_call(body, out_shape=[jax.ShapeDtypeStruct(s, jnp.float32) for...]
  transfers between devices with their start and end apart: 21 -> 21, of which waited for: 9 -> 9; matrix products, arithmetic and copies ran while one was open for 0% -> 0% of each run, Pallas kernels for 10% -> 7%
where the time goes in v6:
time: 69.1 us; the launch traced here: 68.7 us
  starting transfers between devices  29.2 us (42%)
  waiting for transfers between devices  27.6 us (40%)
  Pallas kernels  10.3 us (15%)
  local copies, waits for them, and re-layouts  1.34 us (2%)
    ppermute x18, waiting for transfers between devices, turned(): found.append(array if r == 0 else lax.ppermute(array, 'tm', plan.pairs(r)))  26.7 us
    ppermute x18, starting transfers between devices, turned(): found.append(array if r == 0 else lax.ppermute(array, 'tm', plan.pairs(r)))  24.5 us
    pallas_call x7, Pallas kernels, kernel_call(): pl.pallas_call(body, out_shape=[jax.ShapeDtypeStruct(s, jnp.float32) for...  10.3 us
    ppermute x1, starting transfers between devices, local(): odd = lax.ppermute(x_odd, 'tm', plan.x_pairs(1))  4.54 us
  transfers between devices with their start and end apart: 21, of which 9 were waited for; matrix products, arithmetic and copies ran while one was open for 0% of the time, Pallas kernels for 7%

profile of v6, /device:TPU:8, one launch (start us, length us, event | category | flops | bytes accessed | tf_op | source)
XLA Modules:
  0.0 68.7 jit_solution(9438967440797515501)
XLA Ops:
  0.1 1.3 %copy-done.1 = f32[1,2,16,64,128]{4,3,2,1,0:T(8,128)S(1)} copy-done((f32[1,2,16,64,128]{4,3,2,1,0:T(8,128)S(1)}, f32[1,2,16,64,128]{4,3,2,1,0:T(8,128)}, u32[]{:S(2)}) %copy-start.1) | copy-done | bytes 1048600
  2.1 2.7 %collective-permute-start = (f32[256,128]{1,0:T(8,128)S(1)}, f32[256,128]{1,0:T(8,128)S(1)}, u32[]{:S(2)}, u32[]{:S(2)}) collective-permute-start(f32[256,128]{1,0:T(8,128)S(1)} %get-tuple-element.61), channel_id=1, source_target_pairs={{0,8},{2,10},{4,12},{6,14},{8,0},{10,2},{12,4},{14,6},{1,9},{3,11}... | collective-permute-start | bytes 393224 | tf_op jit(solution)/shard_map/ppermute | solution.py:582
  4.8 1.3 %collective-permute-start.4 = (f32[256,128]{1,0:T(8,128)S(1)}, f32[256,128]{1,0:T(8,128)S(1)}, u32[]{:S(2)}, u32[]{:S(2)}) collective-permute-start(f32[256,128]{1,0:T(8,128)S(1)} %get-tuple-element.65), channel_id=1, source_target_pairs={{0,10},{2,8},{4,14},{6,12},{8,2},{10,0},{12,6},{14,4},{1,11},{3,9}... | collective-permute-start | bytes 393224 | tf_op jit(solution)/shard_map/ppermute | solution.py:582
  6.5 1.5 %collective-permute-start.2 = (f32[384,128]{1,0:T(8,128)S(1)}, f32[384,128]{1,0:T(8,128)S(1)}, u32[]{:S(2)}, u32[]{:S(2)}) collective-permute-start(f32[384,128]{1,0:T(8,128)S(1)} %get-tuple-element.63), channel_id=1, source_target_pairs={{0,6},{2,4},{4,2},{6,0},{8,14},{10,12},{12,10},{14,8},{1,7},{3,5},... | collective-permute-start | bytes 589832 | tf_op jit(solution)/shard_map/ppermute | solution.py:582
  8.1 1.5 %collective-permute-start.3 = (f32[384,128]{1,0:T(8,128)S(1)}, f32[384,128]{1,0:T(8,128)S(1)}, u32[]{:S(2)}, u32[]{:S(2)}) collective-permute-start(f32[384,128]{1,0:T(8,128)S(1)} %get-tuple-element.64), channel_id=1, source_target_pairs={{0,2},{2,0},{4,6},{6,4},{8,10},{10,8},{12,14},{14,12},{1,3},{3,1},... | collective-permute-start | bytes 589832 | tf_op jit(solution)/shard_map/ppermute | solution.py:582
  9.6 3.6 %collective-permute-done.refs_0_ = f32[256,128]{1,0:T(8,128)S(1)} collective-permute-done((f32[256,128]{1,0:T(8,128)S(1)}, f32[256,128]{1,0:T(8,128)S(1)}, u32[]{:S(2)}, u32[]{:S(2)}) %collective-permute-start) | collective-permute-done | bytes 131104 | tf_op jit(solution)/shard_map/ppermute | solution.py:582
  13.2 2.9 %collective-permute-done.4.refs_4_ = f32[256,128]{1,0:T(8,128)S(1)} collective-permute-done((f32[256,128]{1,0:T(8,128)S(1)}, f32[256,128]{1,0:T(8,128)S(1)}, u32[]{:S(2)}, u32[]{:S(2)}) %collective-permute-start.4) | collective-permute-done | bytes 131104 | tf_op jit(solution)/shard_map/ppermute | solution.py:582
  16.3 3.5 %collective-permute-done.5.refs_5_ = f32[256,128]{1,0:T(8,128)S(1)} collective-permute-done((f32[256,128]{1,0:T(8,128)S(1)}, f32[256,128]{1,0:T(8,128)S(1)}, u32[]{:S(2)}, u32[]{:S(2)}) %collective-permute-start.5) | collective-permute-done | bytes 131104 | tf_op jit(solution)/shard_map/ppermute | solution.py:582
  19.8 8.2 %collective-permute-done.6.refs_6_ = f32[256,128]{1,0:T(8,128)S(1)} collective-permute-done((f32[256,128]{1,0:T(8,128)S(1)}, f32[256,128]{1,0:T(8,128)S(1)}, u32[]{:S(2)}, u32[]{:S(2)}) %collective-permute-start.6) | collective-permute-done | bytes 131104 | tf_op jit(solution)/shard_map/ppermute | solution.py:582
  28.7 4.5 %collective-permute-start.8 = (f32[192,128]{1,0:T(8,128)S(1)}, f32[192,128]{1,0:T(8,128)S(1)}, u32[]{:S(2)}, u32[]{:S(2)}) collective-permute-start(f32[192,128]{1,0:T(8,128)S(1)} %get-tuple-element.91), channel_id=1, source_target_pairs={{4,8},{8,4},{6,10},{10,6},{5,9},{9,5},{7,11},{11,7},{20,24},{24,20... | collective-permute-start | bytes 294920 | tf_op jit(solution)/shard_map/ppermute | solution.py:595
  33.3 1.1 %shard_map.38 = (f32[4752,128]{1,0:T(8,128)S(1)}, f32[288,128]{1,0:T(8,128)S(1)}) custom-call(s32[2]{0:T(128)S(1)} %pad_add_fusion.place_ref, f32[1024,128]{1,0:T(8,128)S(1)} %bitcast.20, f32[3072,128]{1,0:T(8,128)S(1)} %bitcast.18), custom_call_target="tpu_custom_call" | custom-call | tf_op jit(solution)/shard_map/pallas_call | solution.py:113
  36.2 2.8 %shard_map.41 = (f32[128,128]{1,0:T(8,128)S(1)}, f32[128,128]{1,0:T(8,128)S(1)}, f32[128,128]{1,0:T(8,128)S(1)}, f32[128,128]{1,0:T(8,128)S(1)}, f32[4224,128]{1...) custom-call(s32[2]{0:T(128)S(1)} %pad_add_fusion.place_ref, ...), custom_call_target="tpu_custom_call", output_to_operand_aliasing={{4}: (2, {}), {5}: (3, {})} | custom-call | tf_op jit(solution)/shard_map/pallas_call | solution.py:113
  39.4 1.6 %collective-permute-start.9 = (f32[128,128]{1,0:T(8,128)S(1)}, f32[128,128]{1,0:T(8,128)S(1)}, u32[]{:S(2)}, u32[]{:S(2)}) collective-permute-start(f32[128,128]{1,0:T(8,128)S(1)} %get-tuple-element.93), channel_id=1, source_target_pairs={{0,12},{2,14},{4,8},{6,10},{8,4},{10,6},{12,0},{14,2},{1,13},{3,15... | collective-permute-start | bytes 196616 | tf_op jit(solution)/shard_map/ppermute | solution.py:582
  41.0 1.0 %collective-permute-start.10 = (f32[128,128]{1,0:T(8,128)S(1)}, f32[128,128]{1,0:T(8,128)S(1)}, u32[]{:S(2)}, u32[]{:S(2)}) collective-permute-start(f32[128,128]{1,0:T(8,128)S(1)} %get-tuple-element.94), channel_id=1, source_target_pairs={{0,14},{2,12},{4,10},{6,8},{8,6},{10,4},{12,2},{14,0},{1,15},{3,13... | collective-permute-start | bytes 196616 | tf_op jit(solution)/shard_map/ppermute | solution.py:582
  42.0 4.9 %collective-permute-start.11 = (f32[128,128]{1,0:T(8,128)S(1)}, f32[128,128]{1,0:T(8,128)S(1)}, u32[]{:S(2)}, u32[]{:S(2)}) collective-permute-start(f32[128,128]{1,0:T(8,128)S(1)} %get-tuple-element.95), channel_id=1, source_target_pairs={{0,8},{2,10},{4,12},{6,14},{8,0},{10,2},{12,4},{14,6},{1,9},{3,11}... | collective-permute-start | bytes 196616 | tf_op jit(solution)/shard_map/ppermute | solution.py:582
  46.8 2.5 %shard_map.42 = (f32[128,128]{1,0:T(8,128)S(1)}, f32[128,128]{1,0:T(8,128)S(1)}, f32[128,128]{1,0:T(8,128)S(1)}, f32[128,128]{1,0:T(8,128)S(1)}, f32[256,128]{1,...) custom-call(s32[2]{0:T(128)S(1)} %pad_add_fusion.place_ref, ...), custom_call_target="tpu_custom_call", output_to_operand_aliasing={{8}: (3, {}), {9}: (4, {}), {10}: (5, {}), {11}: (6, {}), {... | custom-call | tf_op jit(solution)/shard_map/pallas_call | solution.py:113
  49.4 1.8 %collective-permute-start.14 = (f32[128,128]{1,0:T(8,128)S(1)}, f32[128,128]{1,0:T(8,128)S(1)}, u32[]{:S(2)}, u32[]{:S(2)}) collective-permute-start(f32[128,128]{1,0:T(8,128)S(1)} %get-tuple-element.109), channel_id=1, source_target_pairs={{0,12},{2,14},{4,8},{6,10},{8,4},{10,6},{12,0},{14,2},{1,13},{3,15... | collective-permute-start | bytes 196616 | tf_op jit(solution)/shard_map/ppermute | solution.py:582
  51.2 1.0 %collective-permute-start.15 = (f32[128,128]{1,0:T(8,128)S(1)}, f32[128,128]{1,0:T(8,128)S(1)}, u32[]{:S(2)}, u32[]{:S(2)}) collective-permute-start(f32[128,128]{1,0:T(8,128)S(1)} %get-tuple-element.110), channel_id=1, source_target_pairs={{0,14},{2,12},{4,10},{6,8},{8,6},{10,4},{12,2},{14,0},{1,15},{3,13... | collective-permute-start | bytes 196616 | tf_op jit(solution)/shard_map/ppermute | solution.py:582
  53.2 2.7 %collective-permute-start.19 = (f32[256,128]{1,0:T(8,128)S(1)}, f32[256,128]{1,0:T(8,128)S(1)}, u32[]{:S(2)}, u32[]{:S(2)}) collective-permute-start(f32[256,128]{1,0:T(8,128)S(1)} %get-tuple-element.114), channel_id=1, source_target_pairs={{0,6},{2,4},{4,2},{6,0},{8,14},{10,12},{12,10},{14,8},{1,7},{3,5},... | collective-permute-start | bytes 393224 | tf_op jit(solution)/shard_map/ppermute | solution.py:582
  55.9 2.1 %collective-permute-start.18 = (f32[256,128]{1,0:T(8,128)S(1)}, f32[256,128]{1,0:T(8,128)S(1)}, u32[]{:S(2)}, u32[]{:S(2)}) collective-permute-start(f32[256,128]{1,0:T(8,128)S(1)} %get-tuple-element.113), channel_id=1, source_target_pairs={{0,4},{2,6},{4,0},{6,2},{8,12},{10,14},{12,8},{14,10},{1,5},{3,7},... | collective-permute-start | bytes 393224 | tf_op jit(solution)/shard_map/ppermute | solution.py:582
  58.0 3.0 %collective-permute-done.15 = f32[128,128]{1,0:T(8,128)S(1)} collective-permute-done((f32[128,128]{1,0:T(8,128)S(1)}, f32[128,128]{1,0:T(8,128)S(1)}, u32[]{:S(2)}, u32[]{:S(2)}) %collective-permute-start.15) | collective-permute-done | bytes 65568 | tf_op jit(solution)/shard_map/ppermute | solution.py:582
  61.8 1.6 %collective-permute-done.16 = f32[128,128]{1,0:T(8,128)S(1)} collective-permute-done((f32[128,128]{1,0:T(8,128)S(1)}, f32[128,128]{1,0:T(8,128)S(1)}, u32[]{:S(2)}, u32[]{:S(2)}) %collective-permute-start.16) | collective-permute-done | bytes 65568 | tf_op jit(solution)/shard_map/ppermute | solution.py:582
  63.4 3.6 %collective-permute-done.17 = f32[128,128]{1,0:T(8,128)S(1)} collective-permute-done((f32[128,128]{1,0:T(8,128)S(1)}, f32[128,128]{1,0:T(8,128)S(1)}, u32[]{:S(2)}, u32[]{:S(2)}) %collective-permute-start.17) | collective-permute-done | bytes 65568 | tf_op jit(solution)/shard_map/ppermute | solution.py:582
  67.1 1.6 %shard_map.43 = f32[2,16,64,128]{3,2,1,0:T(8,128)} custom-call(s32[2]{0:T(128)S(1)} %pad_add_fusion.place_ref, f32[8,16,128]{2,1,0:T(8,128)S(1)} %bitcast.26, f32[8,16,128]{2,1,0:T(8,128)S(1)} %bitcast.27, f32[8,16,128]{2,1,0:T(8,128)S(1)} %bitcast.28, f32[8,16,128]{2,1,0:T(8,128)S(1)} %bitcast.25, f32[8,16,128]{2,1,0:T(8,128)S(1)} %bitcast.29, ...), custom_call_target="tpu_custom_call" | custom-call | tf_op jit(solution)/shard_map/pallas_call | solution.py:113
  (32 shorter events, 6.2 us)
Async XLA Ops:
  0.0 33.2 %copy-start = (f32[3,16,64,128]{3,2,1,0:T(8,128)S(1)}, f32[3,16,64,128]{3,2,1,0:T(8,128)}, u32[]{:S(2)}) copy-start(f32[3,16,64,128]{3,2,1,0:T(8,128)} %param.5) | copy-start | bytes 4718596
  0.1 1.3 %copy-start.1 = (f32[1,2,16,64,128]{4,3,2,1,0:T(8,128)S(1)}, f32[1,2,16,64,128]{4,3,2,1,0:T(8,128)}, u32[]{:S(2)}) copy-start(f32[1,2,16,64,128]{4,3,2,1,0:T(8,128)} %param.3) | copy-start | bytes 3145732
  1.4 31.8 %copy-start.2 = (f32[16,64,128]{2,1,0:T(8,128)S(1)}, f32[16,64,128]{2,1,0:T(8,128)}, u32[]{:S(2)}) copy-start(f32[16,64,128]{2,1,0:T(8,128)} %param.4) | copy-start | bytes 1572868
  2.1 11.1 %collective-permute-start = (f32[256,128]{1,0:T(8,128)S(1)}, f32[256,128]{1,0:T(8,128)S(1)}, u32[]{:S(2)}, u32[]{:S(2)}) collective-permute-start(f32[256,128]{1,0:T(8,128)S(1)} %get-tuple-element.61), channel_id=1, source_target_pairs={{0,8},{2,10},{4,12},{6,14},{8,0},{10,2},{12,4},{14,6},{1,9},{3,11}... | collective-permute-start | bytes 393224 | tf_op jit(solution)/shard_map/ppermute | solution.py:582
  4.8 11.3 %collective-permute-start.4 = (f32[256,128]{1,0:T(8,128)S(1)}, f32[256,128]{1,0:T(8,128)S(1)}, u32[]{:S(2)}, u32[]{:S(2)}) collective-permute-start(f32[256,128]{1,0:T(8,128)S(1)} %get-tuple-element.65), channel_id=1, source_target_pairs={{0,10},{2,8},{4,14},{6,12},{8,2},{10,0},{12,6},{14,4},{1,11},{3,9}... | collective-permute-start | bytes 393224 | tf_op jit(solution)/shard_map/ppermute | solution.py:582
  6.1 21.9 %collective-permute-start.1 = (f32[384,128]{1,0:T(8,128)S(1)}, f32[384,128]{1,0:T(8,128)S(1)}, u32[]{:S(2)}, u32[]{:S(2)}) collective-permute-start(f32[384,128]{1,0:T(8,128)S(1)} %get-tuple-element.62), channel_id=1, source_target_pairs={{0,4},{2,6},{4,0},{6,2},{8,12},{10,14},{12,8},{14,10},{1,5},{3,7},... | collective-permute-start | bytes 589832 | tf_op jit(solution)/shard_map/ppermute | solution.py:582
  6.5 21.4 %collective-permute-start.2 = (f32[384,128]{1,0:T(8,128)S(1)}, f32[384,128]{1,0:T(8,128)S(1)}, u32[]{:S(2)}, u32[]{:S(2)}) collective-permute-start(f32[384,128]{1,0:T(8,128)S(1)} %get-tuple-element.63), channel_id=1, source_target_pairs={{0,6},{2,4},{4,2},{6,0},{8,14},{10,12},{12,10},{14,8},{1,7},{3,5},... | collective-permute-start | bytes 589832 | tf_op jit(solution)/shard_map/ppermute | solution.py:582
  8.1 19.9 %collective-permute-start.3 = (f32[384,128]{1,0:T(8,128)S(1)}, f32[384,128]{1,0:T(8,128)S(1)}, u32[]{:S(2)}, u32[]{:S(2)}) collective-permute-start(f32[384,128]{1,0:T(8,128)S(1)} %get-tuple-element.64), channel_id=1, source_target_pairs={{0,2},{2,0},{4,6},{6,4},{8,10},{10,8},{12,14},{14,12},{1,3},{3,1},... | collective-permute-start | bytes 589832 | tf_op jit(solution)/shard_map/ppermute | solution.py:582
  13.2 6.6 %collective-permute-start.5 = (f32[256,128]{1,0:T(8,128)S(1)}, f32[256,128]{1,0:T(8,128)S(1)}, u32[]{:S(2)}, u32[]{:S(2)}) collective-permute-start(f32[256,128]{1,0:T(8,128)S(1)} %get-tuple-element.66), channel_id=1, source_target_pairs={{0,12},{2,14},{4,8},{6,10},{8,4},{10,6},{12,0},{14,2},{1,13},{3,15... | collective-permute-start | bytes 393224 | tf_op jit(solution)/shard_map/ppermute | solution.py:582
  16.0 11.9 %collective-permute-start.6 = (f32[256,128]{1,0:T(8,128)S(1)}, f32[256,128]{1,0:T(8,128)S(1)}, u32[]{:S(2)}, u32[]{:S(2)}) collective-permute-start(f32[256,128]{1,0:T(8,128)S(1)} %get-tuple-element.67), channel_id=1, source_target_pairs={{0,14},{2,12},{4,10},{6,8},{8,6},{10,4},{12,2},{14,0},{1,15},{3,13... | collective-permute-start | bytes 393224 | tf_op jit(solution)/shard_map/ppermute | solution.py:582
  28.6 6.7 %collective-permute-start.7 = (f32[192,128]{1,0:T(8,128)S(1)}, f32[192,128]{1,0:T(8,128)S(1)}, u32[]{:S(2)}, u32[]{:S(2)}) collective-permute-start(f32[192,128]{1,0:T(8,128)S(1)} %get-tuple-element.90), channel_id=1, source_target_pairs={{0,4},{4,0},{2,6},{6,2},{8,12},{12,8},{10,14},{14,10},{1,5},{5,1},... | collective-permute-start | bytes 294920 | tf_op jit(solution)/shard_map/ppermute | solution.py:594
  28.7 7.5 %collective-permute-start.8 = (f32[192,128]{1,0:T(8,128)S(1)}, f32[192,128]{1,0:T(8,128)S(1)}, u32[]{:S(2)}, u32[]{:S(2)}) collective-permute-start(f32[192,128]{1,0:T(8,128)S(1)} %get-tuple-element.91), channel_id=1, source_target_pairs={{4,8},{8,4},{6,10},{10,6},{5,9},{9,5},{7,11},{11,7},{20,24},{24,20... | collective-permute-start | bytes 294920 | tf_op jit(solution)/shard_map/ppermute | solution.py:595
  39.0 7.8 %collective-permute-start.12 = (f32[800,128]{1,0:T(8,128)S(1)}, f32[800,128]{1,0:T(8,128)S(1)}, u32[]{:S(2)}, u32[]{:S(2)}) collective-permute-start(f32[800,128]{1,0:T(8,128)S(1)} %get-tuple-element.97), channel_id=1, source_target_pairs={{0,1},{1,0},{2,3},{3,2},{4,5},{5,4},{6,7},{7,6},{8,9},{9,8},{10,11... | collective-permute-start | bytes 1228808 | tf_op jit(solution)/shard_map/ppermute | solution.py:514
  39.1 10.2 %collective-permute-start.13 = (f32[128,128]{1,0:T(8,128)S(1)}, f32[128,128]{1,0:T(8,128)S(1)}, u32[]{:S(2)}, u32[]{:S(2)}) collective-permute-start(f32[128,128]{1,0:T(8,128)S(1)} %get-tuple-element.105), channel_id=1, source_target_pairs={{0,10},{2,8},{4,14},{6,12},{8,2},{10,0},{12,6},{14,4},{1,11},{3,9}... | collective-permute-start | bytes 196616 | tf_op jit(solution)/shard_map/ppermute | solution.py:582
  39.4 12.8 %collective-permute-start.9 = (f32[128,128]{1,0:T(8,128)S(1)}, f32[128,128]{1,0:T(8,128)S(1)}, u32[]{:S(2)}, u32[]{:S(2)}) collective-permute-start(f32[128,128]{1,0:T(8,128)S(1)} %get-tuple-element.93), channel_id=1, source_target_pairs={{0,12},{2,14},{4,8},{6,10},{8,4},{10,6},{12,0},{14,2},{1,13},{3,15... | collective-permute-start | bytes 196616 | tf_op jit(solution)/shard_map/ppermute | solution.py:582
  41.0 12.2 %collective-permute-start.10 = (f32[128,128]{1,0:T(8,128)S(1)}, f32[128,128]{1,0:T(8,128)S(1)}, u32[]{:S(2)}, u32[]{:S(2)}) collective-permute-start(f32[128,128]{1,0:T(8,128)S(1)} %get-tuple-element.94), channel_id=1, source_target_pairs={{0,14},{2,12},{4,10},{6,8},{8,6},{10,4},{12,2},{14,0},{1,15},{3,13... | collective-permute-start | bytes 196616 | tf_op jit(solution)/shard_map/ppermute | solution.py:582
  42.0 13.9 %collective-permute-start.11 = (f32[128,128]{1,0:T(8,128)S(1)}, f32[128,128]{1,0:T(8,128)S(1)}, u32[]{:S(2)}, u32[]{:S(2)}) collective-permute-start(f32[128,128]{1,0:T(8,128)S(1)} %get-tuple-element.95), channel_id=1, source_target_pairs={{0,8},{2,10},{4,12},{6,14},{8,0},{10,2},{12,4},{14,6},{1,9},{3,11}... | collective-permute-start | bytes 196616 | tf_op jit(solution)/shard_map/ppermute | solution.py:582
  49.4 8.6 %collective-permute-start.14 = (f32[128,128]{1,0:T(8,128)S(1)}, f32[128,128]{1,0:T(8,128)S(1)}, u32[]{:S(2)}, u32[]{:S(2)}) collective-permute-start(f32[128,128]{1,0:T(8,128)S(1)} %get-tuple-element.109), channel_id=1, source_target_pairs={{0,12},{2,14},{4,8},{6,10},{8,4},{10,6},{12,0},{14,2},{1,13},{3,15... | collective-permute-start | bytes 196616 | tf_op jit(solution)/shard_map/ppermute | solution.py:582
  51.2 9.8 %collective-permute-start.15 = (f32[128,128]{1,0:T(8,128)S(1)}, f32[128,128]{1,0:T(8,128)S(1)}, u32[]{:S(2)}, u32[]{:S(2)}) collective-permute-start(f32[128,128]{1,0:T(8,128)S(1)} %get-tuple-element.110), channel_id=1, source_target_pairs={{0,14},{2,12},{4,10},{6,8},{8,6},{10,4},{12,2},{14,0},{1,15},{3,13... | collective-permute-start | bytes 196616 | tf_op jit(solution)/shard_map/ppermute | solution.py:582
  52.1 14.9 %collective-permute-start.20 = (f32[256,128]{1,0:T(8,128)S(1)}, f32[256,128]{1,0:T(8,128)S(1)}, u32[]{:S(2)}, u32[]{:S(2)}) collective-permute-start(f32[256,128]{1,0:T(8,128)S(1)} %get-tuple-element.115), channel_id=1, source_target_pairs={{0,2},{2,0},{4,6},{6,4},{8,10},{10,8},{12,14},{14,12},{1,3},{3,1},... | collective-permute-start | bytes 393224 | tf_op jit(solution)/shard_map/ppermute | solution.py:582
  53.2 13.9 %collective-permute-start.19 = (f32[256,128]{1,0:T(8,128)S(1)}, f32[256,128]{1,0:T(8,128)S(1)}, u32[]{:S(2)}, u32[]{:S(2)}) collective-permute-start(f32[256,128]{1,0:T(8,128)S(1)} %get-tuple-element.114), channel_id=1, source_target_pairs={{0,6},{2,4},{4,2},{6,0},{8,14},{10,12},{12,10},{14,8},{1,7},{3,5},... | collective-permute-start | bytes 393224 | tf_op jit(solution)/shard_map/ppermute | solution.py:582
  55.9 11.2 %collective-permute-start.18 = (f32[256,128]{1,0:T(8,128)S(1)}, f32[256,128]{1,0:T(8,128)S(1)}, u32[]{:S(2)}, u32[]{:S(2)}) collective-permute-start(f32[256,128]{1,0:T(8,128)S(1)} %get-tuple-element.113), channel_id=1, source_target_pairs={{0,4},{2,6},{4,0},{6,2},{8,12},{10,14},{12,8},{14,10},{1,5},{3,7},... | collective-permute-start | bytes 393224 | tf_op jit(solution)/shard_map/ppermute | solution.py:582
  58.0 5.4 %collective-permute-start.16 = (f32[128,128]{1,0:T(8,128)S(1)}, f32[128,128]{1,0:T(8,128)S(1)}, u32[]{:S(2)}, u32[]{:S(2)}) collective-permute-start(f32[128,128]{1,0:T(8,128)S(1)} %get-tuple-element.111), channel_id=1, source_target_pairs={{0,8},{2,10},{4,12},{6,14},{8,0},{10,2},{12,4},{14,6},{1,9},{3,11}... | collective-permute-start | bytes 196616 | tf_op jit(solution)/shard_map/ppermute | solution.py:582
  61.0 6.1 %collective-permute-start.17 = (f32[128,128]{1,0:T(8,128)S(1)}, f32[128,128]{1,0:T(8,128)S(1)}, u32[]{:S(2)}, u32[]{:S(2)}) collective-permute-start(f32[128,128]{1,0:T(8,128)S(1)} %get-tuple-element.112), channel_id=1, source_target_pairs={{0,10},{2,8},{4,14},{6,12},{8,2},{10,0},{12,6},{14,4},{1,11},{3,9}... | collective-permute-start | bytes 196616 | tf_op jit(solution)/shard_map/ppermute | solution.py:582

commit v7 on v6

--- a/solution.py
+++ b/solution.py
@@ -14,6 +14,7 @@
 COEFS = 9
 RAW = 4
 GROUP = 6
+EARLY = 6
 
 alpha_circ = 0.1
 inv_step = 2.0
@@ -544,11 +545,11 @@
     return [done, rest[:-5]]
 
 
-def place_blocks(plan, place_ref, *refs):
-    place = Place(plan, place_ref)
-    blocks, (out, sems) = refs[:-2], refs[-2:]
+def place_blocks(plan, listed, place_ref, *refs):
+    place = Place(plan, place_ref)
+    blocks, (out, sems) = refs[: len(listed)], refs[-2:]
     copies = []
-    for n, (block, (r, piece)) in enumerate(zip(blocks, sum(plan.back, []))):
+    for n, (block, (r, piece)) in enumerate(zip(blocks, listed)):
         source = place.t ^ r
         quarter, lo = source // plan.per_quarter, source % plan.per_quarter
         z = lo // 2 * plan.nz + (0 if piece is None else place.piece(plan, piece))
@@ -611,13 +612,22 @@
     back = [
         block.reshape(plan.layers(piece), plan.rows, ny) for block, (r, piece) in zip(back, sum(plan.back, []))
     ]
-    out = call(
-        place_blocks,
-        (parts, half_z, nx, ny),
-        back,
-        scratch=[pltpu.SemaphoreType.DMA((len(back),))],
-        out_space=pltpu.HBM,
-    )
+    listed = sum(plan.back, [])
+    cut = EARLY if len(plan.back) == 2 else 0
+    begun = []
+    for chosen in (range(cut), range(cut, len(back))):
+        if len(chosen):
+            out = call(
+                place_blocks,
+                (parts, half_z, nx, ny),
+                [back[n] for n in chosen] + begun,
+                extra=[listed[n] for n in chosen],
+                spaces=[pltpu.VMEM] * len(chosen) + [pltpu.HBM] * len(begun),
+                scratch=[pltpu.SemaphoreType.DMA((len(chosen),))],
+                out_space=pltpu.HBM,
+                aliases={1 + len(chosen): 0} if begun else None,
+            )
+            begun = [out]
     return out[None]
 
 

time: 69.1 us -> 68.9 us (level)
  waiting for transfers between devices: 27.6 us -> 26.3 us
  Pallas kernels: 10.3 us -> 11.5 us
    ppermute x18, waiting for transfers between devices: 26.7 us -> 25.4 us  [turned(): found.append(array if r == 0 else lax.ppermute(array, 'tm', plan.pairs(r)))]
    pallas_call x7 -> x8, Pallas kernels: 10.3 us -> 11.5 us  [kernel_call(): pl.pallas_call(body, out_shape=[jax.ShapeDtypeStruct(s, jnp.float32) for...]
  transfers between devices with their start and end apart: 21 -> 21, of which waited for: 9 -> 9; matrix products, arithmetic and copies ran while one was open for 0% -> 0% of each run, Pallas kernels for 7% -> 9%
where the time goes in v7:
time: 68.9 us; the launch traced here: 68.5 us
  starting transfers between devices  29.2 us (42%)
  waiting for transfers between devices  26.3 us (38%)
  Pallas kernels  11.5 us (17%)
  local copies, waits for them, and re-layouts  1.34 us (2%)
    ppermute x18, waiting for transfers between devices, turned(): found.append(array if r == 0 else lax.ppermute(array, 'tm', plan.pairs(r)))  25.4 us
    ppermute x18, starting transfers between devices, turned(): found.append(array if r == 0 else lax.ppermute(array, 'tm', plan.pairs(r)))  24.5 us
    pallas_call x8, Pallas kernels, kernel_call(): pl.pallas_call(body, out_shape=[jax.ShapeDtypeStruct(s, jnp.float32) for...  11.5 us
    ppermute x1, starting transfers between devices, local(): odd = lax.ppermute(x_odd, 'tm', plan.x_pairs(1))  4.54 us
  transfers between devices with their start and end apart: 21, of which 9 were waited for; matrix products, arithmetic and copies ran while one was open for 0% of the time, Pallas kernels for 9%

profile of v7, /device:TPU:8, one launch (start us, length us, event | category | flops | bytes accessed | tf_op | source)
XLA Modules:
  0.0 68.5 jit_solution(7147338799335238597)
XLA Ops:
  0.1 1.3 %copy-done.1 = f32[1,2,16,64,128]{4,3,2,1,0:T(8,128)S(1)} copy-done((f32[1,2,16,64,128]{4,3,2,1,0:T(8,128)S(1)}, f32[1,2,16,64,128]{4,3,2,1,0:T(8,128)}, u32[]{:S(2)}) %copy-start.1) | copy-done | bytes 1048600
  2.1 2.7 %collective-permute-start = (f32[256,128]{1,0:T(8,128)S(1)}, f32[256,128]{1,0:T(8,128)S(1)}, u32[]{:S(2)}, u32[]{:S(2)}) collective-permute-start(f32[256,128]{1,0:T(8,128)S(1)} %get-tuple-element.61), channel_id=1, source_target_pairs={{0,8},{2,10},{4,12},{6,14},{8,0},{10,2},{12,4},{14,6},{1,9},{3,11}... | collective-permute-start | bytes 393224 | tf_op jit(solution)/shard_map/ppermute | solution.py:583
  4.8 1.3 %collective-permute-start.4 = (f32[256,128]{1,0:T(8,128)S(1)}, f32[256,128]{1,0:T(8,128)S(1)}, u32[]{:S(2)}, u32[]{:S(2)}) collective-permute-start(f32[256,128]{1,0:T(8,128)S(1)} %get-tuple-element.65), channel_id=1, source_target_pairs={{0,10},{2,8},{4,14},{6,12},{8,2},{10,0},{12,6},{14,4},{1,11},{3,9}... | collective-permute-start | bytes 393224 | tf_op jit(solution)/shard_map/ppermute | solution.py:583
  6.5 1.5 %collective-permute-start.2 = (f32[384,128]{1,0:T(8,128)S(1)}, f32[384,128]{1,0:T(8,128)S(1)}, u32[]{:S(2)}, u32[]{:S(2)}) collective-permute-start(f32[384,128]{1,0:T(8,128)S(1)} %get-tuple-element.63), channel_id=1, source_target_pairs={{0,6},{2,4},{4,2},{6,0},{8,14},{10,12},{12,10},{14,8},{1,7},{3,5},... | collective-permute-start | bytes 589832 | tf_op jit(solution)/shard_map/ppermute | solution.py:583
  8.1 1.5 %collective-permute-start.3 = (f32[384,128]{1,0:T(8,128)S(1)}, f32[384,128]{1,0:T(8,128)S(1)}, u32[]{:S(2)}, u32[]{:S(2)}) collective-permute-start(f32[384,128]{1,0:T(8,128)S(1)} %get-tuple-element.64), channel_id=1, source_target_pairs={{0,2},{2,0},{4,6},{6,4},{8,10},{10,8},{12,14},{14,12},{1,3},{3,1},... | collective-permute-start | bytes 589832 | tf_op jit(solution)/shard_map/ppermute | solution.py:583
  9.6 3.6 %collective-permute-done.refs_0_ = f32[256,128]{1,0:T(8,128)S(1)} collective-permute-done((f32[256,128]{1,0:T(8,128)S(1)}, f32[256,128]{1,0:T(8,128)S(1)}, u32[]{:S(2)}, u32[]{:S(2)}) %collective-permute-start) | collective-permute-done | bytes 131104 | tf_op jit(solution)/shard_map/ppermute | solution.py:583
  13.2 2.9 %collective-permute-done.4.refs_4_ = f32[256,128]{1,0:T(8,128)S(1)} collective-permute-done((f32[256,128]{1,0:T(8,128)S(1)}, f32[256,128]{1,0:T(8,128)S(1)}, u32[]{:S(2)}, u32[]{:S(2)}) %collective-permute-start.4) | collective-permute-done | bytes 131104 | tf_op jit(solution)/shard_map/ppermute | solution.py:583
  16.3 3.5 %collective-permute-done.5.refs_5_ = f32[256,128]{1,0:T(8,128)S(1)} collective-permute-done((f32[256,128]{1,0:T(8,128)S(1)}, f32[256,128]{1,0:T(8,128)S(1)}, u32[]{:S(2)}, u32[]{:S(2)}) %collective-permute-start.5) | collective-permute-done | bytes 131104 | tf_op jit(solution)/shard_map/ppermute | solution.py:583
  19.8 8.2 %collective-permute-done.6.refs_6_ = f32[256,128]{1,0:T(8,128)S(1)} collective-permute-done((f32[256,128]{1,0:T(8,128)S(1)}, f32[256,128]{1,0:T(8,128)S(1)}, u32[]{:S(2)}, u32[]{:S(2)}) %collective-permute-start.6) | collective-permute-done | bytes 131104 | tf_op jit(solution)/shard_map/ppermute | solution.py:583
  28.7 4.5 %collective-permute-start.8 = (f32[192,128]{1,0:T(8,128)S(1)}, f32[192,128]{1,0:T(8,128)S(1)}, u32[]{:S(2)}, u32[]{:S(2)}) collective-permute-start(f32[192,128]{1,0:T(8,128)S(1)} %get-tuple-element.91), channel_id=1, source_target_pairs={{4,8},{8,4},{6,10},{10,6},{5,9},{9,5},{7,11},{11,7},{20,24},{24,20... | collective-permute-start | bytes 294920 | tf_op jit(solution)/shard_map/ppermute | solution.py:596
  33.3 1.1 %shard_map.38 = (f32[4752,128]{1,0:T(8,128)S(1)}, f32[288,128]{1,0:T(8,128)S(1)}) custom-call(s32[2]{0:T(128)S(1)} %pad_add_fusion.place_ref, f32[1024,128]{1,0:T(8,128)S(1)} %bitcast.20, f32[3072,128]{1,0:T(8,128)S(1)} %bitcast.18), custom_call_target="tpu_custom_call" | custom-call | tf_op jit(solution)/shard_map/pallas_call | solution.py:114
  36.2 2.8 %shard_map.41 = (f32[128,128]{1,0:T(8,128)S(1)}, f32[128,128]{1,0:T(8,128)S(1)}, f32[128,128]{1,0:T(8,128)S(1)}, f32[128,128]{1,0:T(8,128)S(1)}, f32[4224,128]{1...) custom-call(s32[2]{0:T(128)S(1)} %pad_add_fusion.place_ref, ...), custom_call_target="tpu_custom_call", output_to_operand_aliasing={{4}: (2, {}), {5}: (3, {})} | custom-call | tf_op jit(solution)/shard_map/pallas_call | solution.py:114
  39.4 1.6 %collective-permute-start.16 = (f32[128,128]{1,0:T(8,128)S(1)}, f32[128,128]{1,0:T(8,128)S(1)}, u32[]{:S(2)}, u32[]{:S(2)}) collective-permute-start(f32[128,128]{1,0:T(8,128)S(1)} %get-tuple-element.111), channel_id=1, source_target_pairs={{0,12},{2,14},{4,8},{6,10},{8,4},{10,6},{12,0},{14,2},{1,13},{3,15... | collective-permute-start | bytes 196616 | tf_op jit(solution)/shard_map/ppermute | solution.py:583
  41.0 1.0 %collective-permute-start.17 = (f32[128,128]{1,0:T(8,128)S(1)}, f32[128,128]{1,0:T(8,128)S(1)}, u32[]{:S(2)}, u32[]{:S(2)}) collective-permute-start(f32[128,128]{1,0:T(8,128)S(1)} %get-tuple-element.112), channel_id=1, source_target_pairs={{0,14},{2,12},{4,10},{6,8},{8,6},{10,4},{12,2},{14,0},{1,15},{3,13... | collective-permute-start | bytes 196616 | tf_op jit(solution)/shard_map/ppermute | solution.py:583
  42.0 4.9 %collective-permute-start.18 = (f32[128,128]{1,0:T(8,128)S(1)}, f32[128,128]{1,0:T(8,128)S(1)}, u32[]{:S(2)}, u32[]{:S(2)}) collective-permute-start(f32[128,128]{1,0:T(8,128)S(1)} %get-tuple-element.113), channel_id=1, source_target_pairs={{0,8},{2,10},{4,12},{6,14},{8,0},{10,2},{12,4},{14,6},{1,9},{3,11}... | collective-permute-start | bytes 196616 | tf_op jit(solution)/shard_map/ppermute | solution.py:583
  46.8 2.5 %shard_map.42 = (f32[128,128]{1,0:T(8,128)S(1)}, f32[128,128]{1,0:T(8,128)S(1)}, f32[128,128]{1,0:T(8,128)S(1)}, f32[128,128]{1,0:T(8,128)S(1)}, f32[256,128]{1,...) custom-call(s32[2]{0:T(128)S(1)} %pad_add_fusion.place_ref, ...), custom_call_target="tpu_custom_call", output_to_operand_aliasing={{8}: (3, {}), {9}: (4, {}), {10}: (5, {}), {11}: (6, {}), {... | custom-call | tf_op jit(solution)/shard_map/pallas_call | solution.py:114
  49.4 1.8 %collective-permute-start.19 = (f32[128,128]{1,0:T(8,128)S(1)}, f32[128,128]{1,0:T(8,128)S(1)}, u32[]{:S(2)}, u32[]{:S(2)}) collective-permute-start(f32[128,128]{1,0:T(8,128)S(1)} %get-tuple-element.115), channel_id=1, source_target_pairs={{0,12},{2,14},{4,8},{6,10},{8,4},{10,6},{12,0},{14,2},{1,13},{3,15... | collective-permute-start | bytes 196616 | tf_op jit(solution)/shard_map/ppermute | solution.py:583
  51.2 1.0 %collective-permute-start.20 = (f32[128,128]{1,0:T(8,128)S(1)}, f32[128,128]{1,0:T(8,128)S(1)}, u32[]{:S(2)}, u32[]{:S(2)}) collective-permute-start(f32[128,128]{1,0:T(8,128)S(1)} %get-tuple-element.116), channel_id=1, source_target_pairs={{0,14},{2,12},{4,10},{6,8},{8,6},{10,4},{12,2},{14,0},{1,15},{3,13... | collective-permute-start | bytes 196616 | tf_op jit(solution)/shard_map/ppermute | solution.py:583
  53.2 2.7 %collective-permute-start.14 = (f32[256,128]{1,0:T(8,128)S(1)}, f32[256,128]{1,0:T(8,128)S(1)}, u32[]{:S(2)}, u32[]{:S(2)}) collective-permute-start(f32[256,128]{1,0:T(8,128)S(1)} %get-tuple-element.106), channel_id=1, source_target_pairs={{0,6},{2,4},{4,2},{6,0},{8,14},{10,12},{12,10},{14,8},{1,7},{3,5},... | collective-permute-start | bytes 393224 | tf_op jit(solution)/shard_map/ppermute | solution.py:583
  55.9 2.1 %collective-permute-start.13 = (f32[256,128]{1,0:T(8,128)S(1)}, f32[256,128]{1,0:T(8,128)S(1)}, u32[]{:S(2)}, u32[]{:S(2)}) collective-permute-start(f32[256,128]{1,0:T(8,128)S(1)} %get-tuple-element.103), channel_id=1, source_target_pairs={{0,4},{2,6},{4,0},{6,2},{8,12},{10,14},{12,8},{14,10},{1,5},{3,7},... | collective-permute-start | bytes 393224 | tf_op jit(solution)/shard_map/ppermute | solution.py:583
  58.0 3.0 %collective-permute-done.20 = f32[128,128]{1,0:T(8,128)S(1)} collective-permute-done((f32[128,128]{1,0:T(8,128)S(1)}, f32[128,128]{1,0:T(8,128)S(1)}, u32[]{:S(2)}, u32[]{:S(2)}) %collective-permute-start.20) | collective-permute-done | bytes 65568 | tf_op jit(solution)/shard_map/ppermute | solution.py:583
  61.8 1.4 %shard_map.43.refs_6_ = f32[2,16,64,128]{3,2,1,0:T(8,128)} custom-call(s32[2]{0:T(128)S(1)} %pad_add_fusion.place_ref, f32[8,16,128]{2,1,0:T(8,128)S(1)} %bitcast.28, f32[8,16,128]{2,1,0:T(8,128)S(1)} %bitcast.29, f32[8,16,128]{2,1,0:T(8,128)S(1)} %bitcast.30, f32[8,16,128]{2,1,0:T(8,128)S(1)} %bitcast.27, f32[8,16,128]{2,1,0:T(8,128)S(1)} %bitcast.31, ...), custom_call_target="tpu_custom_call" | custom-call | tf_op jit(solution)/shard_map/pallas_call | solution.py:114
  63.4 3.6 %collective-permute-done.11 = f32[128,128]{1,0:T(8,128)S(1)} collective-permute-done((f32[128,128]{1,0:T(8,128)S(1)}, f32[128,128]{1,0:T(8,128)S(1)}, u32[]{:S(2)}, u32[]{:S(2)}) %collective-permute-start.11) | collective-permute-done | bytes 65568 | tf_op jit(solution)/shard_map/ppermute | solution.py:583
  67.1 1.5 %shard_map.44 = f32[2,16,64,128]{3,2,1,0:T(8,128)} custom-call(s32[2]{0:T(128)S(1)} %pad_add_fusion.place_ref, f32[8,16,128]{2,1,0:T(8,128)S(1)} %bitcast.25, f32[8,16,128]{2,1,0:T(8,128)S(1)} %bitcast.26, f32[16,16,128]{2,1,0:T(8,128)S(1)} %bitcast.24, f32[16,16,128]{2,1,0:T(8,128)S(1)} %bitcast.23, ...), custom_call_target="tpu_custom_call", output_to_operand_aliasing={{}: (7, {})} | custom-call | tf_op jit(solution)/shard_map/pallas_call | solution.py:114
  (33 shorter events, 6.4 us)
Async XLA Ops:
  0.0 33.2 %copy-start = (f32[3,16,64,128]{3,2,1,0:T(8,128)S(1)}, f32[3,16,64,128]{3,2,1,0:T(8,128)}, u32[]{:S(2)}) copy-start(f32[3,16,64,128]{3,2,1,0:T(8,128)} %param.5) | copy-start | bytes 4718596
  0.1 1.3 %copy-start.1 = (f32[1,2,16,64,128]{4,3,2,1,0:T(8,128)S(1)}, f32[1,2,16,64,128]{4,3,2,1,0:T(8,128)}, u32[]{:S(2)}) copy-start(f32[1,2,16,64,128]{4,3,2,1,0:T(8,128)} %param.3) | copy-start | bytes 3145732
  1.4 31.8 %copy-start.2 = (f32[16,64,128]{2,1,0:T(8,128)S(1)}, f32[16,64,128]{2,1,0:T(8,128)}, u32[]{:S(2)}) copy-start(f32[16,64,128]{2,1,0:T(8,128)} %param.4) | copy-start | bytes 1572868
  2.1 11.1 %collective-permute-start = (f32[256,128]{1,0:T(8,128)S(1)}, f32[256,128]{1,0:T(8,128)S(1)}, u32[]{:S(2)}, u32[]{:S(2)}) collective-permute-start(f32[256,128]{1,0:T(8,128)S(1)} %get-tuple-element.61), channel_id=1, source_target_pairs={{0,8},{2,10},{4,12},{6,14},{8,0},{10,2},{12,4},{14,6},{1,9},{3,11}... | collective-permute-start | bytes 393224 | tf_op jit(solution)/shard_map/ppermute | solution.py:583
  4.8 11.3 %collective-permute-start.4 = (f32[256,128]{1,0:T(8,128)S(1)}, f32[256,128]{1,0:T(8,128)S(1)}, u32[]{:S(2)}, u32[]{:S(2)}) collective-permute-start(f32[256,128]{1,0:T(8,128)S(1)} %get-tuple-element.65), channel_id=1, source_target_pairs={{0,10},{2,8},{4,14},{6,12},{8,2},{10,0},{12,6},{14,4},{1,11},{3,9}... | collective-permute-start | bytes 393224 | tf_op jit(solution)/shard_map/ppermute | solution.py:583
  6.1 21.9 %collective-permute-start.1 = (f32[384,128]{1,0:T(8,128)S(1)}, f32[384,128]{1,0:T(8,128)S(1)}, u32[]{:S(2)}, u32[]{:S(2)}) collective-permute-start(f32[384,128]{1,0:T(8,128)S(1)} %get-tuple-element.62), channel_id=1, source_target_pairs={{0,4},{2,6},{4,0},{6,2},{8,12},{10,14},{12,8},{14,10},{1,5},{3,7},... | collective-permute-start | bytes 589832 | tf_op jit(solution)/shard_map/ppermute | solution.py:583
  6.5 21.4 %collective-permute-start.2 = (f32[384,128]{1,0:T(8,128)S(1)}, f32[384,128]{1,0:T(8,128)S(1)}, u32[]{:S(2)}, u32[]{:S(2)}) collective-permute-start(f32[384,128]{1,0:T(8,128)S(1)} %get-tuple-element.63), channel_id=1, source_target_pairs={{0,6},{2,4},{4,2},{6,0},{8,14},{10,12},{12,10},{14,8},{1,7},{3,5},... | collective-permute-start | bytes 589832 | tf_op jit(solution)/shard_map/ppermute | solution.py:583
  8.1 19.9 %collective-permute-start.3 = (f32[384,128]{1,0:T(8,128)S(1)}, f32[384,128]{1,0:T(8,128)S(1)}, u32[]{:S(2)}, u32[]{:S(2)}) collective-permute-start(f32[384,128]{1,0:T(8,128)S(1)} %get-tuple-element.64), channel_id=1, source_target_pairs={{0,2},{2,0},{4,6},{6,4},{8,10},{10,8},{12,14},{14,12},{1,3},{3,1},... | collective-permute-start | bytes 589832 | tf_op jit(solution)/shard_map/ppermute | solution.py:583
  13.2 6.6 %collective-permute-start.5 = (f32[256,128]{1,0:T(8,128)S(1)}, f32[256,128]{1,0:T(8,128)S(1)}, u32[]{:S(2)}, u32[]{:S(2)}) collective-permute-start(f32[256,128]{1,0:T(8,128)S(1)} %get-tuple-element.66), channel_id=1, source_target_pairs={{0,12},{2,14},{4,8},{6,10},{8,4},{10,6},{12,0},{14,2},{1,13},{3,15... | collective-permute-start | bytes 393224 | tf_op jit(solution)/shard_map/ppermute | solution.py:583
  16.0 11.9 %collective-permute-start.6 = (f32[256,128]{1,0:T(8,128)S(1)}, f32[256,128]{1,0:T(8,128)S(1)}, u32[]{:S(2)}, u32[]{:S(2)}) collective-permute-start(f32[256,128]{1,0:T(8,128)S(1)} %get-tuple-element.67), channel_id=1, source_target_pairs={{0,14},{2,12},{4,10},{6,8},{8,6},{10,4},{12,2},{14,0},{1,15},{3,13... | collective-permute-start | bytes 393224 | tf_op jit(solution)/shard_map/ppermute | solution.py:583
  28.6 6.7 %collective-permute-start.7 = (f32[192,128]{1,0:T(8,128)S(1)}, f32[192,128]{1,0:T(8,128)S(1)}, u32[]{:S(2)}, u32[]{:S(2)}) collective-permute-start(f32[192,128]{1,0:T(8,128)S(1)} %get-tuple-element.90), channel_id=1, source_target_pairs={{0,4},{4,0},{2,6},{6,2},{8,12},{12,8},{10,14},{14,10},{1,5},{5,1},... | collective-permute-start | bytes 294920 | tf_op jit(solution)/shard_map/ppermute | solution.py:595
  28.7 7.5 %collective-permute-start.8 = (f32[192,128]{1,0:T(8,128)S(1)}, f32[192,128]{1,0:T(8,128)S(1)}, u32[]{:S(2)}, u32[]{:S(2)}) collective-permute-start(f32[192,128]{1,0:T(8,128)S(1)} %get-tuple-element.91), channel_id=1, source_target_pairs={{4,8},{8,4},{6,10},{10,6},{5,9},{9,5},{7,11},{11,7},{20,24},{24,20... | collective-permute-start | bytes 294920 | tf_op jit(solution)/shard_map/ppermute | solution.py:596
  39.0 7.8 %collective-permute-start.9 = (f32[800,128]{1,0:T(8,128)S(1)}, f32[800,128]{1,0:T(8,128)S(1)}, u32[]{:S(2)}, u32[]{:S(2)}) collective-permute-start(f32[800,128]{1,0:T(8,128)S(1)} %get-tuple-element.94), channel_id=1, source_target_pairs={{0,1},{1,0},{2,3},{3,2},{4,5},{5,4},{6,7},{7,6},{8,9},{9,8},{10,11... | collective-permute-start | bytes 1228808 | tf_op jit(solution)/shard_map/ppermute | solution.py:515
  39.1 10.2 %collective-permute-start.12 = (f32[128,128]{1,0:T(8,128)S(1)}, f32[128,128]{1,0:T(8,128)S(1)}, u32[]{:S(2)}, u32[]{:S(2)}) collective-permute-start(f32[128,128]{1,0:T(8,128)S(1)} %get-tuple-element.102), channel_id=1, source_target_pairs={{0,10},{2,8},{4,14},{6,12},{8,2},{10,0},{12,6},{14,4},{1,11},{3,9}... | collective-permute-start | bytes 196616 | tf_op jit(solution)/shard_map/ppermute | solution.py:583
  39.4 12.8 %collective-permute-start.16 = (f32[128,128]{1,0:T(8,128)S(1)}, f32[128,128]{1,0:T(8,128)S(1)}, u32[]{:S(2)}, u32[]{:S(2)}) collective-permute-start(f32[128,128]{1,0:T(8,128)S(1)} %get-tuple-element.111), channel_id=1, source_target_pairs={{0,12},{2,14},{4,8},{6,10},{8,4},{10,6},{12,0},{14,2},{1,13},{3,15... | collective-permute-start | bytes 196616 | tf_op jit(solution)/shard_map/ppermute | solution.py:583
  41.0 12.2 %collective-permute-start.17 = (f32[128,128]{1,0:T(8,128)S(1)}, f32[128,128]{1,0:T(8,128)S(1)}, u32[]{:S(2)}, u32[]{:S(2)}) collective-permute-start(f32[128,128]{1,0:T(8,128)S(1)} %get-tuple-element.112), channel_id=1, source_target_pairs={{0,14},{2,12},{4,10},{6,8},{8,6},{10,4},{12,2},{14,0},{1,15},{3,13... | collective-permute-start | bytes 196616 | tf_op jit(solution)/shard_map/ppermute | solution.py:583
  42.0 13.9 %collective-permute-start.18 = (f32[128,128]{1,0:T(8,128)S(1)}, f32[128,128]{1,0:T(8,128)S(1)}, u32[]{:S(2)}, u32[]{:S(2)}) collective-permute-start(f32[128,128]{1,0:T(8,128)S(1)} %get-tuple-element.113), channel_id=1, source_target_pairs={{0,8},{2,10},{4,12},{6,14},{8,0},{10,2},{12,4},{14,6},{1,9},{3,11}... | collective-permute-start | bytes 196616 | tf_op jit(solution)/shard_map/ppermute | solution.py:583
  49.4 8.6 %collective-permute-start.19 = (f32[128,128]{1,0:T(8,128)S(1)}, f32[128,128]{1,0:T(8,128)S(1)}, u32[]{:S(2)}, u32[]{:S(2)}) collective-permute-start(f32[128,128]{1,0:T(8,128)S(1)} %get-tuple-element.115), channel_id=1, source_target_pairs={{0,12},{2,14},{4,8},{6,10},{8,4},{10,6},{12,0},{14,2},{1,13},{3,15... | collective-permute-start | bytes 196616 | tf_op jit(solution)/shard_map/ppermute | solution.py:583
  51.2 9.8 %collective-permute-start.20 = (f32[128,128]{1,0:T(8,128)S(1)}, f32[128,128]{1,0:T(8,128)S(1)}, u32[]{:S(2)}, u32[]{:S(2)}) collective-permute-start(f32[128,128]{1,0:T(8,128)S(1)} %get-tuple-element.116), channel_id=1, source_target_pairs={{0,14},{2,12},{4,10},{6,8},{8,6},{10,4},{12,2},{14,0},{1,15},{3,13... | collective-permute-start | bytes 196616 | tf_op jit(solution)/shard_map/ppermute | solution.py:583
  52.1 14.9 %collective-permute-start.15 = (f32[256,128]{1,0:T(8,128)S(1)}, f32[256,128]{1,0:T(8,128)S(1)}, u32[]{:S(2)}, u32[]{:S(2)}) collective-permute-start(f32[256,128]{1,0:T(8,128)S(1)} %get-tuple-element.109), channel_id=1, source_target_pairs={{0,2},{2,0},{4,6},{6,4},{8,10},{10,8},{12,14},{14,12},{1,3},{3,1},... | collective-permute-start | bytes 393224 | tf_op jit(solution)/shard_map/ppermute | solution.py:583
  53.2 13.9 %collective-permute-start.14 = (f32[256,128]{1,0:T(8,128)S(1)}, f32[256,128]{1,0:T(8,128)S(1)}, u32[]{:S(2)}, u32[]{:S(2)}) collective-permute-start(f32[256,128]{1,0:T(8,128)S(1)} %get-tuple-element.106), channel_id=1, source_target_pairs={{0,6},{2,4},{4,2},{6,0},{8,14},{10,12},{12,10},{14,8},{1,7},{3,5},... | collective-permute-start | bytes 393224 | tf_op jit(solution)/shard_map/ppermute | solution.py:583
  55.9 11.2 %collective-permute-start.13 = (f32[256,128]{1,0:T(8,128)S(1)}, f32[256,128]{1,0:T(8,128)S(1)}, u32[]{:S(2)}, u32[]{:S(2)}) collective-permute-start(f32[256,128]{1,0:T(8,128)S(1)} %get-tuple-element.103), channel_id=1, source_target_pairs={{0,4},{2,6},{4,0},{6,2},{8,12},{10,14},{12,8},{14,10},{1,5},{3,7},... | collective-permute-start | bytes 393224 | tf_op jit(solution)/shard_map/ppermute | solution.py:583
  58.0 5.4 %collective-permute-start.10 = (f32[128,128]{1,0:T(8,128)S(1)}, f32[128,128]{1,0:T(8,128)S(1)}, u32[]{:S(2)}, u32[]{:S(2)}) collective-permute-start(f32[128,128]{1,0:T(8,128)S(1)} %get-tuple-element.99), channel_id=1, source_target_pairs={{0,8},{2,10},{4,12},{6,14},{8,0},{10,2},{12,4},{14,6},{1,9},{3,11}... | collective-permute-start | bytes 196616 | tf_op jit(solution)/shard_map/ppermute | solution.py:583
  61.0 6.1 %collective-permute-start.11 = (f32[128,128]{1,0:T(8,128)S(1)}, f32[128,128]{1,0:T(8,128)S(1)}, u32[]{:S(2)}, u32[]{:S(2)}) collective-permute-start(f32[128,128]{1,0:T(8,128)S(1)} %get-tuple-element.100), channel_id=1, source_target_pairs={{0,10},{2,8},{4,14},{6,12},{8,2},{10,0},{12,6},{14,4},{1,11},{3,9}... | collective-permute-start | bytes 196616 | tf_op jit(solution)/shard_map/ppermute | solution.py:583

commit v8 on v7

--- a/solution.py
+++ b/solution.py
@@ -13,7 +13,7 @@
 TILE = 8
 COEFS = 9
 RAW = 4
-GROUP = 6
+GROUP = 10
 EARLY = 6
 
 alpha_circ = 0.1

time: 68.9 us -> 68.9 us (level)
  no operation moved by 1% of the time
where the time goes in v8:
time: 68.9 us; the launch traced here: 68.5 us
  starting transfers between devices  29.2 us (42%)
  waiting for transfers between devices  26.3 us (38%)
  Pallas kernels  11.5 us (17%)
  local copies, waits for them, and re-layouts  1.34 us (2%)
    ppermute x18, waiting for transfers between devices, turned(): found.append(array if r == 0 else lax.ppermute(array, 'tm', plan.pairs(r)))  25.4 us
    ppermute x18, starting transfers between devices, turned(): found.append(array if r == 0 else lax.ppermute(array, 'tm', plan.pairs(r)))  24.5 us
    pallas_call x8, Pallas kernels, kernel_call(): pl.pallas_call(body, out_shape=[jax.ShapeDtypeStruct(s, jnp.float32) for...  11.5 us
    ppermute x1, starting transfers between devices, local(): odd = lax.ppermute(x_odd, 'tm', plan.x_pairs(1))  4.54 us
  transfers between devices with their start and end apart: 21, of which 9 were waited for; matrix products, arithmetic and copies ran while one was open for 0% of the time, Pallas kernels for 9%

profile of v8, /device:TPU:8, one launch (start us, length us, event | category | flops | bytes accessed | tf_op | source)
XLA Modules:
  0.0 68.5 jit_solution(3542664638079903460)
XLA Ops:
  0.1 1.3 %copy-done.1 = f32[1,2,16,64,128]{4,3,2,1,0:T(8,128)S(1)} copy-done((f32[1,2,16,64,128]{4,3,2,1,0:T(8,128)S(1)}, f32[1,2,16,64,128]{4,3,2,1,0:T(8,128)}, u32[]{:S(2)}) %copy-start.1) | copy-done | bytes 1048600
  2.1 2.7 %collective-permute-start = (f32[256,128]{1,0:T(8,128)S(1)}, f32[256,128]{1,0:T(8,128)S(1)}, u32[]{:S(2)}, u32[]{:S(2)}) collective-permute-start(f32[256,128]{1,0:T(8,128)S(1)} %get-tuple-element.61), channel_id=1, source_target_pairs={{0,8},{2,10},{4,12},{6,14},{8,0},{10,2},{12,4},{14,6},{1,9},{3,11}... | collective-permute-start | bytes 393224 | tf_op jit(solution)/shard_map/ppermute | solution.py:583
  4.8 1.3 %collective-permute-start.4 = (f32[256,128]{1,0:T(8,128)S(1)}, f32[256,128]{1,0:T(8,128)S(1)}, u32[]{:S(2)}, u32[]{:S(2)}) collective-permute-start(f32[256,128]{1,0:T(8,128)S(1)} %get-tuple-element.65), channel_id=1, source_target_pairs={{0,10},{2,8},{4,14},{6,12},{8,2},{10,0},{12,6},{14,4},{1,11},{3,9}... | collective-permute-start | bytes 393224 | tf_op jit(solution)/shard_map/ppermute | solution.py:583
  6.5 1.5 %collective-permute-start.2 = (f32[384,128]{1,0:T(8,128)S(1)}, f32[384,128]{1,0:T(8,128)S(1)}, u32[]{:S(2)}, u32[]{:S(2)}) collective-permute-start(f32[384,128]{1,0:T(8,128)S(1)} %get-tuple-element.63), channel_id=1, source_target_pairs={{0,6},{2,4},{4,2},{6,0},{8,14},{10,12},{12,10},{14,8},{1,7},{3,5},... | collective-permute-start | bytes 589832 | tf_op jit(solution)/shard_map/ppermute | solution.py:583
  8.1 1.5 %collective-permute-start.3 = (f32[384,128]{1,0:T(8,128)S(1)}, f32[384,128]{1,0:T(8,128)S(1)}, u32[]{:S(2)}, u32[]{:S(2)}) collective-permute-start(f32[384,128]{1,0:T(8,128)S(1)} %get-tuple-element.64), channel_id=1, source_target_pairs={{0,2},{2,0},{4,6},{6,4},{8,10},{10,8},{12,14},{14,12},{1,3},{3,1},... | collective-permute-start | bytes 589832 | tf_op jit(solution)/shard_map/ppermute | solution.py:583
  9.6 3.6 %collective-permute-done.refs_0_ = f32[256,128]{1,0:T(8,128)S(1)} collective-permute-done((f32[256,128]{1,0:T(8,128)S(1)}, f32[256,128]{1,0:T(8,128)S(1)}, u32[]{:S(2)}, u32[]{:S(2)}) %collective-permute-start) | collective-permute-done | bytes 131104 | tf_op jit(solution)/shard_map/ppermute | solution.py:583
  13.2 2.9 %collective-permute-done.4.refs_4_ = f32[256,128]{1,0:T(8,128)S(1)} collective-permute-done((f32[256,128]{1,0:T(8,128)S(1)}, f32[256,128]{1,0:T(8,128)S(1)}, u32[]{:S(2)}, u32[]{:S(2)}) %collective-permute-start.4) | collective-permute-done | bytes 131104 | tf_op jit(solution)/shard_map/ppermute | solution.py:583
  16.3 3.5 %collective-permute-done.5.refs_5_ = f32[256,128]{1,0:T(8,128)S(1)} collective-permute-done((f32[256,128]{1,0:T(8,128)S(1)}, f32[256,128]{1,0:T(8,128)S(1)}, u32[]{:S(2)}, u32[]{:S(2)}) %collective-permute-start.5) | collective-permute-done | bytes 131104 | tf_op jit(solution)/shard_map/ppermute | solution.py:583
  19.8 8.2 %collective-permute-done.6.refs_6_ = f32[256,128]{1,0:T(8,128)S(1)} collective-permute-done((f32[256,128]{1,0:T(8,128)S(1)}, f32[256,128]{1,0:T(8,128)S(1)}, u32[]{:S(2)}, u32[]{:S(2)}) %collective-permute-start.6) | collective-permute-done | bytes 131104 | tf_op jit(solution)/shard_map/ppermute | solution.py:583
  28.7 4.5 %collective-permute-start.8 = (f32[192,128]{1,0:T(8,128)S(1)}, f32[192,128]{1,0:T(8,128)S(1)}, u32[]{:S(2)}, u32[]{:S(2)}) collective-permute-start(f32[192,128]{1,0:T(8,128)S(1)} %get-tuple-element.91), channel_id=1, source_target_pairs={{4,8},{8,4},{6,10},{10,6},{5,9},{9,5},{7,11},{11,7},{20,24},{24,20... | collective-permute-start | bytes 294920 | tf_op jit(solution)/shard_map/ppermute | solution.py:596
  33.3 1.1 %shard_map.38 = (f32[4752,128]{1,0:T(8,128)S(1)}, f32[288,128]{1,0:T(8,128)S(1)}) custom-call(s32[2]{0:T(128)S(1)} %pad_add_fusion.place_ref, f32[1024,128]{1,0:T(8,128)S(1)} %bitcast.20, f32[3072,128]{1,0:T(8,128)S(1)} %bitcast.18), custom_call_target="tpu_custom_call" | custom-call | tf_op jit(solution)/shard_map/pallas_call | solution.py:114
  36.2 2.8 %shard_map.41 = (f32[128,128]{1,0:T(8,128)S(1)}, f32[128,128]{1,0:T(8,128)S(1)}, f32[128,128]{1,0:T(8,128)S(1)}, f32[128,128]{1,0:T(8,128)S(1)}, f32[4224,128]{1...) custom-call(s32[2]{0:T(128)S(1)} %pad_add_fusion.place_ref, ...), custom_call_target="tpu_custom_call", output_to_operand_aliasing={{4}: (2, {}), {5}: (3, {})} | custom-call | tf_op jit(solution)/shard_map/pallas_call | solution.py:114
  39.3 1.6 %collective-permute-start.16 = (f32[128,128]{1,0:T(8,128)S(1)}, f32[128,128]{1,0:T(8,128)S(1)}, u32[]{:S(2)}, u32[]{:S(2)}) collective-permute-start(f32[128,128]{1,0:T(8,128)S(1)} %get-tuple-element.111), channel_id=1, source_target_pairs={{0,12},{2,14},{4,8},{6,10},{8,4},{10,6},{12,0},{14,2},{1,13},{3,15... | collective-permute-start | bytes 196616 | tf_op jit(solution)/shard_map/ppermute | solution.py:583
  41.0 1.0 %collective-permute-start.17 = (f32[128,128]{1,0:T(8,128)S(1)}, f32[128,128]{1,0:T(8,128)S(1)}, u32[]{:S(2)}, u32[]{:S(2)}) collective-permute-start(f32[128,128]{1,0:T(8,128)S(1)} %get-tuple-element.112), channel_id=1, source_target_pairs={{0,14},{2,12},{4,10},{6,8},{8,6},{10,4},{12,2},{14,0},{1,15},{3,13... | collective-permute-start | bytes 196616 | tf_op jit(solution)/shard_map/ppermute | solution.py:583
  41.9 4.9 %collective-permute-start.18 = (f32[128,128]{1,0:T(8,128)S(1)}, f32[128,128]{1,0:T(8,128)S(1)}, u32[]{:S(2)}, u32[]{:S(2)}) collective-permute-start(f32[128,128]{1,0:T(8,128)S(1)} %get-tuple-element.113), channel_id=1, source_target_pairs={{0,8},{2,10},{4,12},{6,14},{8,0},{10,2},{12,4},{14,6},{1,9},{3,11}... | collective-permute-start | bytes 196616 | tf_op jit(solution)/shard_map/ppermute | solution.py:583
  46.8 2.5 %shard_map.42 = (f32[128,128]{1,0:T(8,128)S(1)}, f32[128,128]{1,0:T(8,128)S(1)}, f32[128,128]{1,0:T(8,128)S(1)}, f32[128,128]{1,0:T(8,128)S(1)}, f32[256,128]{1,...) custom-call(s32[2]{0:T(128)S(1)} %pad_add_fusion.place_ref, ...), custom_call_target="tpu_custom_call", output_to_operand_aliasing={{8}: (3, {}), {9}: (4, {}), {10}: (5, {}), {11}: (6, {}), {... | custom-call | tf_op jit(solution)/shard_map/pallas_call | solution.py:114
  49.3 1.8 %collective-permute-start.19 = (f32[128,128]{1,0:T(8,128)S(1)}, f32[128,128]{1,0:T(8,128)S(1)}, u32[]{:S(2)}, u32[]{:S(2)}) collective-permute-start(f32[128,128]{1,0:T(8,128)S(1)} %get-tuple-element.115), channel_id=1, source_target_pairs={{0,12},{2,14},{4,8},{6,10},{8,4},{10,6},{12,0},{14,2},{1,13},{3,15... | collective-permute-start | bytes 196616 | tf_op jit(solution)/shard_map/ppermute | solution.py:583
  51.1 1.0 %collective-permute-start.20 = (f32[128,128]{1,0:T(8,128)S(1)}, f32[128,128]{1,0:T(8,128)S(1)}, u32[]{:S(2)}, u32[]{:S(2)}) collective-permute-start(f32[128,128]{1,0:T(8,128)S(1)} %get-tuple-element.116), channel_id=1, source_target_pairs={{0,14},{2,12},{4,10},{6,8},{8,6},{10,4},{12,2},{14,0},{1,15},{3,13... | collective-permute-start | bytes 196616 | tf_op jit(solution)/shard_map/ppermute | solution.py:583
  53.2 2.7 %collective-permute-start.14 = (f32[256,128]{1,0:T(8,128)S(1)}, f32[256,128]{1,0:T(8,128)S(1)}, u32[]{:S(2)}, u32[]{:S(2)}) collective-permute-start(f32[256,128]{1,0:T(8,128)S(1)} %get-tuple-element.106), channel_id=1, source_target_pairs={{0,6},{2,4},{4,2},{6,0},{8,14},{10,12},{12,10},{14,8},{1,7},{3,5},... | collective-permute-start | bytes 393224 | tf_op jit(solution)/shard_map/ppermute | solution.py:583
  55.9 2.1 %collective-permute-start.13 = (f32[256,128]{1,0:T(8,128)S(1)}, f32[256,128]{1,0:T(8,128)S(1)}, u32[]{:S(2)}, u32[]{:S(2)}) collective-permute-start(f32[256,128]{1,0:T(8,128)S(1)} %get-tuple-element.103), channel_id=1, source_target_pairs={{0,4},{2,6},{4,0},{6,2},{8,12},{10,14},{12,8},{14,10},{1,5},{3,7},... | collective-permute-start | bytes 393224 | tf_op jit(solution)/shard_map/ppermute | solution.py:583
  57.9 3.0 %collective-permute-done.20 = f32[128,128]{1,0:T(8,128)S(1)} collective-permute-done((f32[128,128]{1,0:T(8,128)S(1)}, f32[128,128]{1,0:T(8,128)S(1)}, u32[]{:S(2)}, u32[]{:S(2)}) %collective-permute-start.20) | collective-permute-done | bytes 65568 | tf_op jit(solution)/shard_map/ppermute | solution.py:583
  61.8 1.4 %shard_map.43.refs_6_ = f32[2,16,64,128]{3,2,1,0:T(8,128)} custom-call(s32[2]{0:T(128)S(1)} %pad_add_fusion.place_ref, f32[8,16,128]{2,1,0:T(8,128)S(1)} %bitcast.28, f32[8,16,128]{2,1,0:T(8,128)S(1)} %bitcast.29, f32[8,16,128]{2,1,0:T(8,128)S(1)} %bitcast.30, f32[8,16,128]{2,1,0:T(8,128)S(1)} %bitcast.27, f32[8,16,128]{2,1,0:T(8,128)S(1)} %bitcast.31, ...), custom_call_target="tpu_custom_call" | custom-call | tf_op jit(solution)/shard_map/pallas_call | solution.py:114
  63.4 3.7 %collective-permute-done.11 = f32[128,128]{1,0:T(8,128)S(1)} collective-permute-done((f32[128,128]{1,0:T(8,128)S(1)}, f32[128,128]{1,0:T(8,128)S(1)}, u32[]{:S(2)}, u32[]{:S(2)}) %collective-permute-start.11) | collective-permute-done | bytes 65568 | tf_op jit(solution)/shard_map/ppermute | solution.py:583
  67.0 1.5 %shard_map.44 = f32[2,16,64,128]{3,2,1,0:T(8,128)} custom-call(s32[2]{0:T(128)S(1)} %pad_add_fusion.place_ref, f32[8,16,128]{2,1,0:T(8,128)S(1)} %bitcast.25, f32[8,16,128]{2,1,0:T(8,128)S(1)} %bitcast.26, f32[16,16,128]{2,1,0:T(8,128)S(1)} %bitcast.24, f32[16,16,128]{2,1,0:T(8,128)S(1)} %bitcast.23, ...), custom_call_target="tpu_custom_call", output_to_operand_aliasing={{}: (7, {})} | custom-call | tf_op jit(solution)/shard_map/pallas_call | solution.py:114
  (33 shorter events, 6.4 us)
Async XLA Ops:
  0.0 33.2 %copy-start = (f32[3,16,64,128]{3,2,1,0:T(8,128)S(1)}, f32[3,16,64,128]{3,2,1,0:T(8,128)}, u32[]{:S(2)}) copy-start(f32[3,16,64,128]{3,2,1,0:T(8,128)} %param.5) | copy-start | bytes 4718596
  0.1 1.3 %copy-start.1 = (f32[1,2,16,64,128]{4,3,2,1,0:T(8,128)S(1)}, f32[1,2,16,64,128]{4,3,2,1,0:T(8,128)}, u32[]{:S(2)}) copy-start(f32[1,2,16,64,128]{4,3,2,1,0:T(8,128)} %param.3) | copy-start | bytes 3145732
  1.4 31.8 %copy-start.2 = (f32[16,64,128]{2,1,0:T(8,128)S(1)}, f32[16,64,128]{2,1,0:T(8,128)}, u32[]{:S(2)}) copy-start(f32[16,64,128]{2,1,0:T(8,128)} %param.4) | copy-start | bytes 1572868
  2.1 11.1 %collective-permute-start = (f32[256,128]{1,0:T(8,128)S(1)}, f32[256,128]{1,0:T(8,128)S(1)}, u32[]{:S(2)}, u32[]{:S(2)}) collective-permute-start(f32[256,128]{1,0:T(8,128)S(1)} %get-tuple-element.61), channel_id=1, source_target_pairs={{0,8},{2,10},{4,12},{6,14},{8,0},{10,2},{12,4},{14,6},{1,9},{3,11}... | collective-permute-start | bytes 393224 | tf_op jit(solution)/shard_map/ppermute | solution.py:583
  4.8 11.3 %collective-permute-start.4 = (f32[256,128]{1,0:T(8,128)S(1)}, f32[256,128]{1,0:T(8,128)S(1)}, u32[]{:S(2)}, u32[]{:S(2)}) collective-permute-start(f32[256,128]{1,0:T(8,128)S(1)} %get-tuple-element.65), channel_id=1, source_target_pairs={{0,10},{2,8},{4,14},{6,12},{8,2},{10,0},{12,6},{14,4},{1,11},{3,9}... | collective-permute-start | bytes 393224 | tf_op jit(solution)/shard_map/ppermute | solution.py:583
  6.1 21.9 %collective-permute-start.1 = (f32[384,128]{1,0:T(8,128)S(1)}, f32[384,128]{1,0:T(8,128)S(1)}, u32[]{:S(2)}, u32[]{:S(2)}) collective-permute-start(f32[384,128]{1,0:T(8,128)S(1)} %get-tuple-element.62), channel_id=1, source_target_pairs={{0,4},{2,6},{4,0},{6,2},{8,12},{10,14},{12,8},{14,10},{1,5},{3,7},... | collective-permute-start | bytes 589832 | tf_op jit(solution)/shard_map/ppermute | solution.py:583
  6.5 21.4 %collective-permute-start.2 = (f32[384,128]{1,0:T(8,128)S(1)}, f32[384,128]{1,0:T(8,128)S(1)}, u32[]{:S(2)}, u32[]{:S(2)}) collective-permute-start(f32[384,128]{1,0:T(8,128)S(1)} %get-tuple-element.63), channel_id=1, source_target_pairs={{0,6},{2,4},{4,2},{6,0},{8,14},{10,12},{12,10},{14,8},{1,7},{3,5},... | collective-permute-start | bytes 589832 | tf_op jit(solution)/shard_map/ppermute | solution.py:583
  8.1 19.9 %collective-permute-start.3 = (f32[384,128]{1,0:T(8,128)S(1)}, f32[384,128]{1,0:T(8,128)S(1)}, u32[]{:S(2)}, u32[]{:S(2)}) collective-permute-start(f32[384,128]{1,0:T(8,128)S(1)} %get-tuple-element.64), channel_id=1, source_target_pairs={{0,2},{2,0},{4,6},{6,4},{8,10},{10,8},{12,14},{14,12},{1,3},{3,1},... | collective-permute-start | bytes 589832 | tf_op jit(solution)/shard_map/ppermute | solution.py:583
  13.2 6.6 %collective-permute-start.5 = (f32[256,128]{1,0:T(8,128)S(1)}, f32[256,128]{1,0:T(8,128)S(1)}, u32[]{:S(2)}, u32[]{:S(2)}) collective-permute-start(f32[256,128]{1,0:T(8,128)S(1)} %get-tuple-element.66), channel_id=1, source_target_pairs={{0,12},{2,14},{4,8},{6,10},{8,4},{10,6},{12,0},{14,2},{1,13},{3,15... | collective-permute-start | bytes 393224 | tf_op jit(solution)/shard_map/ppermute | solution.py:583
  16.0 11.9 %collective-permute-start.6 = (f32[256,128]{1,0:T(8,128)S(1)}, f32[256,128]{1,0:T(8,128)S(1)}, u32[]{:S(2)}, u32[]{:S(2)}) collective-permute-start(f32[256,128]{1,0:T(8,128)S(1)} %get-tuple-element.67), channel_id=1, source_target_pairs={{0,14},{2,12},{4,10},{6,8},{8,6},{10,4},{12,2},{14,0},{1,15},{3,13... | collective-permute-start | bytes 393224 | tf_op jit(solution)/shard_map/ppermute | solution.py:583
  28.6 6.7 %collective-permute-start.7 = (f32[192,128]{1,0:T(8,128)S(1)}, f32[192,128]{1,0:T(8,128)S(1)}, u32[]{:S(2)}, u32[]{:S(2)}) collective-permute-start(f32[192,128]{1,0:T(8,128)S(1)} %get-tuple-element.90), channel_id=1, source_target_pairs={{0,4},{4,0},{2,6},{6,2},{8,12},{12,8},{10,14},{14,10},{1,5},{5,1},... | collective-permute-start | bytes 294920 | tf_op jit(solution)/shard_map/ppermute | solution.py:595
  28.7 7.5 %collective-permute-start.8 = (f32[192,128]{1,0:T(8,128)S(1)}, f32[192,128]{1,0:T(8,128)S(1)}, u32[]{:S(2)}, u32[]{:S(2)}) collective-permute-start(f32[192,128]{1,0:T(8,128)S(1)} %get-tuple-element.91), channel_id=1, source_target_pairs={{4,8},{8,4},{6,10},{10,6},{5,9},{9,5},{7,11},{11,7},{20,24},{24,20... | collective-permute-start | bytes 294920 | tf_op jit(solution)/shard_map/ppermute | solution.py:596
  39.0 7.8 %collective-permute-start.9 = (f32[800,128]{1,0:T(8,128)S(1)}, f32[800,128]{1,0:T(8,128)S(1)}, u32[]{:S(2)}, u32[]{:S(2)}) collective-permute-start(f32[800,128]{1,0:T(8,128)S(1)} %get-tuple-element.94), channel_id=1, source_target_pairs={{0,1},{1,0},{2,3},{3,2},{4,5},{5,4},{6,7},{7,6},{8,9},{9,8},{10,11... | collective-permute-start | bytes 1228808 | tf_op jit(solution)/shard_map/ppermute | solution.py:515
  39.1 10.2 %collective-permute-start.12 = (f32[128,128]{1,0:T(8,128)S(1)}, f32[128,128]{1,0:T(8,128)S(1)}, u32[]{:S(2)}, u32[]{:S(2)}) collective-permute-start(f32[128,128]{1,0:T(8,128)S(1)} %get-tuple-element.102), channel_id=1, source_target_pairs={{0,10},{2,8},{4,14},{6,12},{8,2},{10,0},{12,6},{14,4},{1,11},{3,9}... | collective-permute-start | bytes 196616 | tf_op jit(solution)/shard_map/ppermute | solution.py:583
  39.3 12.8 %collective-permute-start.16 = (f32[128,128]{1,0:T(8,128)S(1)}, f32[128,128]{1,0:T(8,128)S(1)}, u32[]{:S(2)}, u32[]{:S(2)}) collective-permute-start(f32[128,128]{1,0:T(8,128)S(1)} %get-tuple-element.111), channel_id=1, source_target_pairs={{0,12},{2,14},{4,8},{6,10},{8,4},{10,6},{12,0},{14,2},{1,13},{3,15... | collective-permute-start | bytes 196616 | tf_op jit(solution)/shard_map/ppermute | solution.py:583
  41.0 12.2 %collective-permute-start.17 = (f32[128,128]{1,0:T(8,128)S(1)}, f32[128,128]{1,0:T(8,128)S(1)}, u32[]{:S(2)}, u32[]{:S(2)}) collective-permute-start(f32[128,128]{1,0:T(8,128)S(1)} %get-tuple-element.112), channel_id=1, source_target_pairs={{0,14},{2,12},{4,10},{6,8},{8,6},{10,4},{12,2},{14,0},{1,15},{3,13... | collective-permute-start | bytes 196616 | tf_op jit(solution)/shard_map/ppermute | solution.py:583
  41.9 13.9 %collective-permute-start.18 = (f32[128,128]{1,0:T(8,128)S(1)}, f32[128,128]{1,0:T(8,128)S(1)}, u32[]{:S(2)}, u32[]{:S(2)}) collective-permute-start(f32[128,128]{1,0:T(8,128)S(1)} %get-tuple-element.113), channel_id=1, source_target_pairs={{0,8},{2,10},{4,12},{6,14},{8,0},{10,2},{12,4},{14,6},{1,9},{3,11}... | collective-permute-start | bytes 196616 | tf_op jit(solution)/shard_map/ppermute | solution.py:583
  49.3 8.6 %collective-permute-start.19 = (f32[128,128]{1,0:T(8,128)S(1)}, f32[128,128]{1,0:T(8,128)S(1)}, u32[]{:S(2)}, u32[]{:S(2)}) collective-permute-start(f32[128,128]{1,0:T(8,128)S(1)} %get-tuple-element.115), channel_id=1, source_target_pairs={{0,12},{2,14},{4,8},{6,10},{8,4},{10,6},{12,0},{14,2},{1,13},{3,15... | collective-permute-start | bytes 196616 | tf_op jit(solution)/shard_map/ppermute | solution.py:583
  51.1 9.8 %collective-permute-start.20 = (f32[128,128]{1,0:T(8,128)S(1)}, f32[128,128]{1,0:T(8,128)S(1)}, u32[]{:S(2)}, u32[]{:S(2)}) collective-permute-start(f32[128,128]{1,0:T(8,128)S(1)} %get-tuple-element.116), channel_id=1, source_target_pairs={{0,14},{2,12},{4,10},{6,8},{8,6},{10,4},{12,2},{14,0},{1,15},{3,13... | collective-permute-start | bytes 196616 | tf_op jit(solution)/shard_map/ppermute | solution.py:583
  52.1 14.9 %collective-permute-start.15 = (f32[256,128]{1,0:T(8,128)S(1)}, f32[256,128]{1,0:T(8,128)S(1)}, u32[]{:S(2)}, u32[]{:S(2)}) collective-permute-start(f32[256,128]{1,0:T(8,128)S(1)} %get-tuple-element.109), channel_id=1, source_target_pairs={{0,2},{2,0},{4,6},{6,4},{8,10},{10,8},{12,14},{14,12},{1,3},{3,1},... | collective-permute-start | bytes 393224 | tf_op jit(solution)/shard_map/ppermute | solution.py:583
  53.2 13.9 %collective-permute-start.14 = (f32[256,128]{1,0:T(8,128)S(1)}, f32[256,128]{1,0:T(8,128)S(1)}, u32[]{:S(2)}, u32[]{:S(2)}) collective-permute-start(f32[256,128]{1,0:T(8,128)S(1)} %get-tuple-element.106), channel_id=1, source_target_pairs={{0,6},{2,4},{4,2},{6,0},{8,14},{10,12},{12,10},{14,8},{1,7},{3,5},... | collective-permute-start | bytes 393224 | tf_op jit(solution)/shard_map/ppermute | solution.py:583
  55.9 11.2 %collective-permute-start.13 = (f32[256,128]{1,0:T(8,128)S(1)}, f32[256,128]{1,0:T(8,128)S(1)}, u32[]{:S(2)}, u32[]{:S(2)}) collective-permute-start(f32[256,128]{1,0:T(8,128)S(1)} %get-tuple-element.103), channel_id=1, source_target_pairs={{0,4},{2,6},{4,0},{6,2},{8,12},{10,14},{12,8},{14,10},{1,5},{3,7},... | collective-permute-start | bytes 393224 | tf_op jit(solution)/shard_map/ppermute | solution.py:583
  57.9 5.4 %collective-permute-start.10 = (f32[128,128]{1,0:T(8,128)S(1)}, f32[128,128]{1,0:T(8,128)S(1)}, u32[]{:S(2)}, u32[]{:S(2)}) collective-permute-start(f32[128,128]{1,0:T(8,128)S(1)} %get-tuple-element.99), channel_id=1, source_target_pairs={{0,8},{2,10},{4,12},{6,14},{8,0},{10,2},{12,4},{14,6},{1,9},{3,11}... | collective-permute-start | bytes 196616 | tf_op jit(solution)/shard_map/ppermute | solution.py:583
  61.0 6.1 %collective-permute-start.11 = (f32[128,128]{1,0:T(8,128)S(1)}, f32[128,128]{1,0:T(8,128)S(1)}, u32[]{:S(2)}, u32[]{:S(2)}) collective-permute-start(f32[128,128]{1,0:T(8,128)S(1)} %get-tuple-element.100), channel_id=1, source_target_pairs={{0,10},{2,8},{4,14},{6,12},{8,2},{10,0},{12,6},{14,4},{1,11},{3,9}... | collective-permute-start | bytes 196616 | tf_op jit(solution)/shard_map/ppermute | solution.py:583
